TPU v7x, 32 devices: a whole 2x2x4 slice. The times are simulated.
32 devices in a mesh: groups: 2 (over x), node: 2 (over core), local: 8 (over z, y).
Axes of the slice: x: 2, y: 2, z: 4, core: 2. Of those that a mesh axis runs over, the one named last changes fastest.
Arguments:
- tokens: bfloat16 [256, 7168], P(('groups', 'node', 'local')), parts along dimension 0, may hold values from -6 to 6
- expert_ids: int32 [256, 8], P(('groups', 'node', 'local')), parts along dimension 0, may hold values from 0 to 15, all different within a row; in each aligned block of 8 rows (0 to 7, 8 to 15, ...) at most 6 rows name the same one
- route_weights: bfloat16 [256, 8], P(('groups', 'node', 'local')), parts along dimension 0, may hold values from 0.049804688 to 1
- w_gate: bfloat16 [16, 7168, 1024], P(('node', 'local')), may hold values from -0.0625 to 0.0625
- w_up: bfloat16 [16, 7168, 1024], P(('node', 'local')), may hold values from -0.0625 to 0.0625
- w_down: bfloat16 [16, 1024, 7168], P(('node', 'local')), may hold values from -0.1875 to 0.1875
Outputs:
- layer_out: bfloat16 [256, 7168], P(('groups', 'node', 'local')), parts along dimension 0
There are 2 independent parts, one for each index of `groups`. A program takes and returns all parts, laid end to end along the dimension named above; an argument that names none is the same for every part. Nothing has to cross between parts.
Inputs may be any that keep to these rules, and one draw needn't show every extreme that they name: `expert_ids`: each row names 8 different experts; among the 8 rows of one device no expert is named by more than 6 rows, and in every draw some expert is named by exactly 6 rows of some device.
All inputs are finite; a program needn't handle non-finite values.
Results may differ from a plain program's by a relative error of at most 0.0057.
Values may be sent and summed in bfloat16 or wider, within the bound.
No kernel may reach another device: no remote copies, remote signals or barrier semaphores. Data moves between devices by JAX's collectives and lax.ppermute only.
A program may use at most 128 MiB of HBM per device.

v0:
```python
import jax
import jax.numpy as jnp
from jax import lax
from jax.sharding import PartitionSpec as P

EXPERTS = 16


def expert_rows(block_rows, gate_proj, up_proj, down_proj):
    model_width = block_rows.shape[-1]
    flat_rows = block_rows.reshape(-1, model_width)
    gate_val = jnp.dot(flat_rows, gate_proj, preferred_element_type=jnp.float32)
    up_val = jnp.dot(flat_rows, up_proj, preferred_element_type=jnp.float32)
    hidden = (jax.nn.silu(gate_val) * up_val).astype(jnp.bfloat16)
    partial_out = jnp.dot(hidden, down_proj, preferred_element_type=jnp.float32).astype(
        jnp.bfloat16
    )
    return partial_out.reshape(block_rows.shape)


def shards(tokens, expert_ids, route_weights, w_gate, w_up, w_down):
    tok_rows = tokens.shape[0]
    model_width = tokens.shape[1]
    chosen_count = expert_ids.shape[1]
    node_count = lax.axis_size("node")
    local_count = lax.axis_size("local")
    split_count = node_count * local_count // EXPERTS
    capacity = 3 * tok_rows // 4
    gate_proj = w_gate[0]
    up_proj = w_up[0]
    down_proj = w_down[0]
    expert_hits = (
        expert_ids[:, :, None] == jnp.arange(EXPERTS, dtype=jnp.int32)[None, None, :]
    ).astype(jnp.int32)
    flat_hits = expert_hits.reshape(tok_rows * chosen_count, EXPERTS)
    before = jnp.cumsum(flat_hits, axis=0) - flat_hits
    slot_index = jnp.sum(before * flat_hits, axis=1).reshape(tok_rows, chosen_count)
    position = expert_ids * capacity + slot_index
    placement_map = (
        position.reshape(1, tok_rows * chosen_count)
        == jnp.arange(EXPERTS * capacity, dtype=jnp.int32)[:, None]
    )
    placement_map = jnp.any(
        placement_map.reshape(EXPERTS * capacity, tok_rows, chosen_count), axis=2
    ).astype(jnp.bfloat16)
    send_buffer = jnp.dot(placement_map, tokens, preferred_element_type=jnp.float32).astype(
        jnp.bfloat16
    )
    send_buffer = send_buffer.reshape(EXPERTS, capacity, model_width)
    repeated = jnp.repeat(send_buffer, split_count, axis=0)
    partial_out = expert_rows(
        lax.all_to_all(repeated, ("node", "local"), split_axis=0, concat_axis=0, tiled=True),
        gate_proj,
        up_proj,
        down_proj,
    )
    returned = lax.all_to_all(
        partial_out, ("node", "local"), split_axis=0, concat_axis=0, tiled=True
    )
    summed = returned.reshape(EXPERTS, split_count, capacity, model_width).astype(jnp.float32)
    expert_out = jnp.sum(summed, axis=1).astype(jnp.bfloat16)
    table_rows = expert_out.reshape(EXPERTS * capacity, model_width)
    picked = table_rows[position.reshape(-1)].reshape(tok_rows, chosen_count, model_width)
    combined = jnp.sum(
        route_weights.astype(jnp.float32)[:, :, None] * picked.astype(jnp.float32), axis=1
    )
    return combined.astype(jnp.bfloat16)


def solution(mesh):
    return jax.shard_map(
        shards,
        mesh=mesh,
        in_specs=(
            P(("groups", "node", "local"), None),
            P(("groups", "node", "local"), None),
            P(("groups", "node", "local"), None),
            P(("node", "local"), None, None),
            P(("node", "local"), None, None),
            P(("node", "local"), None, None),
        ),
        out_specs=P(("groups", "node", "local"), None),
        check_vma=False,
    )
```

profile of v0, /device:TPU:0, one launch (start us, length us, event | category | flops | bytes accessed | tf_op | source)
XLA Modules:
  0.0 128.7 jit_solution(6452482391582919174)
XLA Ops:
  0.0 0.0 copy-start
  0.0 0.8 eq.30
  0.8 0.1 fusion.24
  0.9 0.1 reduce_window_sum.11
  1.0 0.2 select_reduce_fusion
  1.2 0.1 reshape.66
  1.2 0.7 multiply_add_fusion
  1.9 0.1 fusion.25
  2.0 0.0 copy-done
  2.0 0.6 convolution_convert_fusion
  2.6 0.5 reshape_broadcast_in_dim_reshape.3
  3.2 51.4 %all_to_all.10 = bf16[16,6,7168]{2,1,0:T(8,128)(2,1)} all-to-all(bf16[16,6,7168]{2,1,0:T(8,128)(2,1)S(1)} %reshape_broadcast_in_dim_reshape.3), channel_id=1, replica_groups=mesh['groups'=2,'node'=2,'local'=8] {'node','local'}, dimensions={0} | all-to-all | bytes 2752512 | tf_op jit(solution)/shard_map/all_to_all | solution.py:52
  54.5 1.7 %reshape.67 = bf16[96,7168]{1,0:T(8,128)(2,1)S(1)} reshape(bf16[16,6,7168]{2,1,0:T(8,128)(2,1)} %all_to_all.10) | data formatting | bytes 2752512 | tf_op jit(solution)/shard_map/reshape | solution.py:11
  56.3 7.6 %fusion.4 = f32[96,1024]{1,0:T(8,128)S(1)} fusion(bf16[96,7168]{1,0:T(8,128)(2,1)S(1)} %reshape.67, bf16[1,7168,1024]{2,1,0:T(8,128)(2,1)} %param.9), kind=kOutput, calls=%fused_computation.5 | convolution fusion | flops 1409286144 | bytes 16449536 | tf_op jit(solution)/shard_map/dot_general | solution.py:12
  63.9 14.2 %fusion.6 = bf16[96,7168]{1,0:T(8,128)(2,1)S(1)} fusion(bf16[1,1024,7168]{2,1,0:T(8,128)(2,1)} %param.11, bf16[96,7168]{1,0:T(8,128)(2,1)S(1)} %reshape.67, bf16[1,7168,1024]{2,1,0:T(8,128)(2,1)} %param.10, f32[96,1024]{1,0:T(8,128)S(1)} %fusion.4), kind=kOutput, calls=%fused_computation.7 | convolution fusion | flops 2819850240 | bytes 32505856 | tf_op jit(solution)/shard_map/dot_general | solution.py:15
  78.0 1.5 %reshape.68 = bf16[16,6,7168]{2,1,0:T(8,128)(2,1)} reshape(bf16[96,7168]{1,0:T(8,128)(2,1)S(1)} %fusion.6) | data formatting | bytes 2752512 | tf_op jit(solution)/shard_map/reshape | solution.py:18
  79.6 0.0 copy-start.1
  79.6 3.8 %all-to-all-start.1 = ((bf16[16,6,7168]{2,1,0:T(8,128)(2,1)}), bf16[16,6,7168]{2,1,0:T(8,128)(2,1)S(1)}, u32[]{:S(2)}, u32[]{:S(2)}) async-start(bf16[16,6,7168]{2,1,0:T(8,128)(2,1)} %reshape.68), calls=%async_computation.1 | async-start | bytes 3670016 | tf_op jit(solution)/shard_map/all_to_all | solution.py:57
  83.4 0.1 reshape.69
  83.5 0.0 copy-done.1
  83.5 42.1 %all-to-all-done.1 = bf16[16,6,7168]{2,1,0:T(8,128)(2,1)S(1)} async-done(((bf16[16,6,7168]{2,1,0:T(8,128)(2,1)}), bf16[16,6,7168]{2,1,0:T(8,128)(2,1)S(1)}, u32[]{:S(2)}, u32[]{:S(2)}) %all-to-all-start.1) | async-done | bytes 1376288 | tf_op jit(solution)/shard_map/all_to_all | solution.py:57
  125.6 0.5 convert_element_type.38
  126.2 1.1 gather_fusion
  127.3 1.4 %fusion.9 = bf16[8,7168]{1,0:T(8,128)(2,1)} fusion(bf16[64,7168]{1,0:T(8,128)(2,1)S(1)} %gather_fusion, f32[8,8]{1,0:T(8,128)S(1)} %convert_element_type.33), kind=kLoop, calls=%fused_computation.10 | loop fusion | flops 1318912 | bytes 1032448 | tf_op jit(solution)/shard_map/reduce_sum | solution.py:64
  (3 shorter events, 0.0 us)
Async XLA Ops:
  0.0 2.0 %copy-start = (bf16[8,7168]{1,0:T(8,128)(2,1)S(1)}, bf16[8,7168]{1,0:T(8,128)(2,1)}, u32[]{:S(2)}) copy-start(bf16[8,7168]{1,0:T(8,128)(2,1)} %param.6) | copy-start | bytes 344068
  79.6 3.9 %copy-start.1 = (bf16[8,8]{1,0:T(8,128)(2,1)S(1)}, bf16[8,8]{1,0:T(8,128)(2,1)}, u32[]{:S(2)}) copy-start(bf16[8,8]{1,0:T(8,128)(2,1)} %param.8) | copy-start | bytes 388
  79.6 46.1 %all-to-all-start.1 = ((bf16[16,6,7168]{2,1,0:T(8,128)(2,1)}), bf16[16,6,7168]{2,1,0:T(8,128)(2,1)S(1)}, u32[]{:S(2)}, u32[]{:S(2)}) async-start(bf16[16,6,7168]{2,1,0:T(8,128)(2,1)} %reshape.68), calls=%async_computation.1 | async-start | bytes 3670016 | tf_op jit(solution)/shard_map/all_to_all | solution.py:57
where the time goes:
time: 129 us
  blocking collectives  51.4 us (40%)
  waiting for transfers between devices  42.1 us (33%)
  matrix products  22.3 us (17%)
  local copies, waits for them, and re-layouts  6.39 us (5%)
  starting transfers between devices  3.84 us (3%)
  other arithmetic  2.57 us (2%)
    all_to_all x1, blocking collectives, shards(): lax.all_to_all(repeated, ('node', 'local'), split_axis=0, concat_axis=0,...  51.4 us
    all_to_all x1, waiting for transfers between devices, shards(): lax.all_to_all(partial_out, ('node', 'local'), split_axis=0, concat_axis=...  42.1 us
    dot_general x1, matrix products, expert_rows(): jnp.dot(hidden, down_proj, preferred_element_type=jnp.float32)  14.2 us
    dot_general x1, matrix products, expert_rows(): gate_val = jnp.dot(flat_rows, gate_proj, preferred_element_type=jnp.float32)  7.61 us
    all_to_all x1, starting transfers between devices, shards(): lax.all_to_all(partial_out, ('node', 'local'), split_axis=0, concat_axis=...  3.84 us
  transfers between devices with their start and end apart: 1, of which 1 were waited for; matrix products, arithmetic and copies ran while one was open for 0% of the time, Pallas kernels for 0%

commit v1 on v0

v1 whole, which is shorter than its diff:
```python
import functools

import jax
import jax.numpy as jnp
from jax import lax
from jax.experimental import pallas as pl
from jax.experimental.pallas import tpu as pltpu
from jax.sharding import PartitionSpec as P

EXPERTS = 16
LANES = 128
GATHER_CHUNKS = 2
RETURN_CHUNKS = 2
VM = pltpu.VMEM
F32 = jnp.float32
BF16 = jnp.bfloat16


def in_vmem(array):
    return pltpu.with_memory_space_constraint(array, VM)


def call(kernel, outs, *args, limit, flops, nbytes):
    return pl.pallas_call(
        kernel,
        out_shape=outs,
        in_specs=[pl.BlockSpec(memory_space=VM)] * len(args),
        out_specs=jax.tree.map(lambda _: pl.BlockSpec(memory_space=VM), outs),
        compiler_params=pltpu.CompilerParams(vmem_limit_bytes=limit * 2**20),
        cost_estimate=pl.CostEstimate(
            flops=flops, bytes_accessed=nbytes, transcendentals=0
        ),
    )(*args)


def level_bits(node_count, bits):
    even = list(range(bits - 1, -1, -1))
    odd = even[:-2] + even[-2:][::-1]
    return [[(even, odd)[n % 2][k] for n in range(node_count)] for k in range(bits)]


def swap(array, level, local_count):
    perm = [
        (n * local_count + i, n * local_count + (i ^ (1 << bit)))
        for n, bit in enumerate(level)
        for i in range(local_count)
    ]
    return lax.ppermute(array, ("node", "local"), perm)


def swap_core(array, node_count):
    return lax.ppermute(array, "node", [(n, n ^ 1) for n in range(node_count)])


def proj_kernel(lo, hi, first, last, *refs):
    if first:
        own, other, w_gate, w_up = refs[:4]
        outs = refs[4:]
        gate = up = None
    else:
        own, other, w_gate, w_up, gate_in, up_in = refs[:6]
        outs = refs[6:]
        gate, up = gate_in[...], up_in[...]
    step = 512 if (hi - lo) % 512 == 0 else LANES
    for c in range(lo, hi, step):
        rows = jnp.concatenate(
            [own[:, c - lo : c - lo + step], other[:, c - lo : c - lo + step]], axis=0
        )
        g = jnp.dot(rows, w_gate[0, c : c + step, :], preferred_element_type=F32)
        u = jnp.dot(rows, w_up[0, c : c + step, :], preferred_element_type=F32)
        gate = g if gate is None else gate + g
        up = u if up is None else up + u
    if last:
        outs[0][...] = (gate / (1.0 + jnp.exp(-gate)) * up).astype(BF16)
    else:
        outs[0][...] = gate
        outs[1][...] = up


def down_kernel(lo, hi, hidden, own_coef, other_coef, pick, w_down, own_out, other_out):
    half = own_out.shape[0]
    coef = jnp.concatenate([own_coef[...], other_coef[...]], axis=0).astype(F32)
    coef = jnp.sum(coef * pick[...], axis=1, keepdims=True)
    step = 512 if (hi - lo) % 512 == 0 else LANES
    h = hidden[...]
    for c in range(lo, hi, step):
        part = coef * jnp.dot(
            h, w_down[0, :, c : c + step], preferred_element_type=F32
        )
        own_out[:, c - lo : c - lo + step] = part[:half]
        other_out[:, c - lo : c - lo + step] = part[half:].astype(BF16)


def edges(width, chunks):
    tiles = width // LANES
    return [tiles * i // chunks * LANES for i in range(chunks + 1)]


def shards(tokens, expert_ids, route_weights, w_gate, w_up, w_down):
    tok_rows, width = tokens.shape
    hid = w_gate.shape[2]
    node_count = lax.axis_size("node")
    local_count = lax.axis_size("local")
    split_count = node_count * local_count // EXPERTS
    bits = local_count.bit_length() - 1
    levels = level_bits(node_count, bits)
    half = tok_rows * local_count
    rows = 2 * half
    me = lax.axis_index("node") * local_count + lax.axis_index("local")
    pick = (jnp.arange(LANES, dtype=jnp.int32)[None, :] == me // split_count).astype(F32)
    hits = expert_ids[:, :, None] == jnp.arange(LANES, dtype=jnp.int32)[None, None, :]
    coef = jnp.sum(
        jnp.where(hits, route_weights.astype(F32)[:, :, None], 0.0), axis=1
    ).astype(BF16)

    cuts = edges(width, GATHER_CHUNKS)
    blocks = [tokens[:, a:b] for a, b in zip(cuts, cuts[1:])]
    blocks[-1] = jnp.concatenate([blocks[-1], coef], axis=1)
    for level in levels:
        blocks = [
            jnp.concatenate([b, swap(b, level, local_count)], axis=0) for b in blocks
        ]
    others = [swap_core(b, node_count) for b in blocks]

    w_gate, w_up, w_down = in_vmem(w_gate), in_vmem(w_up), in_vmem(w_down)
    state = ()
    for i, (a, b) in enumerate(zip(cuts, cuts[1:])):
        first, last = i == 0, i == GATHER_CHUNKS - 1
        outs = (
            [VM((rows, hid), BF16)] if last else [VM((rows, hid), F32)] * 2
        )
        state = call(
            functools.partial(proj_kernel, a, b, first, last),
            outs,
            blocks[i],
            others[i],
            w_gate,
            w_up,
            *state,
            limit=8,
            flops=4 * rows * hid * (b - a),
            nbytes=4 * hid * (b - a),
        )
    hidden = state[0]
    own_coef, other_coef = blocks[-1][:, -LANES:], others[-1][:, -LANES:]

    cuts = edges(width, RETURN_CHUNKS)
    results = []
    for a, b in zip(cuts, cuts[1:]):
        own, other = call(
            functools.partial(down_kernel, a, b),
            [VM((half, b - a), F32), VM((half, b - a), BF16)],
            hidden,
            own_coef,
            other_coef,
            pick,
            w_down,
            limit=8,
            flops=2 * rows * hid * (b - a),
            nbytes=2 * hid * (b - a),
        )
        total = own + swap_core(other, node_count).astype(F32)
        for level in levels[::-1]:
            n = total.shape[0] // 2
            total = total[:n] + swap(total[n:].astype(BF16), level, local_count).astype(
                F32
            )
        results.append(total.astype(BF16))
    return jnp.concatenate(results, axis=1)


def solution(mesh):
    return jax.shard_map(
        shards,
        mesh=mesh,
        in_specs=(
            P(("groups", "node", "local"), None),
            P(("groups", "node", "local"), None),
            P(("groups", "node", "local"), None),
            P(("node", "local"), None, None),
            P(("node", "local"), None, None),
            P(("node", "local"), None, None),
        ),
        out_specs=P(("groups", "node", "local"), None),
        check_vma=False,
    )
```

time: 129 us -> 76.2 us (0.59)
  blocking collectives: 51.4 us -> 0 us
  waiting for transfers between devices: 42.1 us -> 19.7 us
  matrix products: 22.3 us -> 0 us
  local copies, waits for them, and re-layouts: 6.39 us -> 24.7 us
  starting transfers between devices: 3.84 us -> 22 us
  Pallas kernels: 0 us -> 6.48 us
    all_to_all x1 -> x0, blocking collectives: 51.4 us -> none  [shards(): lax.all_to_all(repeated, ('node', 'local'), split_axis=0, concat_axis=0,...]
    all_to_all x1 -> x0, waiting for transfers between devices: 42.1 us -> none  [shards(): lax.all_to_all(partial_out, ('node', 'local'), split_axis=0, concat_axis=...]
    unnamed x4 -> x10, local copies, waits for them, and re-layouts: 0.01 us -> 23.8 us
    dot_general x3 -> x0, matrix products: 22.3 us -> none  [the longest x1 14.2 us: expert_rows(): jnp.dot(hidden, down_proj, preferred_element_type=jnp.float32)]
    ppermute x0 -> x16, starting transfers between devices: none -> 22 us  [the longest x12 21.2 us: swap(): return lax.ppermute(array, ('node', 'local'), perm)]
    ppermute x0 -> x16, waiting for transfers between devices: none -> 19.7 us  [the longest x12 19.2 us: swap(): return lax.ppermute(array, ('node', 'local'), perm)]
    pallas_call x0 -> x4, Pallas kernels: none -> 6.48 us  [call(): pl.pallas_call(kernel, out_shape=outs, in_specs=[pl.BlockSpec(memory_spac...]
    all_to_all x1 -> x0, starting transfers between devices: 3.84 us -> none  [shards(): lax.all_to_all(partial_out, ('node', 'local'), split_axis=0, concat_axis=...]
  transfers between devices with their start and end apart: 1 -> 16, of which waited for: 1 -> 14; matrix products, arithmetic and copies ran while one was open for 0% -> 3% of each run, Pallas kernels for 0% -> 4%
where the time goes in v1:
time: 76.2 us; the launch traced here: 75.8 us
  local copies, waits for them, and re-layouts  24.7 us (32%)
  starting transfers between devices  22 us (29%)
  waiting for transfers between devices  19.7 us (26%)
  Pallas kernels  6.48 us (9%)
  other arithmetic  2.61 us (3%)
    unnamed x10, local copies, waits for them, and re-layouts  23.8 us
    ppermute x12, starting transfers between devices, swap(): return lax.ppermute(array, ('node', 'local'), perm)  21.2 us
    ppermute x12, waiting for transfers between devices, swap(): return lax.ppermute(array, ('node', 'local'), perm)  19.2 us
    pallas_call x4, Pallas kernels, call(): pl.pallas_call(kernel, out_shape=outs, in_specs=[pl.BlockSpec(memory_spac...  6.48 us
  transfers between devices with their start and end apart: 16, of which 14 were waited for; matrix products, arithmetic and copies ran while one was open for 3% of the time, Pallas kernels for 4%

profile of v1, /device:TPU:0, one launch (start us, length us, event | category | flops | bytes accessed | tf_op | source)
XLA Modules:
  0.0 75.8 jit_solution(5291419533001118716)
XLA Ops:
  0.9 4.1 %collective-permute-start.4 = (bf16[8,3584]{1,0:T(8,128)(2,1)S(1)}, bf16[8,3584]{1,0:T(8,128)(2,1)S(1)}, u32[]{:S(2)}, u32[]{:S(2)}) collective-permute-start(bf16[8,3584]{1,0:T(8,128)(2,1)S(1)} %get-tuple-element.17), channel_id=1, source_target_pairs={{0,4},{1,5},{2,6},{3,7},{4,0},{5,1},{6,2},{7,3},{8,12},{9,13},{10,... | collective-permute-start | bytes 172040 | tf_op jit(solution)/shard_map/ppermute | solution.py:48
  6.5 1.2 %collective-permute-done.4 = bf16[8,3584]{1,0:T(8,128)(2,1)S(1)} collective-permute-done((bf16[8,3584]{1,0:T(8,128)(2,1)S(1)}, bf16[8,3584]{1,0:T(8,128)(2,1)S(1)}, u32[]{:S(2)}, u32[]{:S(2)}) %collective-permute-start.4) | collective-permute-done | bytes 57376 | tf_op jit(solution)/shard_map/ppermute | solution.py:48
  7.7 3.0 %collective-permute-start.5 = (bf16[16,3584]{1,0:T(8,128)(2,1)S(1)}, bf16[16,3584]{1,0:T(8,128)(2,1)S(1)}, u32[]{:S(2)}, u32[]{:S(2)}) collective-permute-start(bf16[16,3584]{1,0:T(8,128)(2,1)S(1)} %pad_maximum_fusion.5), channel_id=1, source_target_pairs={{0,2},{1,3},{2,0},{3,1},{4,6},{5,7},{6,4},{7,5},{8,9},{9,8},{10,11... | collective-permute-start | bytes 344072 | tf_op jit(solution)/shard_map/ppermute | solution.py:48
  11.8 1.4 %collective-permute-start.1 = (bf16[16,3712]{1,0:T(8,128)(2,1)S(1)}, bf16[16,3712]{1,0:T(8,128)(2,1)S(1)}, u32[]{:S(2)}, u32[]{:S(2)}) collective-permute-start(bf16[16,3712]{1,0:T(8,128)(2,1)S(1)} %pad_maximum_fusion.4), channel_id=1, source_target_pairs={{0,2},{1,3},{2,0},{3,1},{4,6},{5,7},{6,4},{7,5},{8,9},{9,8},{10,11... | collective-permute-start | bytes 356360 | tf_op jit(solution)/shard_map/ppermute | solution.py:48
  13.6 1.9 %collective-permute-start.6 = (bf16[32,3584]{1,0:T(8,128)(2,1)S(1)}, bf16[32,3584]{1,0:T(8,128)(2,1)S(1)}, u32[]{:S(2)}, u32[]{:S(2)}) collective-permute-start(bf16[32,3584]{1,0:T(8,128)(2,1)S(1)} %pad_maximum_fusion.3), channel_id=1, source_target_pairs={{0,1},{1,0},{2,3},{3,2},{4,5},{5,4},{6,7},{7,6},{8,10},{9,11},{10,... | collective-permute-start | bytes 688136 | tf_op jit(solution)/shard_map/ppermute | solution.py:48
  15.5 2.6 %collective-permute-done.1 = bf16[16,3712]{1,0:T(8,128)(2,1)S(1)} collective-permute-done((bf16[16,3712]{1,0:T(8,128)(2,1)S(1)}, bf16[16,3712]{1,0:T(8,128)(2,1)S(1)}, u32[]{:S(2)}, u32[]{:S(2)}) %collective-permute-start.1) | collective-permute-done | bytes 118816 | tf_op jit(solution)/shard_map/ppermute | solution.py:48
  19.8 4.5 %collective-permute-done.2 = bf16[32,3712]{1,0:T(8,128)(2,1)S(1)} collective-permute-done((bf16[32,3712]{1,0:T(8,128)(2,1)S(1)}, bf16[32,3712]{1,0:T(8,128)(2,1)S(1)}, u32[]{:S(2)}, u32[]{:S(2)}) %collective-permute-start.2) | collective-permute-done | bytes 237600 | tf_op jit(solution)/shard_map/ppermute | solution.py:48
  24.5 5.2 %copy-done = bf16[1,7168,1024]{2,1,0:T(8,128)(2,1)S(1)} copy-done((bf16[1,7168,1024]{2,1,0:T(8,128)(2,1)S(1)}, bf16[1,7168,1024]{2,1,0:T(8,128)(2,1)}, u32[]{:S(2)}) %copy-start) | copy-done | bytes 14680088
  29.6 5.2 %copy-done.2 = bf16[1,7168,1024]{2,1,0:T(8,128)(2,1)S(1)} copy-done((bf16[1,7168,1024]{2,1,0:T(8,128)(2,1)S(1)}, bf16[1,7168,1024]{2,1,0:T(8,128)(2,1)}, u32[]{:S(2)}) %copy-start.2) | copy-done | bytes 14680088
  34.8 2.1 %shard_map.64 = (f32[128,1024]{1,0:T(8,128)S(1)}, f32[128,1024]{1,0:T(8,128)S(1)}) custom-call(bf16[64,3584]{1,0:T(8,128)(2,1)S(1)} %pad_maximum_fusion.1.refs_0_, bf16[64,3584]{1,0:T(8,128)(2,1)S(1)} %collective-permute-done.7.refs_1_, bf16[1,7168,1024]{2,1,0:T(8,128)(2,1)S(1)} %copy-done, bf16[1,7168,1024]{2,1,0:T(8,128)(2,1)S(1)} %copy-done.2), custom_call_target="tpu_custom_call" | custom-call | flops 1879048192 | bytes 14680064 | tf_op jit(solution)/shard_map/pallas_call | solution.py:24
  36.9 3.1 %copy-done.1 = bf16[1,7168,1024]{2,1,0:T(8,128)(2,1)S(1)} copy-done((bf16[1,7168,1024]{2,1,0:T(8,128)(2,1)S(1)}, bf16[1,7168,1024]{2,1,0:T(8,128)(2,1)}, u32[]{:S(2)}) %copy-start.1) | copy-done | bytes 14680088
  40.0 5.2 %copy-done.3 = bf16[1,7168,1024]{2,1,0:T(8,128)(2,1)S(1)} copy-done((bf16[1,7168,1024]{2,1,0:T(8,128)(2,1)S(1)}, bf16[1,7168,1024]{2,1,0:T(8,128)(2,1)}, u32[]{:S(2)}) %copy-start.3) | copy-done | bytes 14680088
  45.1 2.1 %shard_map.65.hidden = bf16[128,1024]{1,0:T(8,128)(2,1)S(1)} custom-call(bf16[64,3712]{1,0:T(8,128)(2,1)S(1)} %pad_maximum_fusion.refs_0_, bf16[64,3712]{1,0:T(8,128)(2,1)S(1)} %collective-permute-done.3.refs_1_, bf16[1,7168,1024]{2,1,0:T(8,128)(2,1)S(1)} %copy-done.1, bf16[1,7168,1024]{2,1,0:T(8,128)(2,1)S(1)} %copy-done.3, ...), custom_call_target="tpu_custom_call" | custom-call | flops 1879048192 | bytes 14680064 | tf_op jit(solution)/shard_map/pallas_call | solution.py:24
  47.2 5.2 %copy-done.4 = bf16[1,1024,7168]{2,1,0:T(8,128)(2,1)S(1)} copy-done((bf16[1,1024,7168]{2,1,0:T(8,128)(2,1)S(1)}, bf16[1,1024,7168]{2,1,0:T(8,128)(2,1)}, u32[]{:S(2)}) %copy-start.4) | copy-done | bytes 14680088
  52.4 1.2 %shard_map.67 = (f32[64,3584]{1,0:T(8,128)S(1)}, bf16[64,3584]{1,0:T(8,128)(2,1)S(1)}) custom-call(bf16[128,1024]{1,0:T(8,128)(2,1)S(1)} %shard_map.65.hidden, bf16[64,128]{1,0:T(8,128)(2,1)S(1)} %slice.70.own_coef, bf16[64,128]{1,0:T(8,128)(2,1)S(1)} %slice.71.other_coef, f32[1,128]{1,0:T(1,128)S(1)} %compare_convert_fusion.pick, ...), custom_call_target="tpu_custom_call" | custom-call | flops 939524096 | bytes 7340032 | tf_op jit(solution)/shard_map/pallas_call | solution.py:24
  54.1 1.2 %shard_map.66 = (f32[64,3584]{1,0:T(8,128)S(1)}, bf16[64,3584]{1,0:T(8,128)(2,1)S(1)}) custom-call(bf16[128,1024]{1,0:T(8,128)(2,1)S(1)} %shard_map.65.hidden, bf16[64,128]{1,0:T(8,128)(2,1)S(1)} %slice.70.own_coef, bf16[64,128]{1,0:T(8,128)(2,1)S(1)} %slice.71.other_coef, f32[1,128]{1,0:T(1,128)S(1)} %compare_convert_fusion.pick, ...), custom_call_target="tpu_custom_call" | custom-call | flops 939524096 | bytes 7340032 | tf_op jit(solution)/shard_map/pallas_call | solution.py:24
  58.4 3.3 %collective-permute-done.13 = bf16[32,3584]{1,0:T(8,128)(2,1)S(1)} collective-permute-done((bf16[32,3584]{1,0:T(8,128)(2,1)S(1)}, bf16[32,3584]{1,0:T(8,128)(2,1)S(1)}, u32[]{:S(2)}, u32[]{:S(2)}) %collective-permute-start.13) | collective-permute-done | bytes 229408 | tf_op jit(solution)/shard_map/ppermute | solution.py:48
  61.8 1.4 %collective-permute-start.14 = (bf16[16,3584]{1,0:T(8,128)(2,1)S(1)}, bf16[16,3584]{1,0:T(8,128)(2,1)S(1)}, u32[]{:S(2)}, u32[]{:S(2)}) collective-permute-start(bf16[16,3584]{1,0:T(8,128)(2,1)S(1)} %slice.102), channel_id=1, source_target_pairs={{0,2},{1,3},{2,0},{3,1},{4,6},{5,7},{6,4},{7,5},{8,9},{9,8},{10,11... | collective-permute-start | bytes 344072 | tf_op jit(solution)/shard_map/ppermute | solution.py:48
  63.2 1.2 %collective-permute-done.9 = bf16[32,3584]{1,0:T(8,128)(2,1)S(1)} collective-permute-done((bf16[32,3584]{1,0:T(8,128)(2,1)S(1)}, bf16[32,3584]{1,0:T(8,128)(2,1)S(1)}, u32[]{:S(2)}, u32[]{:S(2)}) %collective-permute-start.9) | collective-permute-done | bytes 229408 | tf_op jit(solution)/shard_map/ppermute | solution.py:48
  64.4 1.4 %collective-permute-start.10 = (bf16[16,3584]{1,0:T(8,128)(2,1)S(1)}, bf16[16,3584]{1,0:T(8,128)(2,1)S(1)}, u32[]{:S(2)}, u32[]{:S(2)}) collective-permute-start(bf16[16,3584]{1,0:T(8,128)(2,1)S(1)} %slice.103), channel_id=1, source_target_pairs={{0,2},{1,3},{2,0},{3,1},{4,6},{5,7},{6,4},{7,5},{8,9},{9,8},{10,11... | collective-permute-start | bytes 344072 | tf_op jit(solution)/shard_map/ppermute | solution.py:48
  66.7 2.4 %collective-permute-start.15 = (bf16[8,3584]{1,0:T(8,128)(2,1)S(1)}, bf16[8,3584]{1,0:T(8,128)(2,1)S(1)}, u32[]{:S(2)}, u32[]{:S(2)}) collective-permute-start(bf16[8,3584]{1,0:T(8,128)(2,1)S(1)} %slice.104), channel_id=1, source_target_pairs={{0,4},{1,5},{2,6},{3,7},{4,0},{5,1},{6,2},{7,3},{8,12},{9,13},{10,... | collective-permute-start | bytes 172040 | tf_op jit(solution)/shard_map/ppermute | solution.py:48
  69.9 2.2 %collective-permute-start.11 = (bf16[8,3584]{1,0:T(8,128)(2,1)S(1)}, bf16[8,3584]{1,0:T(8,128)(2,1)S(1)}, u32[]{:S(2)}, u32[]{:S(2)}) collective-permute-start(bf16[8,3584]{1,0:T(8,128)(2,1)S(1)} %slice.105), channel_id=1, source_target_pairs={{0,4},{1,5},{2,6},{3,7},{4,0},{5,1},{6,2},{7,3},{8,12},{9,13},{10,... | collective-permute-start | bytes 172040 | tf_op jit(solution)/shard_map/ppermute | solution.py:48
  72.2 1.4 %collective-permute-done.15 = bf16[8,3584]{1,0:T(8,128)(2,1)S(1)} collective-permute-done((bf16[8,3584]{1,0:T(8,128)(2,1)S(1)}, bf16[8,3584]{1,0:T(8,128)(2,1)S(1)}, u32[]{:S(2)}, u32[]{:S(2)}) %collective-permute-start.15) | collective-permute-done | bytes 57376 | tf_op jit(solution)/shard_map/ppermute | solution.py:48
  73.6 1.5 %collective-permute-done.11 = bf16[8,3584]{1,0:T(8,128)(2,1)S(1)} collective-permute-done((bf16[8,3584]{1,0:T(8,128)(2,1)S(1)}, bf16[8,3584]{1,0:T(8,128)(2,1)S(1)}, u32[]{:S(2)}, u32[]{:S(2)}) %collective-permute-start.11) | collective-permute-done | bytes 57376 | tf_op jit(solution)/shard_map/ppermute | solution.py:48
  (50 shorter events, 11.8 us)
Async XLA Ops:
  0.9 6.9 %collective-permute-start.4 = (bf16[8,3584]{1,0:T(8,128)(2,1)S(1)}, bf16[8,3584]{1,0:T(8,128)(2,1)S(1)}, u32[]{:S(2)}, u32[]{:S(2)}) collective-permute-start(bf16[8,3584]{1,0:T(8,128)(2,1)S(1)} %get-tuple-element.17), channel_id=1, source_target_pairs={{0,4},{1,5},{2,6},{3,7},{4,0},{5,1},{6,2},{7,3},{8,12},{9,13},{10,... | collective-permute-start | bytes 172040 | tf_op jit(solution)/shard_map/ppermute | solution.py:48
  6.4 5.4 %collective-permute-start = (bf16[8,3712]{1,0:T(8,128)(2,1)S(1)}, bf16[8,3712]{1,0:T(8,128)(2,1)S(1)}, u32[]{:S(2)}, u32[]{:S(2)}) collective-permute-start(bf16[8,3712]{1,0:T(8,128)(2,1)S(1)} %pad_maximum_fusion.7), channel_id=1, source_target_pairs={{0,4},{1,5},{2,6},{3,7},{4,0},{5,1},{6,2},{7,3},{8,12},{9,13},{10,... | collective-permute-start | bytes 178184 | tf_op jit(solution)/shard_map/ppermute | solution.py:48
  7.7 5.8 %collective-permute-start.5 = (bf16[16,3584]{1,0:T(8,128)(2,1)S(1)}, bf16[16,3584]{1,0:T(8,128)(2,1)S(1)}, u32[]{:S(2)}, u32[]{:S(2)}) collective-permute-start(bf16[16,3584]{1,0:T(8,128)(2,1)S(1)} %pad_maximum_fusion.5), channel_id=1, source_target_pairs={{0,2},{1,3},{2,0},{3,1},{4,6},{5,7},{6,4},{7,5},{8,9},{9,8},{10,11... | collective-permute-start | bytes 344072 | tf_op jit(solution)/shard_map/ppermute | solution.py:48
  11.8 6.2 %collective-permute-start.1 = (bf16[16,3712]{1,0:T(8,128)(2,1)S(1)}, bf16[16,3712]{1,0:T(8,128)(2,1)S(1)}, u32[]{:S(2)}, u32[]{:S(2)}) collective-permute-start(bf16[16,3712]{1,0:T(8,128)(2,1)S(1)} %pad_maximum_fusion.4), channel_id=1, source_target_pairs={{0,2},{1,3},{2,0},{3,1},{4,6},{5,7},{6,4},{7,5},{8,9},{9,8},{10,11... | collective-permute-start | bytes 356360 | tf_op jit(solution)/shard_map/ppermute | solution.py:48
  13.6 6.1 %collective-permute-start.6 = (bf16[32,3584]{1,0:T(8,128)(2,1)S(1)}, bf16[32,3584]{1,0:T(8,128)(2,1)S(1)}, u32[]{:S(2)}, u32[]{:S(2)}) collective-permute-start(bf16[32,3584]{1,0:T(8,128)(2,1)S(1)} %pad_maximum_fusion.3), channel_id=1, source_target_pairs={{0,1},{1,0},{2,3},{3,2},{4,5},{5,4},{6,7},{7,6},{8,10},{9,11},{10,... | collective-permute-start | bytes 688136 | tf_op jit(solution)/shard_map/ppermute | solution.py:48
  18.1 6.2 %collective-permute-start.2 = (bf16[32,3712]{1,0:T(8,128)(2,1)S(1)}, bf16[32,3712]{1,0:T(8,128)(2,1)S(1)}, u32[]{:S(2)}, u32[]{:S(2)}) collective-permute-start(bf16[32,3712]{1,0:T(8,128)(2,1)S(1)} %pad_maximum_fusion.2), channel_id=1, source_target_pairs={{0,1},{1,0},{2,3},{3,2},{4,5},{5,4},{6,7},{7,6},{8,10},{9,11},{10,... | collective-permute-start | bytes 712712 | tf_op jit(solution)/shard_map/ppermute | solution.py:48
  19.7 4.7 %collective-permute-start.7 = (bf16[64,3584]{1,0:T(8,128)(2,1)S(1)}, bf16[64,3584]{1,0:T(8,128)(2,1)S(1)}, u32[]{:S(2)}, u32[]{:S(2)}) collective-permute-start(bf16[64,3584]{1,0:T(8,128)(2,1)S(1)} %pad_maximum_fusion.1.refs_0_), channel_id=1, source_target_pairs={{0,8},{8,0},{1,9},{9,1},{2,10},{10,2},{3,11},{11,3},{4,12},{12,4},... | collective-permute-start | bytes 1376264 | tf_op jit(solution)/shard_map/ppermute | solution.py:52
  24.3 12.5 %collective-permute-start.3 = (bf16[64,3712]{1,0:T(8,128)(2,1)S(1)}, bf16[64,3712]{1,0:T(8,128)(2,1)S(1)}, u32[]{:S(2)}, u32[]{:S(2)}) collective-permute-start(bf16[64,3712]{1,0:T(8,128)(2,1)S(1)} %pad_maximum_fusion.refs_0_), channel_id=1, source_target_pairs={{0,8},{8,0},{1,9},{9,1},{2,10},{10,2},{3,11},{11,3},{4,12},{12,4},... | collective-permute-start | bytes 1425416 | tf_op jit(solution)/shard_map/ppermute | solution.py:52
  24.4 5.2 %copy-start = (bf16[1,7168,1024]{2,1,0:T(8,128)(2,1)S(1)}, bf16[1,7168,1024]{2,1,0:T(8,128)(2,1)}, u32[]{:S(2)}) copy-start(bf16[1,7168,1024]{2,1,0:T(8,128)(2,1)} %refs_2_.3) | copy-start | bytes 44040196
  29.6 5.2 %copy-start.2 = (bf16[1,7168,1024]{2,1,0:T(8,128)(2,1)S(1)}, bf16[1,7168,1024]{2,1,0:T(8,128)(2,1)}, u32[]{:S(2)}) copy-start(bf16[1,7168,1024]{2,1,0:T(8,128)(2,1)} %refs_3_.3) | copy-start | bytes 44040196
  34.8 5.2 %copy-start.1 = (bf16[1,7168,1024]{2,1,0:T(8,128)(2,1)S(1)}, bf16[1,7168,1024]{2,1,0:T(8,128)(2,1)}, u32[]{:S(2)}) copy-start(bf16[1,7168,1024]{2,1,0:T(8,128)(2,1)} %refs_2_.3) | copy-start | bytes 44040196
  40.0 5.2 %copy-start.3 = (bf16[1,7168,1024]{2,1,0:T(8,128)(2,1)S(1)}, bf16[1,7168,1024]{2,1,0:T(8,128)(2,1)}, u32[]{:S(2)}) copy-start(bf16[1,7168,1024]{2,1,0:T(8,128)(2,1)} %refs_3_.3) | copy-start | bytes 44040196
  47.2 5.2 %copy-start.4 = (bf16[1,1024,7168]{2,1,0:T(8,128)(2,1)S(1)}, bf16[1,1024,7168]{2,1,0:T(8,128)(2,1)}, u32[]{:S(2)}) copy-start(bf16[1,1024,7168]{2,1,0:T(8,128)(2,1)} %w_down.3) | copy-start | bytes 44040196
  53.6 2.0 %collective-permute-start.12 = (bf16[64,3584]{1,0:T(8,128)(2,1)S(1)}, bf16[64,3584]{1,0:T(8,128)(2,1)S(1)}, u32[]{:S(2)}, u32[]{:S(2)}) collective-permute-start(bf16[64,3584]{1,0:T(8,128)(2,1)S(1)} %get-tuple-element.16), channel_id=1, source_target_pairs={{0,8},{8,0},{1,9},{9,1},{2,10},{10,2},{3,11},{11,3},{4,12},{12,4},... | collective-permute-start | bytes 1376264 | tf_op jit(solution)/shard_map/ppermute | solution.py:52
  55.3 1.9 %collective-permute-start.8 = (bf16[64,3584]{1,0:T(8,128)(2,1)S(1)}, bf16[64,3584]{1,0:T(8,128)(2,1)S(1)}, u32[]{:S(2)}, u32[]{:S(2)}) collective-permute-start(bf16[64,3584]{1,0:T(8,128)(2,1)S(1)} %get-tuple-element.14), channel_id=1, source_target_pairs={{0,8},{8,0},{1,9},{9,1},{2,10},{10,2},{3,11},{11,3},{4,12},{12,4},... | collective-permute-start | bytes 1376264 | tf_op jit(solution)/shard_map/ppermute | solution.py:52
  55.7 6.1 %collective-permute-start.13 = (bf16[32,3584]{1,0:T(8,128)(2,1)S(1)}, bf16[32,3584]{1,0:T(8,128)(2,1)S(1)}, u32[]{:S(2)}, u32[]{:S(2)}) collective-permute-start(bf16[32,3584]{1,0:T(8,128)(2,1)S(1)} %slice.100), channel_id=1, source_target_pairs={{0,1},{1,0},{2,3},{3,2},{4,5},{5,4},{6,7},{7,6},{8,10},{9,11},{10,... | collective-permute-start | bytes 688136 | tf_op jit(solution)/shard_map/ppermute | solution.py:48
  57.3 7.1 %collective-permute-start.9 = (bf16[32,3584]{1,0:T(8,128)(2,1)S(1)}, bf16[32,3584]{1,0:T(8,128)(2,1)S(1)}, u32[]{:S(2)}, u32[]{:S(2)}) collective-permute-start(bf16[32,3584]{1,0:T(8,128)(2,1)S(1)} %slice.101), channel_id=1, source_target_pairs={{0,1},{1,0},{2,3},{3,2},{4,5},{5,4},{6,7},{7,6},{8,10},{9,11},{10,... | collective-permute-start | bytes 688136 | tf_op jit(solution)/shard_map/ppermute | solution.py:48
  61.8 4.9 %collective-permute-start.14 = (bf16[16,3584]{1,0:T(8,128)(2,1)S(1)}, bf16[16,3584]{1,0:T(8,128)(2,1)S(1)}, u32[]{:S(2)}, u32[]{:S(2)}) collective-permute-start(bf16[16,3584]{1,0:T(8,128)(2,1)S(1)} %slice.102), channel_id=1, source_target_pairs={{0,2},{1,3},{2,0},{3,1},{4,6},{5,7},{6,4},{7,5},{8,9},{9,8},{10,11... | collective-permute-start | bytes 344072 | tf_op jit(solution)/shard_map/ppermute | solution.py:48
  64.4 5.5 %collective-permute-start.10 = (bf16[16,3584]{1,0:T(8,128)(2,1)S(1)}, bf16[16,3584]{1,0:T(8,128)(2,1)S(1)}, u32[]{:S(2)}, u32[]{:S(2)}) collective-permute-start(bf16[16,3584]{1,0:T(8,128)(2,1)S(1)} %slice.103), channel_id=1, source_target_pairs={{0,2},{1,3},{2,0},{3,1},{4,6},{5,7},{6,4},{7,5},{8,9},{9,8},{10,11... | collective-permute-start | bytes 344072 | tf_op jit(solution)/shard_map/ppermute | solution.py:48
  66.7 6.8 %collective-permute-start.15 = (bf16[8,3584]{1,0:T(8,128)(2,1)S(1)}, bf16[8,3584]{1,0:T(8,128)(2,1)S(1)}, u32[]{:S(2)}, u32[]{:S(2)}) collective-permute-start(bf16[8,3584]{1,0:T(8,128)(2,1)S(1)} %slice.104), channel_id=1, source_target_pairs={{0,4},{1,5},{2,6},{3,7},{4,0},{5,1},{6,2},{7,3},{8,12},{9,13},{10,... | collective-permute-start | bytes 172040 | tf_op jit(solution)/shard_map/ppermute | solution.py:48
  69.9 5.2 %collective-permute-start.11 = (bf16[8,3584]{1,0:T(8,128)(2,1)S(1)}, bf16[8,3584]{1,0:T(8,128)(2,1)S(1)}, u32[]{:S(2)}, u32[]{:S(2)}) collective-permute-start(bf16[8,3584]{1,0:T(8,128)(2,1)S(1)} %slice.105), channel_id=1, source_target_pairs={{0,4},{1,5},{2,6},{3,7},{4,0},{5,1},{6,2},{7,3},{8,12},{9,13},{10,... | collective-permute-start | bytes 172040 | tf_op jit(solution)/shard_map/ppermute | solution.py:48

commit v2 on v1

v2 whole, which is shorter than its diff:
```python
import functools

import jax
import jax.numpy as jnp
from jax import lax
from jax.experimental import pallas as pl
from jax.experimental.pallas import tpu as pltpu
from jax.sharding import PartitionSpec as P

EXPERTS = 16
LANES = 128
GATHER_CHUNKS = 2
RETURN_CHUNKS = 2
QUARTERS = 4
VM = pltpu.VMEM
F32 = jnp.float32
BF16 = jnp.bfloat16


def in_vmem(array):
    return pltpu.with_memory_space_constraint(array, VM)


def in_hbm(array):
    return pltpu.with_memory_space_constraint(array, pltpu.HBM)


def call(kernel, outs, *args, limit, flops, nbytes, scalars=(), after=()):
    def body(*refs):
        kernel(*refs[: len(scalars)], *refs[len(scalars) + len(after) :])

    return pl.pallas_call(
        body,
        out_shape=outs,
        in_specs=[pl.BlockSpec(memory_space=pltpu.SMEM)] * len(scalars)
        + [pl.BlockSpec(memory_space=pl.ANY)] * len(after)
        + [pl.BlockSpec(memory_space=VM)] * len(args),
        out_specs=[pl.BlockSpec(memory_space=VM)] * len(outs),
        compiler_params=pltpu.CompilerParams(vmem_limit_bytes=limit * 2**20),
        cost_estimate=pl.CostEstimate(
            flops=flops, bytes_accessed=nbytes, transcendentals=0
        ),
    )(*scalars, *after, *args)


def load_rows(arrays, lo, hi, after):
    count = len(arrays)

    def body(_, *refs):
        sems = refs[-1]
        copies = [
            pltpu.make_async_copy(
                refs[i].at[0, pl.ds(lo, hi - lo)], refs[count + i], sems.at[i]
            )
            for i in range(count)
        ]
        for copy in copies:
            copy.start()
        for copy in copies:
            copy.wait()

    outs = [VM((hi - lo, x.shape[2]), BF16) for x in arrays]
    return pl.pallas_call(
        body,
        out_shape=outs,
        in_specs=[pl.BlockSpec(memory_space=pl.ANY)]
        + [pl.BlockSpec(memory_space=pltpu.HBM)] * count,
        out_specs=[pl.BlockSpec(memory_space=VM)] * count,
        scratch_shapes=[pltpu.SemaphoreType.DMA((count,))],
        compiler_params=pltpu.CompilerParams(vmem_limit_bytes=2**20),
        cost_estimate=pl.CostEstimate(
            flops=0,
            bytes_accessed=2 * (hi - lo) * sum(x.shape[2] for x in arrays),
            transcendentals=0,
        ),
    )(after, *[in_hbm(x) for x in arrays])


def level_bits(node_count, bits):
    even = list(range(bits - 1, -1, -1))
    odd = even[:-2] + even[-2:][::-1]
    return [[(even, odd)[n % 2][k] for n in range(node_count)] for k in range(bits)]


def swap(array, level, local_count):
    perm = [
        (n * local_count + i, n * local_count + (i ^ (1 << bit)))
        for n, bit in enumerate(level)
        for i in range(local_count)
    ]
    return lax.ppermute(array, ("node", "local"), perm)


def swap_core(array, node_count):
    return lax.ppermute(array, "node", [(n, n ^ 1) for n in range(node_count)])


def prepare_kernel(tokens, ids, weights, out):
    width = tokens.shape[1]
    lane = lax.broadcasted_iota(jnp.int32, (tokens.shape[0], LANES), 1)
    coef = jnp.zeros((tokens.shape[0], LANES), F32)
    for k in range(ids.shape[1]):
        named = weights[:, k : k + 1].astype(F32)
        coef = coef + jnp.where(lane == ids[:, k : k + 1], named, 0.0)
    out[:, :width] = tokens[...]
    out[:, width:] = coef.astype(BF16)


def join_kernel(cuts, own, other, *outs):
    for out, a, b in zip(outs, cuts, cuts[1:]):
        rows = [own[:, a:b].astype(F32), other[:, a:b].astype(F32)]
        out[...] = jnp.concatenate(rows, axis=0).astype(BF16)


def proj_kernel(pieces, last, *refs):
    count = len(pieces) - 1
    weights, refs = refs[: 2 * count], refs[2 * count :]
    parts, refs = refs[:4], refs[4:]
    gate = up = None
    if not (pieces[0] == 0):
        gate, up = refs[0][...], refs[1][...]
        refs = refs[2:]
    for i, (lo, hi) in enumerate(zip(pieces, pieces[1:])):
        step = 896 if (hi - lo) % 896 == 0 else LANES
        for c in range(0, hi - lo, step):
            at = lo - pieces[0] + c
            rows = jnp.concatenate([p[:, at : at + step] for p in parts], axis=0)
            g = jnp.dot(
                rows, weights[2 * i][c : c + step, :], preferred_element_type=F32
            )
            u = jnp.dot(
                rows, weights[2 * i + 1][c : c + step, :], preferred_element_type=F32
            )
            gate = g if gate is None else gate + g
            up = u if up is None else up + u
    if last:
        refs[0][...] = (gate / (1.0 + jnp.exp(-gate)) * up).astype(BF16)
    else:
        refs[0][...] = gate
        refs[1][...] = up


def down_kernel(lo, hi, expert, w_down, hidden, *refs):
    parts, (own_out, other_out) = refs[:-2], refs[-2:]
    half = own_out.shape[0]
    coef = jnp.concatenate([p[:, -LANES:] for p in parts], axis=0).astype(F32)
    lane = lax.broadcasted_iota(jnp.int32, coef.shape, 1)
    coef = jnp.sum(jnp.where(lane == expert[0], coef, 0.0), axis=1, keepdims=True)
    step = 512 if (hi - lo) % 512 == 0 else LANES
    h = hidden[...]
    for c in range(lo, hi, step):
        part = coef * jnp.dot(
            h, w_down[0, :, c : c + step], preferred_element_type=F32
        )
        own_out[:, c - lo : c - lo + step] = part[:half]
        other_out[:, c - lo : c - lo + step] = part[half:].astype(BF16)


def edges(width, chunks):
    tiles = width // LANES
    return [tiles * i // chunks * LANES for i in range(chunks + 1)]


def shards(tokens, expert_ids, route_weights, w_gate, w_up, w_down):
    tok_rows, width = tokens.shape
    hid = w_gate.shape[2]
    node_count = lax.axis_size("node")
    local_count = lax.axis_size("local")
    split_count = node_count * local_count // EXPERTS
    bits = local_count.bit_length() - 1
    levels = level_bits(node_count, bits)
    half = tok_rows * local_count
    rows = 2 * half
    me = lax.axis_index("node") * local_count + lax.axis_index("local")
    expert = (me // split_count).astype(jnp.int32).reshape(1)

    block = call(
        lambda _, *refs: prepare_kernel(*refs),
        [VM((tok_rows, width + LANES), BF16)],
        tokens,
        expert_ids,
        route_weights,
        scalars=(expert,),
        limit=2,
        flops=0,
        nbytes=200_000,
    )[0]
    quarters = edges(width, QUARTERS)
    spans = list(zip(quarters, quarters[1:]))
    loads = [[0, 1], [2], [3]]
    loaded = {}

    def load(k, after):
        for q in loads[k] if k < len(loads) else []:
            loaded[q] = load_rows((w_gate, w_up), *spans[q], after)
        return [loaded[q][0] for q in (loads[k] if k < len(loads) else [])]

    cuts = edges(width, GATHER_CHUNKS)
    wide = cuts[:-1] + [cuts[-1] + LANES]
    for k, level in enumerate(levels[:-1]):
        other = swap(block, level, local_count)
        ties = load(k, block)
        ends = wide if k == bits - 2 else [0, width + LANES]
        blocks = call(
            functools.partial(join_kernel, ends),
            [VM((2 * block.shape[0], b - a), BF16) for a, b in zip(ends, ends[1:])],
            block,
            other,
            after=ties,
            limit=4,
            flops=0,
            nbytes=200_000,
        )
        block = blocks[0]
    for q in range(len(spans)):
        if q not in loaded:
            loaded[q] = load_rows((w_gate, w_up), *spans[q], block)
    parts = []
    for b in blocks:
        far = swap(b, levels[-1], local_count)
        parts.append([b, far, swap_core(b, node_count), swap_core(far, node_count)])

    w_down = in_vmem(w_down)
    state = ()
    each = QUARTERS // GATHER_CHUNKS
    for i in range(GATHER_CHUNKS):
        last = i == GATHER_CHUNKS - 1
        use = range(i * each, (i + 1) * each)
        state = call(
            functools.partial(
                proj_kernel, quarters[i * each : (i + 1) * each + 1], last
            ),
            [VM((rows, hid), BF16)] if last else [VM((rows, hid), F32)] * 2,
            *[w for q in use for w in loaded[q]],
            *parts[i],
            *state,
            limit=8,
            flops=4 * rows * hid * (cuts[i + 1] - cuts[i]),
            nbytes=4 * hid * (cuts[i + 1] - cuts[i]),
        )
    hidden = state[0]

    cuts = edges(width, RETURN_CHUNKS)
    results = []
    for a, b in zip(cuts, cuts[1:]):
        own, other = call(
            functools.partial(down_kernel, a, b),
            [VM((half, b - a), F32), VM((half, b - a), BF16)],
            w_down,
            hidden,
            *parts[-1],
            scalars=(expert,),
            limit=8,
            flops=2 * rows * hid * (b - a),
            nbytes=2 * hid * (b - a),
        )
        total = own + swap_core(other, node_count).astype(F32)
        for level in levels[::-1]:
            n = total.shape[0] // 2
            total = total[:n] + swap(total[n:].astype(BF16), level, local_count).astype(
                F32
            )
        results.append(total.astype(BF16))
    return jnp.concatenate(results, axis=1)


def solution(mesh):
    return jax.shard_map(
        shards,
        mesh=mesh,
        in_specs=(
            P(("groups", "node", "local"), None),
            P(("groups", "node", "local"), None),
            P(("groups", "node", "local"), None),
            P(("node", "local"), None, None),
            P(("node", "local"), None, None),
            P(("node", "local"), None, None),
        ),
        out_specs=P(("groups", "node", "local"), None),
        check_vma=False,
    )
```

time: 76.2 us -> 60 us (0.79)
  local copies, waits for them, and re-layouts: 24.7 us -> 2.99 us
  Pallas kernels: 6.48 us -> 19.9 us
  starting transfers between devices: 22 us -> 17.9 us
  waiting for transfers between devices: 19.7 us -> 17.7 us
  other arithmetic: 2.61 us -> 0.98 us
    unnamed x10 -> x14, local copies, waits for them, and re-layouts: 23.8 us -> 2.89 us
    pallas_call x4 -> x11, Pallas kernels: 6.48 us -> 19.9 us  [the longest x4 12.7 us: load_rows(): pl.pallas_call(body, out_shape=outs, in_specs=[pl.BlockSpec(memory_space=...]
    ppermute x12 -> x10, starting transfers between devices: 21.2 us -> 16.7 us  [swap(): return lax.ppermute(array, ('node', 'local'), perm)]
    ppermute x12 -> x10, waiting for transfers between devices: 19.2 us -> 17.5 us  [swap(): return lax.ppermute(array, ('node', 'local'), perm)]
    slice x3 -> x0, local copies, waits for them, and re-layouts: 0.86 us -> none  [the longest x1 0.85 us: shards(): blocks = [tokens[:, a:b] for a, b in zip(cuts, cuts[1:])]]
    reduce_sum x1 -> x0, other arithmetic: 0.78 us -> none  [shards(): jnp.sum(jnp.where(hits, route_weights.astype(F32)[:, :, None], 0.0), axis=1)]
  transfers between devices with their start and end apart: 16 -> 16, of which waited for: 14 -> 10; matrix products, arithmetic and copies ran while one was open for 3% -> 1% of each run, Pallas kernels for 4% -> 27%
where the time goes in v2:
time: 60 us; the launch traced here: 59.7 us
  Pallas kernels  19.9 us (33%)
  starting transfers between devices  17.9 us (30%)
  waiting for transfers between devices  17.7 us (30%)
  local copies, waits for them, and re-layouts  2.99 us (5%)
  other arithmetic  0.98 us (2%)
    ppermute x10, waiting for transfers between devices, swap(): return lax.ppermute(array, ('node', 'local'), perm)  17.5 us
    ppermute x10, starting transfers between devices, swap(): return lax.ppermute(array, ('node', 'local'), perm)  16.7 us
    pallas_call x4, Pallas kernels, load_rows(): pl.pallas_call(body, out_shape=outs, in_specs=[pl.BlockSpec(memory_space=...  12.7 us
    pallas_call x7, Pallas kernels, call(): pl.pallas_call(body, out_shape=outs, in_specs=[pl.BlockSpec(memory_space=...  7.2 us
    unnamed x14, local copies, waits for them, and re-layouts  2.89 us
  transfers between devices with their start and end apart: 16, of which 10 were waited for; matrix products, arithmetic and copies ran while one was open for 1% of the time, Pallas kernels for 27%

profile of v2, /device:TPU:0, one launch (start us, length us, event | category | flops | bytes accessed | tf_op | source)
XLA Modules:
  0.0 59.7 jit_solution(5955834979853893661)
XLA Ops:
  2.4 4.1 %collective-permute-start = (bf16[8,7296]{1,0:T(8,128)(2,1)S(1)}, bf16[8,7296]{1,0:T(8,128)(2,1)S(1)}, u32[]{:S(2)}, u32[]{:S(2)}) collective-permute-start(bf16[8,7296]{1,0:T(8,128)(2,1)S(1)} %shard_map.64._.refs_2_), channel_id=1, source_target_pairs={{0,4},{1,5},{2,6},{3,7},{4,0},{5,1},{6,2},{7,3},{8,12},{9,13},{10,... | collective-permute-start | bytes 350216 | tf_op jit(solution)/shard_map/ppermute | solution.py:91
  6.5 3.2 %shard_map.66 = (bf16[1792,1024]{1,0:T(8,128)(2,1)S(1)}, bf16[1792,1024]{1,0:T(8,128)(2,1)S(1)}) custom-call(bf16[8,7296]{1,0:T(8,128)(2,1)S(1)} %shard_map.64._.refs_2_, bf16[1,7168,1024]{2,1,0:T(8,128)(2,1)} %refs_0_.7, bf16[1,7168,1024]{2,1,0:T(8,128)(2,1)} %refs_1_.11), custom_call_target="tpu_custom_call" | custom-call | bytes 7340032 | tf_op jit(solution)/shard_map/pallas_call | solution.py:63
  9.6 3.2 %shard_map.65 = (bf16[1792,1024]{1,0:T(8,128)(2,1)S(1)}, bf16[1792,1024]{1,0:T(8,128)(2,1)S(1)}) custom-call(bf16[8,7296]{1,0:T(8,128)(2,1)S(1)} %shard_map.64._.refs_2_, bf16[1,7168,1024]{2,1,0:T(8,128)(2,1)} %refs_0_.7, bf16[1,7168,1024]{2,1,0:T(8,128)(2,1)} %refs_1_.11), custom_call_target="tpu_custom_call" | custom-call | bytes 7340032 | tf_op jit(solution)/shard_map/pallas_call | solution.py:63
  12.9 1.6 %collective-permute-start.1 = (bf16[16,7296]{1,0:T(8,128)(2,1)S(1)}, bf16[16,7296]{1,0:T(8,128)(2,1)S(1)}, u32[]{:S(2)}, u32[]{:S(2)}) collective-permute-start(bf16[16,7296]{1,0:T(8,128)(2,1)S(1)} %shard_map.67._.refs_1_), channel_id=1, source_target_pairs={{0,2},{1,3},{2,0},{3,1},{4,6},{5,7},{6,4},{7,5},{8,9},{9,8},{10,11... | collective-permute-start | bytes 700424 | tf_op jit(solution)/shard_map/ppermute | solution.py:91
  14.5 3.2 %shard_map.68 = (bf16[1792,1024]{1,0:T(8,128)(2,1)S(1)}, bf16[1792,1024]{1,0:T(8,128)(2,1)S(1)}) custom-call(bf16[16,7296]{1,0:T(8,128)(2,1)S(1)} %shard_map.67._.refs_1_, bf16[1,7168,1024]{2,1,0:T(8,128)(2,1)} %refs_0_.7, bf16[1,7168,1024]{2,1,0:T(8,128)(2,1)} %refs_1_.11), custom_call_target="tpu_custom_call" | custom-call | bytes 7340032 | tf_op jit(solution)/shard_map/pallas_call | solution.py:63
  17.7 1.3 %collective-permute-done.1.refs_2_ = bf16[16,7296]{1,0:T(8,128)(2,1)S(1)} collective-permute-done((bf16[16,7296]{1,0:T(8,128)(2,1)S(1)}, bf16[16,7296]{1,0:T(8,128)(2,1)S(1)}, u32[]{:S(2)}, u32[]{:S(2)}) %collective-permute-start.1) | collective-permute-done | bytes 233504 | tf_op jit(solution)/shard_map/ppermute | solution.py:91
  19.0 1.6 %collective-permute-start.5 = (bf16[32,3584]{1,0:T(8,128)(2,1)S(1)}, bf16[32,3584]{1,0:T(8,128)(2,1)S(1)}, u32[]{:S(2)}, u32[]{:S(2)}) collective-permute-start(bf16[32,3584]{1,0:T(8,128)(2,1)S(1)} %get-tuple-element.25._.refs_4_), channel_id=1, source_target_pairs={{0,1},{1,0},{2,3},{3,2},{4,5},{5,4},{6,7},{7,6},{8,10},{9,11},{10,... | collective-permute-start | bytes 688136 | tf_op jit(solution)/shard_map/ppermute | solution.py:91
  21.1 4.0 %collective-permute-done.5.refs_5_ = bf16[32,3584]{1,0:T(8,128)(2,1)S(1)} collective-permute-done((bf16[32,3584]{1,0:T(8,128)(2,1)S(1)}, bf16[32,3584]{1,0:T(8,128)(2,1)S(1)}, u32[]{:S(2)}, u32[]{:S(2)}) %collective-permute-start.5) | collective-permute-done | bytes 229408 | tf_op jit(solution)/shard_map/ppermute | solution.py:91
  25.6 2.0 %collective-permute-done.2.refs_5_.refs_4_ = bf16[32,3712]{1,0:T(8,128)(2,1)S(1)} collective-permute-done((bf16[32,3712]{1,0:T(8,128)(2,1)S(1)}, bf16[32,3712]{1,0:T(8,128)(2,1)S(1)}, u32[]{:S(2)}, u32[]{:S(2)}) %collective-permute-start.2) | collective-permute-done | bytes 237600 | tf_op jit(solution)/shard_map/ppermute | solution.py:91
  27.7 3.2 %shard_map.70 = (bf16[1792,1024]{1,0:T(8,128)(2,1)S(1)}, bf16[1792,1024]{1,0:T(8,128)(2,1)S(1)}) custom-call(bf16[32,3584]{1,0:T(8,128)(2,1)S(1)} %get-tuple-element.25._.refs_4_, bf16[1,7168,1024]{2,1,0:T(8,128)(2,1)} %refs_0_.7, bf16[1,7168,1024]{2,1,0:T(8,128)(2,1)} %refs_1_.11), custom_call_target="tpu_custom_call" | custom-call | bytes 7340032 | tf_op jit(solution)/shard_map/pallas_call | solution.py:63
  30.9 2.4 %shard_map.71 = (f32[128,1024]{1,0:T(8,128)S(1)}, f32[128,1024]{1,0:T(8,128)S(1)}) custom-call(bf16[1792,1024]{1,0:T(8,128)(2,1)S(1)} %get-tuple-element.21.refs_0_, bf16[1792,1024]{1,0:T(8,128)(2,1)S(1)} %get-tuple-element.29.refs_1_, bf16[1792,1024]{1,0:T(8,128)(2,1)S(1)} %get-tuple-element.22.refs_1_.refs_2_, ...), custom_call_target="tpu_custom_call" | custom-call | flops 1879048192 | bytes 14680064 | tf_op jit(solution)/shard_map/pallas_call | solution.py:32
  33.3 2.4 %shard_map.72.refs_2_ = bf16[128,1024]{1,0:T(8,128)(2,1)S(1)} custom-call(bf16[1792,1024]{1,0:T(8,128)(2,1)S(1)} %get-tuple-element.23.refs_0_, bf16[1792,1024]{1,0:T(8,128)(2,1)S(1)} %get-tuple-element.24.refs_1_, bf16[1792,1024]{1,0:T(8,128)(2,1)S(1)} %get-tuple-element.26.refs_2_, bf16[1792,1024]{1,0:T(8,128)(2,1)S(1)} %get-tuple-element.27.refs_3_, ...), custom_call_target="tpu_custom_call" | custom-call | flops 1879048192 | bytes 14680064 | tf_op jit(solution)/shard_map/pallas_call | solution.py:32
  36.4 1.1 %shard_map.73 = (f32[64,3584]{1,0:T(8,128)S(1)}, bf16[64,3584]{1,0:T(8,128)(2,1)S(1)}) custom-call(s32[1]{0:T(128)} %bitcast.refs_0_, bf16[1,1024,7168]{2,1,0:T(8,128)(2,1)S(1)} %bitcast.2, bf16[128,1024]{1,0:T(8,128)(2,1)S(1)} %shard_map.72.refs_2_, bf16[32,3712]{1,0:T(8,128)(2,1)S(1)} %get-tuple-element.28.refs_4_.refs_3_, ...), custom_call_target="tpu_custom_call" | custom-call | flops 939524096 | bytes 7340032 | tf_op jit(solution)/shard_map/pallas_call | solution.py:32
  38.1 1.1 %shard_map.74 = (f32[64,3584]{1,0:T(8,128)S(1)}, bf16[64,3584]{1,0:T(8,128)(2,1)S(1)}) custom-call(s32[1]{0:T(128)} %bitcast.refs_0_, bf16[1,1024,7168]{2,1,0:T(8,128)(2,1)S(1)} %bitcast.2, bf16[128,1024]{1,0:T(8,128)(2,1)S(1)} %shard_map.72.refs_2_, bf16[32,3712]{1,0:T(8,128)(2,1)S(1)} %get-tuple-element.28.refs_4_.refs_3_, ...), custom_call_target="tpu_custom_call" | custom-call | flops 939524096 | bytes 7340032 | tf_op jit(solution)/shard_map/pallas_call | solution.py:32
  39.6 1.6 %collective-permute-start.9 = (bf16[32,3584]{1,0:T(8,128)(2,1)S(1)}, bf16[32,3584]{1,0:T(8,128)(2,1)S(1)}, u32[]{:S(2)}, u32[]{:S(2)}) collective-permute-start(bf16[32,3584]{1,0:T(8,128)(2,1)S(1)} %slice.83), channel_id=1, source_target_pairs={{0,1},{1,0},{2,3},{3,2},{4,5},{5,4},{6,7},{7,6},{8,10},{9,11},{10,... | collective-permute-start | bytes 688136 | tf_op jit(solution)/shard_map/ppermute | solution.py:91
  41.4 1.5 %collective-permute-start.13 = (bf16[32,3584]{1,0:T(8,128)(2,1)S(1)}, bf16[32,3584]{1,0:T(8,128)(2,1)S(1)}, u32[]{:S(2)}, u32[]{:S(2)}) collective-permute-start(bf16[32,3584]{1,0:T(8,128)(2,1)S(1)} %slice.82), channel_id=1, source_target_pairs={{0,1},{1,0},{2,3},{3,2},{4,5},{5,4},{6,7},{7,6},{8,10},{9,11},{10,... | collective-permute-start | bytes 688136 | tf_op jit(solution)/shard_map/ppermute | solution.py:91
  42.8 2.9 %collective-permute-done.9 = bf16[32,3584]{1,0:T(8,128)(2,1)S(1)} collective-permute-done((bf16[32,3584]{1,0:T(8,128)(2,1)S(1)}, bf16[32,3584]{1,0:T(8,128)(2,1)S(1)}, u32[]{:S(2)}, u32[]{:S(2)}) %collective-permute-start.9) | collective-permute-done | bytes 229408 | tf_op jit(solution)/shard_map/ppermute | solution.py:91
  45.8 1.6 %collective-permute-start.10 = (bf16[16,3584]{1,0:T(8,128)(2,1)S(1)}, bf16[16,3584]{1,0:T(8,128)(2,1)S(1)}, u32[]{:S(2)}, u32[]{:S(2)}) collective-permute-start(bf16[16,3584]{1,0:T(8,128)(2,1)S(1)} %slice.85), channel_id=1, source_target_pairs={{0,2},{1,3},{2,0},{3,1},{4,6},{5,7},{6,4},{7,5},{8,9},{9,8},{10,11... | collective-permute-start | bytes 344072 | tf_op jit(solution)/shard_map/ppermute | solution.py:91
  48.4 1.6 %collective-permute-start.14 = (bf16[16,3584]{1,0:T(8,128)(2,1)S(1)}, bf16[16,3584]{1,0:T(8,128)(2,1)S(1)}, u32[]{:S(2)}, u32[]{:S(2)}) collective-permute-start(bf16[16,3584]{1,0:T(8,128)(2,1)S(1)} %slice.84), channel_id=1, source_target_pairs={{0,2},{1,3},{2,0},{3,1},{4,6},{5,7},{6,4},{7,5},{8,9},{9,8},{10,11... | collective-permute-start | bytes 344072 | tf_op jit(solution)/shard_map/ppermute | solution.py:91
  50.7 1.5 %collective-permute-start.11 = (bf16[8,3584]{1,0:T(8,128)(2,1)S(1)}, bf16[8,3584]{1,0:T(8,128)(2,1)S(1)}, u32[]{:S(2)}, u32[]{:S(2)}) collective-permute-start(bf16[8,3584]{1,0:T(8,128)(2,1)S(1)} %slice.87), channel_id=1, source_target_pairs={{0,4},{1,5},{2,6},{3,7},{4,0},{5,1},{6,2},{7,3},{8,12},{9,13},{10,... | collective-permute-start | bytes 172040 | tf_op jit(solution)/shard_map/ppermute | solution.py:91
  52.2 1.7 %collective-permute-done.14 = bf16[16,3584]{1,0:T(8,128)(2,1)S(1)} collective-permute-done((bf16[16,3584]{1,0:T(8,128)(2,1)S(1)}, bf16[16,3584]{1,0:T(8,128)(2,1)S(1)}, u32[]{:S(2)}, u32[]{:S(2)}) %collective-permute-start.14) | collective-permute-done | bytes 114720 | tf_op jit(solution)/shard_map/ppermute | solution.py:91
  53.9 1.1 %collective-permute-start.15 = (bf16[8,3584]{1,0:T(8,128)(2,1)S(1)}, bf16[8,3584]{1,0:T(8,128)(2,1)S(1)}, u32[]{:S(2)}, u32[]{:S(2)}) collective-permute-start(bf16[8,3584]{1,0:T(8,128)(2,1)S(1)} %slice.86), channel_id=1, source_target_pairs={{0,4},{1,5},{2,6},{3,7},{4,0},{5,1},{6,2},{7,3},{8,12},{9,13},{10,... | collective-permute-start | bytes 172040 | tf_op jit(solution)/shard_map/ppermute | solution.py:91
  55.0 2.5 %collective-permute-done.11 = bf16[8,3584]{1,0:T(8,128)(2,1)S(1)} collective-permute-done((bf16[8,3584]{1,0:T(8,128)(2,1)S(1)}, bf16[8,3584]{1,0:T(8,128)(2,1)S(1)}, u32[]{:S(2)}, u32[]{:S(2)}) %collective-permute-start.11) | collective-permute-done | bytes 57376 | tf_op jit(solution)/shard_map/ppermute | solution.py:91
  57.6 1.5 %collective-permute-done.15 = bf16[8,3584]{1,0:T(8,128)(2,1)S(1)} collective-permute-done((bf16[8,3584]{1,0:T(8,128)(2,1)S(1)}, bf16[8,3584]{1,0:T(8,128)(2,1)S(1)}, u32[]{:S(2)}, u32[]{:S(2)}) %collective-permute-start.15) | collective-permute-done | bytes 57376 | tf_op jit(solution)/shard_map/ppermute | solution.py:91
  (49 shorter events, 7.5 us)
Async XLA Ops:
  0.0 0.9 %copy-start = (bf16[8,7168]{1,0:T(8,128)(2,1)S(1)}, bf16[8,7168]{1,0:T(8,128)(2,1)}, u32[]{:S(2)}) copy-start(bf16[8,7168]{1,0:T(8,128)(2,1)} %refs_1_.7) | copy-start | bytes 344068
  0.9 0.7 %copy-start.1 = (s32[8,8]{1,0:T(8,128)S(1)}, s32[8,8]{1,0:T(8,128)}, u32[]{:S(2)}) copy-start(s32[8,8]{1,0:T(8,128)} %refs_2_.1) | copy-start | bytes 772
  1.6 0.7 %copy-start.2 = (bf16[8,8]{1,0:T(8,128)(2,1)S(1)}, bf16[8,8]{1,0:T(8,128)(2,1)}, u32[]{:S(2)}) copy-start(bf16[8,8]{1,0:T(8,128)(2,1)} %refs_3_.1) | copy-start | bytes 388
  2.4 10.5 %collective-permute-start = (bf16[8,7296]{1,0:T(8,128)(2,1)S(1)}, bf16[8,7296]{1,0:T(8,128)(2,1)S(1)}, u32[]{:S(2)}, u32[]{:S(2)}) collective-permute-start(bf16[8,7296]{1,0:T(8,128)(2,1)S(1)} %shard_map.64._.refs_2_), channel_id=1, source_target_pairs={{0,4},{1,5},{2,6},{3,7},{4,0},{5,1},{6,2},{7,3},{8,12},{9,13},{10,... | collective-permute-start | bytes 350216 | tf_op jit(solution)/shard_map/ppermute | solution.py:91
  12.9 6.1 %collective-permute-start.1 = (bf16[16,7296]{1,0:T(8,128)(2,1)S(1)}, bf16[16,7296]{1,0:T(8,128)(2,1)S(1)}, u32[]{:S(2)}, u32[]{:S(2)}) collective-permute-start(bf16[16,7296]{1,0:T(8,128)(2,1)S(1)} %shard_map.67._.refs_1_), channel_id=1, source_target_pairs={{0,2},{1,3},{2,0},{3,1},{4,6},{5,7},{6,4},{7,5},{8,9},{9,8},{10,11... | collective-permute-start | bytes 700424 | tf_op jit(solution)/shard_map/ppermute | solution.py:91
  19.0 6.1 %collective-permute-start.5 = (bf16[32,3584]{1,0:T(8,128)(2,1)S(1)}, bf16[32,3584]{1,0:T(8,128)(2,1)S(1)}, u32[]{:S(2)}, u32[]{:S(2)}) collective-permute-start(bf16[32,3584]{1,0:T(8,128)(2,1)S(1)} %get-tuple-element.25._.refs_4_), channel_id=1, source_target_pairs={{0,1},{1,0},{2,3},{3,2},{4,5},{5,4},{6,7},{7,6},{8,10},{9,11},{10,... | collective-permute-start | bytes 688136 | tf_op jit(solution)/shard_map/ppermute | solution.py:91
  20.6 7.0 %collective-permute-start.2 = (bf16[32,3712]{1,0:T(8,128)(2,1)S(1)}, bf16[32,3712]{1,0:T(8,128)(2,1)S(1)}, u32[]{:S(2)}, u32[]{:S(2)}) collective-permute-start(bf16[32,3712]{1,0:T(8,128)(2,1)S(1)} %get-tuple-element.28.refs_4_.refs_3_), channel_id=1, source_target_pairs={{0,1},{1,0},{2,3},{3,2},{4,5},{5,4},{6,7},{7,6},{8,10},{9,11},{10,... | collective-permute-start | bytes 712712 | tf_op jit(solution)/shard_map/ppermute | solution.py:91
  21.1 9.7 %collective-permute-start.6 = (bf16[32,3584]{1,0:T(8,128)(2,1)S(1)}, bf16[32,3584]{1,0:T(8,128)(2,1)S(1)}, u32[]{:S(2)}, u32[]{:S(2)}) collective-permute-start(bf16[32,3584]{1,0:T(8,128)(2,1)S(1)} %get-tuple-element.25._.refs_4_), channel_id=1, source_target_pairs={{0,8},{8,0},{1,9},{9,1},{2,10},{10,2},{3,11},{11,3},{4,12},{12,4},... | collective-permute-start | bytes 688136 | tf_op jit(solution)/shard_map/ppermute | solution.py:95
  25.1 5.7 %collective-permute-start.7 = (bf16[32,3584]{1,0:T(8,128)(2,1)S(1)}, bf16[32,3584]{1,0:T(8,128)(2,1)S(1)}, u32[]{:S(2)}, u32[]{:S(2)}) collective-permute-start(bf16[32,3584]{1,0:T(8,128)(2,1)S(1)} %collective-permute-done.5.refs_5_), channel_id=1, source_target_pairs={{0,8},{8,0},{1,9},{9,1},{2,10},{10,2},{3,11},{11,3},{4,12},{12,4},... | collective-permute-start | bytes 688136 | tf_op jit(solution)/shard_map/ppermute | solution.py:95
  25.1 8.2 %collective-permute-start.3 = (bf16[32,3712]{1,0:T(8,128)(2,1)S(1)}, bf16[32,3712]{1,0:T(8,128)(2,1)S(1)}, u32[]{:S(2)}, u32[]{:S(2)}) collective-permute-start(bf16[32,3712]{1,0:T(8,128)(2,1)S(1)} %get-tuple-element.28.refs_4_.refs_3_), channel_id=1, source_target_pairs={{0,8},{8,0},{1,9},{9,1},{2,10},{10,2},{3,11},{11,3},{4,12},{12,4},... | collective-permute-start | bytes 712712 | tf_op jit(solution)/shard_map/ppermute | solution.py:95
  27.7 5.6 %collective-permute-start.4 = (bf16[32,3712]{1,0:T(8,128)(2,1)S(1)}, bf16[32,3712]{1,0:T(8,128)(2,1)S(1)}, u32[]{:S(2)}, u32[]{:S(2)}) collective-permute-start(bf16[32,3712]{1,0:T(8,128)(2,1)S(1)} %collective-permute-done.2.refs_5_.refs_4_), channel_id=1, source_target_pairs={{0,8},{8,0},{1,9},{9,1},{2,10},{10,2},{3,11},{11,3},{4,12},{12,4},... | collective-permute-start | bytes 712712 | tf_op jit(solution)/shard_map/ppermute | solution.py:95
  30.9 4.9 %slice-start = ((s8[14680064]{0:T(1024)(128)(4,1)}), s8[4194304]{0:T(1024)(128)(4,1)S(1)}, s32[]{:S(2)}) async-start(s8[14680064]{0:T(1024)(128)(4,1)} %bitcast.1), calls=%async_computation | async-start | bytes 8388608
  30.9 4.9 %slice-start.1 = ((s8[14680064]{0:T(1024)(128)(4,1)}), s8[4194304]{0:T(1024)(128)(4,1)S(1)}, s32[]{:S(2)}) async-start(s8[14680064]{0:T(1024)(128)(4,1)} %bitcast.1), calls=%async_computation.1 | async-start | bytes 8388608
  33.3 2.4 %slice-start.2 = ((s8[14680064]{0:T(1024)(128)(4,1)}), s8[4194304]{0:T(1024)(128)(4,1)S(1)}, s32[]{:S(2)}) async-start(s8[14680064]{0:T(1024)(128)(4,1)} %bitcast.1), calls=%async_computation.2 | async-start | bytes 8388608
  33.3 3.0 %slice-start.3 = ((s8[14680064]{0:T(1024)(128)(4,1)}), s8[2097152]{0:T(1024)(128)(4,1)S(1)}, s32[]{:S(2)}) async-start(s8[14680064]{0:T(1024)(128)(4,1)} %bitcast.1), calls=%async_computation.3 | async-start | bytes 4194304
  37.5 2.0 %collective-permute-start.8 = (bf16[64,3584]{1,0:T(8,128)(2,1)S(1)}, bf16[64,3584]{1,0:T(8,128)(2,1)S(1)}, u32[]{:S(2)}, u32[]{:S(2)}) collective-permute-start(bf16[64,3584]{1,0:T(8,128)(2,1)S(1)} %get-tuple-element.34), channel_id=1, source_target_pairs={{0,8},{8,0},{1,9},{9,1},{2,10},{10,2},{3,11},{11,3},{4,12},{12,4},... | collective-permute-start | bytes 1376264 | tf_op jit(solution)/shard_map/ppermute | solution.py:95
  39.2 2.0 %collective-permute-start.12 = (bf16[64,3584]{1,0:T(8,128)(2,1)S(1)}, bf16[64,3584]{1,0:T(8,128)(2,1)S(1)}, u32[]{:S(2)}, u32[]{:S(2)}) collective-permute-start(bf16[64,3584]{1,0:T(8,128)(2,1)S(1)} %get-tuple-element.36), channel_id=1, source_target_pairs={{0,8},{8,0},{1,9},{9,1},{2,10},{10,2},{3,11},{11,3},{4,12},{12,4},... | collective-permute-start | bytes 1376264 | tf_op jit(solution)/shard_map/ppermute | solution.py:95
  39.6 6.1 %collective-permute-start.9 = (bf16[32,3584]{1,0:T(8,128)(2,1)S(1)}, bf16[32,3584]{1,0:T(8,128)(2,1)S(1)}, u32[]{:S(2)}, u32[]{:S(2)}) collective-permute-start(bf16[32,3584]{1,0:T(8,128)(2,1)S(1)} %slice.83), channel_id=1, source_target_pairs={{0,1},{1,0},{2,3},{3,2},{4,5},{5,4},{6,7},{7,6},{8,10},{9,11},{10,... | collective-permute-start | bytes 688136 | tf_op jit(solution)/shard_map/ppermute | solution.py:91
  41.4 7.0 %collective-permute-start.13 = (bf16[32,3584]{1,0:T(8,128)(2,1)S(1)}, bf16[32,3584]{1,0:T(8,128)(2,1)S(1)}, u32[]{:S(2)}, u32[]{:S(2)}) collective-permute-start(bf16[32,3584]{1,0:T(8,128)(2,1)S(1)} %slice.82), channel_id=1, source_target_pairs={{0,1},{1,0},{2,3},{3,2},{4,5},{5,4},{6,7},{7,6},{8,10},{9,11},{10,... | collective-permute-start | bytes 688136 | tf_op jit(solution)/shard_map/ppermute | solution.py:91
  45.8 4.9 %collective-permute-start.10 = (bf16[16,3584]{1,0:T(8,128)(2,1)S(1)}, bf16[16,3584]{1,0:T(8,128)(2,1)S(1)}, u32[]{:S(2)}, u32[]{:S(2)}) collective-permute-start(bf16[16,3584]{1,0:T(8,128)(2,1)S(1)} %slice.85), channel_id=1, source_target_pairs={{0,2},{1,3},{2,0},{3,1},{4,6},{5,7},{6,4},{7,5},{8,9},{9,8},{10,11... | collective-permute-start | bytes 344072 | tf_op jit(solution)/shard_map/ppermute | solution.py:91
  48.4 5.5 %collective-permute-start.14 = (bf16[16,3584]{1,0:T(8,128)(2,1)S(1)}, bf16[16,3584]{1,0:T(8,128)(2,1)S(1)}, u32[]{:S(2)}, u32[]{:S(2)}) collective-permute-start(bf16[16,3584]{1,0:T(8,128)(2,1)S(1)} %slice.84), channel_id=1, source_target_pairs={{0,2},{1,3},{2,0},{3,1},{4,6},{5,7},{6,4},{7,5},{8,9},{9,8},{10,11... | collective-permute-start | bytes 344072 | tf_op jit(solution)/shard_map/ppermute | solution.py:91
  50.7 6.8 %collective-permute-start.11 = (bf16[8,3584]{1,0:T(8,128)(2,1)S(1)}, bf16[8,3584]{1,0:T(8,128)(2,1)S(1)}, u32[]{:S(2)}, u32[]{:S(2)}) collective-permute-start(bf16[8,3584]{1,0:T(8,128)(2,1)S(1)} %slice.87), channel_id=1, source_target_pairs={{0,4},{1,5},{2,6},{3,7},{4,0},{5,1},{6,2},{7,3},{8,12},{9,13},{10,... | collective-permute-start | bytes 172040 | tf_op jit(solution)/shard_map/ppermute | solution.py:91
  53.9 5.1 %collective-permute-start.15 = (bf16[8,3584]{1,0:T(8,128)(2,1)S(1)}, bf16[8,3584]{1,0:T(8,128)(2,1)S(1)}, u32[]{:S(2)}, u32[]{:S(2)}) collective-permute-start(bf16[8,3584]{1,0:T(8,128)(2,1)S(1)} %slice.86), channel_id=1, source_target_pairs={{0,4},{1,5},{2,6},{3,7},{4,0},{5,1},{6,2},{7,3},{8,12},{9,13},{10,... | collective-permute-start | bytes 172040 | tf_op jit(solution)/shard_map/ppermute | solution.py:91

commit v3 on v2

v3 whole, which is shorter than its diff:
```python
import functools

import jax
import jax.numpy as jnp
from jax import lax
from jax.experimental import pallas as pl
from jax.experimental.pallas import tpu as pltpu
from jax.sharding import PartitionSpec as P

EXPERTS = 16
LANES = 128
GATHER_CHUNKS = 2
RETURN_CHUNKS = 2
VM = pltpu.VMEM
F32 = jnp.float32
BF16 = jnp.bfloat16


def in_vmem(array):
    return pltpu.with_memory_space_constraint(array, VM)


def in_hbm(array):
    return pltpu.with_memory_space_constraint(array, pltpu.HBM)


def call(kernel, outs, *args, limit, flops, nbytes, scalars=(), far=()):
    def body(*refs):
        kernel(*refs[: len(scalars)], *refs[len(scalars) + len(far) :])


    return pl.pallas_call(
        body,
        out_shape=outs,
        in_specs=[pl.BlockSpec(memory_space=pltpu.SMEM)] * len(scalars)
        + [pl.BlockSpec(memory_space=pltpu.HBM)] * len(far)
        + [pl.BlockSpec(memory_space=VM)] * len(args),
        out_specs=[pl.BlockSpec(memory_space=VM)] * len(outs),
        compiler_params=pltpu.CompilerParams(vmem_limit_bytes=limit * 2**20),
        cost_estimate=pl.CostEstimate(
            flops=flops, bytes_accessed=nbytes, transcendentals=0
        ),
    )(*scalars, *[in_hbm(x) for x in far], *args)


def level_bits(node_count, bits):
    even = list(range(bits - 1, -1, -1))
    odd = even[:-2] + even[-2:][::-1]
    return [[(even, odd)[n % 2][k] for n in range(node_count)] for k in range(bits)]


def swap(array, level, local_count):
    perm = [
        (n * local_count + i, n * local_count + (i ^ (1 << bit)))
        for n, bit in enumerate(level)
        for i in range(local_count)
    ]
    return lax.ppermute(array, ("node", "local"), perm)


def swap_core(array, node_count):
    return lax.ppermute(array, "node", [(n, n ^ 1) for n in range(node_count)])


def prepare_kernel(_, tokens_far, ids_far, weights_far, __, out, tokens, ids, weights, sems):
    pairs = ((tokens_far, tokens), (ids_far, ids), (weights_far, weights))
    copies = [
        pltpu.make_async_copy(src, dst, sems.at[i]) for i, (src, dst) in enumerate(pairs)
    ]
    for copy in copies:
        copy.start()
    for copy in copies[::-1]:
        copy.wait()
    width = tokens.shape[1]
    lane = lax.broadcasted_iota(jnp.int32, (tokens.shape[0], LANES), 1)
    coef = jnp.zeros((tokens.shape[0], LANES), F32)
    for k in range(ids.shape[1]):
        named = weights[:, k : k + 1].astype(F32)
        coef = coef + jnp.where(lane == ids[:, k : k + 1], named, 0.0)
    out[:, :width] = tokens[...]
    out[:, width:] = coef.astype(BF16)


def prepare(expert, tokens, expert_ids, route_weights, far):
    held = (tokens, expert_ids, route_weights)
    return pl.pallas_call(
        prepare_kernel,
        out_shape=VM((tokens.shape[0], tokens.shape[1] + LANES), BF16),
        in_specs=[pl.BlockSpec(memory_space=pltpu.SMEM)]
        + [pl.BlockSpec(memory_space=pltpu.HBM)] * 4,
        out_specs=pl.BlockSpec(memory_space=VM),
        scratch_shapes=[VM(x.shape, x.dtype) for x in held]
        + [pltpu.SemaphoreType.DMA((3,))],
        compiler_params=pltpu.CompilerParams(vmem_limit_bytes=2**20),
    )(expert, *[in_hbm(x) for x in (*held, far)])


def join_kernel(cuts, own, other, *outs):
    for out, a, b in zip(outs, cuts, cuts[1:]):
        rows = [own[:, a:b].astype(F32), other[:, a:b].astype(F32)]
        out[...] = jnp.concatenate(rows, axis=0).astype(BF16)


def proj_kernel(lo, hi, last, w_gate, w_up, *refs):
    parts, refs = refs[:4], refs[4:]
    gate = up = None
    if lo > 0:
        gate, up = refs[0][...], refs[1][...]
        refs = refs[2:]
    step = 896 if (hi - lo) % 896 == 0 else LANES
    for c in range(lo, hi, step):
        rows = jnp.concatenate([p[:, c - lo : c - lo + step] for p in parts], axis=0)
        g = jnp.dot(rows, w_gate[0, c : c + step, :], preferred_element_type=F32)
        u = jnp.dot(rows, w_up[0, c : c + step, :], preferred_element_type=F32)
        gate = g if gate is None else gate + g
        up = u if up is None else up + u
    if last:
        refs[0][...] = (gate / (1.0 + jnp.exp(-gate)) * up).astype(BF16)
    else:
        refs[0][...] = gate
        refs[1][...] = up


def down_kernel(lo, hi, expert, w_down, hidden, *refs):
    parts, (own_out, other_out) = refs[:-2], refs[-2:]
    half = own_out.shape[0]
    coef = jnp.concatenate([p[:, -LANES:] for p in parts], axis=0).astype(F32)
    lane = lax.broadcasted_iota(jnp.int32, coef.shape, 1)
    coef = jnp.sum(jnp.where(lane == expert[0], coef, 0.0), axis=1, keepdims=True)
    step = 512 if (hi - lo) % 512 == 0 else LANES
    h = hidden[...]
    for c in range(lo, hi, step):
        part = coef * jnp.dot(
            h, w_down[0, :, c : c + step], preferred_element_type=F32
        )
        own_out[:, c - lo : c - lo + step] = part[:half]
        other_out[:, c - lo : c - lo + step] = part[half:].astype(BF16)


def edges(width, chunks):
    tiles = width // LANES
    return [tiles * i // chunks * LANES for i in range(chunks + 1)]


def shards(tokens, expert_ids, route_weights, w_gate, w_up, w_down):
    tok_rows, width = tokens.shape
    hid = w_gate.shape[2]
    node_count = lax.axis_size("node")
    local_count = lax.axis_size("local")
    split_count = node_count * local_count // EXPERTS
    bits = local_count.bit_length() - 1
    levels = level_bits(node_count, bits)
    half = tok_rows * local_count
    rows = 2 * half
    me = lax.axis_index("node") * local_count + lax.axis_index("local")
    expert = (me // split_count).astype(jnp.int32).reshape(1)

    block = prepare(expert, tokens, expert_ids, route_weights, w_down)
    cuts = edges(width, GATHER_CHUNKS)
    wide = cuts[:-1] + [cuts[-1] + LANES]
    for k, level in enumerate(levels[:-1]):
        other = swap(block, level, local_count)
        ends = wide if k == bits - 2 else [0, width + LANES]
        blocks = call(
            functools.partial(join_kernel, ends),
            [VM((2 * block.shape[0], b - a), BF16) for a, b in zip(ends, ends[1:])],
            block,
            other,
            far=(w_down,),
            limit=1,
            flops=0,
            nbytes=200_000,
        )
        block = blocks[0]
    parts = []
    for b in blocks:
        far = swap(b, levels[-1], local_count)
        parts.append([b, far, swap_core(b, node_count), swap_core(far, node_count)])

    w_gate, w_up, w_down = in_vmem(w_gate), in_vmem(w_up), in_vmem(w_down)
    state = ()
    for i in range(GATHER_CHUNKS):
        last = i == GATHER_CHUNKS - 1
        state = call(
            functools.partial(proj_kernel, cuts[i], cuts[i + 1], last),
            [VM((rows, hid), BF16)] if last else [VM((rows, hid), F32)] * 2,
            w_gate,
            w_up,
            *parts[i],
            *state,
            limit=2,
            flops=4 * rows * hid * (cuts[i + 1] - cuts[i]),
            nbytes=4 * hid * (cuts[i + 1] - cuts[i]),
        )
    hidden = state[0]

    cuts = edges(width, RETURN_CHUNKS)
    results = []
    for a, b in zip(cuts, cuts[1:]):
        own, other = call(
            functools.partial(down_kernel, a, b),
            [VM((half, b - a), F32), VM((half, b - a), BF16)],
            w_down,
            hidden,
            *parts[-1],
            scalars=(expert,),
            limit=2,
            flops=2 * rows * hid * (b - a),
            nbytes=2 * hid * (b - a),
        )
        total = own + swap_core(other, node_count).astype(F32)
        for level in levels[::-1]:
            n = total.shape[0] // 2
            total = total[:n] + swap(total[n:].astype(BF16), level, local_count).astype(
                F32
            )
        results.append(total.astype(BF16))
    return jnp.concatenate(results, axis=1)


def solution(mesh):
    return jax.shard_map(
        shards,
        mesh=mesh,
        in_specs=(
            P(("groups", "node", "local"), None),
            P(("groups", "node", "local"), None),
            P(("groups", "node", "local"), None),
            P(("node", "local"), None, None),
            P(("node", "local"), None, None),
            P(("node", "local"), None, None),
        ),
        out_specs=P(("groups", "node", "local"), None),
        check_vma=False,
    )
```

time: 60 us -> 55.6 us (0.927)
  Pallas kernels: 19.9 us -> 8.29 us
  waiting for transfers between devices: 17.7 us -> 28 us
  local copies, waits for them, and re-layouts: 2.99 us -> 0.75 us
  starting transfers between devices: 17.9 us -> 17.1 us
    pallas_call x4 -> x1, Pallas kernels: 12.7 us -> 1.17 us  [prepare(): pl.pallas_call(prepare_kernel, out_shape=VM((tokens.shape[0], tokens.shap...]
    ppermute x10, waiting for transfers between devices: 17.5 us -> 27.7 us  [swap(): return lax.ppermute(array, ('node', 'local'), perm)]
    unnamed x14 -> x24, local copies, waits for them, and re-layouts: 2.89 us -> 0.65 us
    ppermute x10, starting transfers between devices: 16.7 us -> 15.9 us  [swap(): return lax.ppermute(array, ('node', 'local'), perm)]
    pallas_call x7 -> x6, Pallas kernels: 7.2 us -> 7.12 us  [call(): pl.pallas_call(body, out_shape=outs, in_specs=[pl.BlockSpec(memory_space=...]
  transfers between devices with their start and end apart: 16 -> 16, of which waited for: 10 -> 11; matrix products, arithmetic and copies ran while one was open for 1% -> 1% of each run, Pallas kernels for 27% -> 6%
where the time goes in v3:
time: 55.6 us; the launch traced here: 55.5 us
  waiting for transfers between devices  28 us (50%)
  starting transfers between devices  17.1 us (31%)
  Pallas kernels  8.29 us (15%)
  other arithmetic  1.01 us (2%)
  local copies, waits for them, and re-layouts  0.75 us (1%)
    ppermute x10, waiting for transfers between devices, swap(): return lax.ppermute(array, ('node', 'local'), perm)  27.7 us
    ppermute x10, starting transfers between devices, swap(): return lax.ppermute(array, ('node', 'local'), perm)  15.9 us
    pallas_call x6, Pallas kernels, call(): pl.pallas_call(body, out_shape=outs, in_specs=[pl.BlockSpec(memory_space=...  7.12 us
    pallas_call x1, Pallas kernels, prepare(): pl.pallas_call(prepare_kernel, out_shape=VM((tokens.shape[0], tokens.shap...  1.17 us
    ppermute x6, starting transfers between devices, swap_core(): return lax.ppermute(array, 'node', [(n, n ^ 1) for n in range(node_count)])  1.16 us
  transfers between devices with their start and end apart: 16, of which 11 were waited for; matrix products, arithmetic and copies ran while one was open for 1% of the time, Pallas kernels for 6%

profile of v3, /device:TPU:0, one launch (start us, length us, event | category | flops | bytes accessed | tf_op | source)
XLA Modules:
  0.0 55.5 jit_solution(12345519216293560504)
XLA Ops:
  0.0 1.2 %shard_map.64.refs_1_ = bf16[8,7296]{1,0:T(8,128)(2,1)S(1)} custom-call(s32[1]{0:T(128)} %bitcast._.refs_0_, bf16[8,7168]{1,0:T(8,128)(2,1)} %tokens_far.1, s32[8,8]{1,0:T(8,128)} %ids_far.1, bf16[8,8]{1,0:T(8,128)(2,1)} %weights_far.1, bf16[1,1024,7168]{2,1,0:T(8,128)(2,1)} %refs_1_.7), custom_call_target="tpu_custom_call" | custom-call | tf_op jit(solution)/shard_map/pallas_call | solution.py:86
  1.2 4.1 %collective-permute-start = (bf16[8,7296]{1,0:T(8,128)(2,1)S(1)}, bf16[8,7296]{1,0:T(8,128)(2,1)S(1)}, u32[]{:S(2)}, u32[]{:S(2)}) collective-permute-start(bf16[8,7296]{1,0:T(8,128)(2,1)S(1)} %shard_map.64.refs_1_), channel_id=1, source_target_pairs={{0,4},{1,5},{2,6},{3,7},{4,0},{5,1},{6,2},{7,3},{8,12},{9,13},{10,... | collective-permute-start | bytes 350216 | tf_op jit(solution)/shard_map/ppermute | solution.py:58
  5.3 5.7 %collective-permute-done.refs_2_ = bf16[8,7296]{1,0:T(8,128)(2,1)S(1)} collective-permute-done((bf16[8,7296]{1,0:T(8,128)(2,1)S(1)}, bf16[8,7296]{1,0:T(8,128)(2,1)S(1)}, u32[]{:S(2)}, u32[]{:S(2)}) %collective-permute-start) | collective-permute-done | bytes 116768 | tf_op jit(solution)/shard_map/ppermute | solution.py:58
  11.1 0.8 %collective-permute-start.1 = (bf16[16,7296]{1,0:T(8,128)(2,1)S(1)}, bf16[16,7296]{1,0:T(8,128)(2,1)S(1)}, u32[]{:S(2)}, u32[]{:S(2)}) collective-permute-start(bf16[16,7296]{1,0:T(8,128)(2,1)S(1)} %shard_map.65.refs_1_), channel_id=1, source_target_pairs={{0,2},{1,3},{2,0},{3,1},{4,6},{5,7},{6,4},{7,5},{8,9},{9,8},{10,11... | collective-permute-start | bytes 700424 | tf_op jit(solution)/shard_map/ppermute | solution.py:58
  11.9 5.3 %collective-permute-done.1.refs_2_ = bf16[16,7296]{1,0:T(8,128)(2,1)S(1)} collective-permute-done((bf16[16,7296]{1,0:T(8,128)(2,1)S(1)}, bf16[16,7296]{1,0:T(8,128)(2,1)S(1)}, u32[]{:S(2)}, u32[]{:S(2)}) %collective-permute-start.1) | collective-permute-done | bytes 233504 | tf_op jit(solution)/shard_map/ppermute | solution.py:58
  17.2 1.6 %collective-permute-start.5 = (bf16[32,3584]{1,0:T(8,128)(2,1)S(1)}, bf16[32,3584]{1,0:T(8,128)(2,1)S(1)}, u32[]{:S(2)}, u32[]{:S(2)}) collective-permute-start(bf16[32,3584]{1,0:T(8,128)(2,1)S(1)} %get-tuple-element.14.refs_2_), channel_id=1, source_target_pairs={{0,1},{1,0},{2,3},{3,2},{4,5},{5,4},{6,7},{7,6},{8,10},{9,11},{10,... | collective-permute-start | bytes 688136 | tf_op jit(solution)/shard_map/ppermute | solution.py:58
  19.3 4.0 %collective-permute-done.5.refs_3_ = bf16[32,3584]{1,0:T(8,128)(2,1)S(1)} collective-permute-done((bf16[32,3584]{1,0:T(8,128)(2,1)S(1)}, bf16[32,3584]{1,0:T(8,128)(2,1)S(1)}, u32[]{:S(2)}, u32[]{:S(2)}) %collective-permute-start.5) | collective-permute-done | bytes 229408 | tf_op jit(solution)/shard_map/ppermute | solution.py:58
  23.8 2.0 %collective-permute-done.2.refs_3_.refs_4_ = bf16[32,3712]{1,0:T(8,128)(2,1)S(1)} collective-permute-done((bf16[32,3712]{1,0:T(8,128)(2,1)S(1)}, bf16[32,3712]{1,0:T(8,128)(2,1)S(1)}, u32[]{:S(2)}, u32[]{:S(2)}) %collective-permute-start.2) | collective-permute-done | bytes 237600 | tf_op jit(solution)/shard_map/ppermute | solution.py:58
  26.0 2.4 %shard_map.67 = (f32[128,1024]{1,0:T(8,128)S(1)}, f32[128,1024]{1,0:T(8,128)S(1)}) custom-call(bf16[1,7168,1024]{2,1,0:T(8,128)(2,1)S(1)} %bitcast.4, bf16[1,7168,1024]{2,1,0:T(8,128)(2,1)S(1)} %bitcast.6, bf16[32,3584]{1,0:T(8,128)(2,1)S(1)} %get-tuple-element.14.refs_2_, bf16[32,3584]{1,0:T(8,128)(2,1)S(1)} %collective-permute-done.5.refs_3_, ...), custom_call_target="tpu_custom_call" | custom-call | flops 1879048192 | bytes 14680064 | tf_op jit(solution)/shard_map/pallas_call | solution.py:32
  28.4 2.4 %shard_map.68.refs_2_ = bf16[128,1024]{1,0:T(8,128)(2,1)S(1)} custom-call(bf16[1,7168,1024]{2,1,0:T(8,128)(2,1)S(1)} %bitcast.4, bf16[1,7168,1024]{2,1,0:T(8,128)(2,1)S(1)} %bitcast.6, bf16[32,3712]{1,0:T(8,128)(2,1)S(1)} %get-tuple-element.13.refs_2_.refs_3_, bf16[32,3712]{1,0:T(8,128)(2,1)S(1)} %collective-permute-done.2.refs_3_.refs_4_, ...), custom_call_target="tpu_custom_call" | custom-call | flops 1879048192 | bytes 14680064 | tf_op jit(solution)/shard_map/pallas_call | solution.py:32
  31.5 1.1 %shard_map.69 = (f32[64,3584]{1,0:T(8,128)S(1)}, bf16[64,3584]{1,0:T(8,128)(2,1)S(1)}) custom-call(s32[1]{0:T(128)} %bitcast._.refs_0_, bf16[1,1024,7168]{2,1,0:T(8,128)(2,1)S(1)} %bitcast.2, bf16[128,1024]{1,0:T(8,128)(2,1)S(1)} %shard_map.68.refs_2_, bf16[32,3712]{1,0:T(8,128)(2,1)S(1)} %get-tuple-element.13.refs_2_.refs_3_, ...), custom_call_target="tpu_custom_call" | custom-call | flops 939524096 | bytes 7340032 | tf_op jit(solution)/shard_map/pallas_call | solution.py:32
  33.2 1.1 %shard_map.70 = (f32[64,3584]{1,0:T(8,128)S(1)}, bf16[64,3584]{1,0:T(8,128)(2,1)S(1)}) custom-call(s32[1]{0:T(128)} %bitcast._.refs_0_, bf16[1,1024,7168]{2,1,0:T(8,128)(2,1)S(1)} %bitcast.2, bf16[128,1024]{1,0:T(8,128)(2,1)S(1)} %shard_map.68.refs_2_, bf16[32,3712]{1,0:T(8,128)(2,1)S(1)} %get-tuple-element.13.refs_2_.refs_3_, ...), custom_call_target="tpu_custom_call" | custom-call | flops 939524096 | bytes 7340032 | tf_op jit(solution)/shard_map/pallas_call | solution.py:32
  34.7 1.6 %collective-permute-start.9 = (bf16[32,3584]{1,0:T(8,128)(2,1)S(1)}, bf16[32,3584]{1,0:T(8,128)(2,1)S(1)}, u32[]{:S(2)}, u32[]{:S(2)}) collective-permute-start(bf16[32,3584]{1,0:T(8,128)(2,1)S(1)} %slice.83), channel_id=1, source_target_pairs={{0,1},{1,0},{2,3},{3,2},{4,5},{5,4},{6,7},{7,6},{8,10},{9,11},{10,... | collective-permute-start | bytes 688136 | tf_op jit(solution)/shard_map/ppermute | solution.py:58
  36.5 1.5 %collective-permute-start.13 = (bf16[32,3584]{1,0:T(8,128)(2,1)S(1)}, bf16[32,3584]{1,0:T(8,128)(2,1)S(1)}, u32[]{:S(2)}, u32[]{:S(2)}) collective-permute-start(bf16[32,3584]{1,0:T(8,128)(2,1)S(1)} %slice.82), channel_id=1, source_target_pairs={{0,1},{1,0},{2,3},{3,2},{4,5},{5,4},{6,7},{7,6},{8,10},{9,11},{10,... | collective-permute-start | bytes 688136 | tf_op jit(solution)/shard_map/ppermute | solution.py:58
  38.0 2.8 %collective-permute-done.9 = bf16[32,3584]{1,0:T(8,128)(2,1)S(1)} collective-permute-done((bf16[32,3584]{1,0:T(8,128)(2,1)S(1)}, bf16[32,3584]{1,0:T(8,128)(2,1)S(1)}, u32[]{:S(2)}, u32[]{:S(2)}) %collective-permute-start.9) | collective-permute-done | bytes 229408 | tf_op jit(solution)/shard_map/ppermute | solution.py:58
  40.9 0.8 %collective-permute-start.10 = (bf16[16,3584]{1,0:T(8,128)(2,1)S(1)}, bf16[16,3584]{1,0:T(8,128)(2,1)S(1)}, u32[]{:S(2)}, u32[]{:S(2)}) collective-permute-start(bf16[16,3584]{1,0:T(8,128)(2,1)S(1)} %slice.85), channel_id=1, source_target_pairs={{0,2},{1,3},{2,0},{3,1},{4,6},{5,7},{6,4},{7,5},{8,9},{9,8},{10,11... | collective-permute-start | bytes 344072 | tf_op jit(solution)/shard_map/ppermute | solution.py:58
  41.7 1.7 %collective-permute-done.13 = bf16[32,3584]{1,0:T(8,128)(2,1)S(1)} collective-permute-done((bf16[32,3584]{1,0:T(8,128)(2,1)S(1)}, bf16[32,3584]{1,0:T(8,128)(2,1)S(1)}, u32[]{:S(2)}, u32[]{:S(2)}) %collective-permute-start.13) | collective-permute-done | bytes 229408 | tf_op jit(solution)/shard_map/ppermute | solution.py:58
  43.5 0.8 %collective-permute-start.14 = (bf16[16,3584]{1,0:T(8,128)(2,1)S(1)}, bf16[16,3584]{1,0:T(8,128)(2,1)S(1)}, u32[]{:S(2)}, u32[]{:S(2)}) collective-permute-start(bf16[16,3584]{1,0:T(8,128)(2,1)S(1)} %slice.84), channel_id=1, source_target_pairs={{0,2},{1,3},{2,0},{3,1},{4,6},{5,7},{6,4},{7,5},{8,9},{9,8},{10,11... | collective-permute-start | bytes 344072 | tf_op jit(solution)/shard_map/ppermute | solution.py:58
  44.3 1.5 %collective-permute-done.10 = bf16[16,3584]{1,0:T(8,128)(2,1)S(1)} collective-permute-done((bf16[16,3584]{1,0:T(8,128)(2,1)S(1)}, bf16[16,3584]{1,0:T(8,128)(2,1)S(1)}, u32[]{:S(2)}, u32[]{:S(2)}) %collective-permute-start.10) | collective-permute-done | bytes 114720 | tf_op jit(solution)/shard_map/ppermute | solution.py:58
  45.8 2.1 %collective-permute-start.11 = (bf16[8,3584]{1,0:T(8,128)(2,1)S(1)}, bf16[8,3584]{1,0:T(8,128)(2,1)S(1)}, u32[]{:S(2)}, u32[]{:S(2)}) collective-permute-start(bf16[8,3584]{1,0:T(8,128)(2,1)S(1)} %slice.87), channel_id=1, source_target_pairs={{0,4},{1,5},{2,6},{3,7},{4,0},{5,1},{6,2},{7,3},{8,12},{9,13},{10,... | collective-permute-start | bytes 172040 | tf_op jit(solution)/shard_map/ppermute | solution.py:58
  47.9 1.0 %collective-permute-done.14 = bf16[16,3584]{1,0:T(8,128)(2,1)S(1)} collective-permute-done((bf16[16,3584]{1,0:T(8,128)(2,1)S(1)}, bf16[16,3584]{1,0:T(8,128)(2,1)S(1)}, u32[]{:S(2)}, u32[]{:S(2)}) %collective-permute-start.14) | collective-permute-done | bytes 114720 | tf_op jit(solution)/shard_map/ppermute | solution.py:58
  49.0 2.1 %collective-permute-start.15 = (bf16[8,3584]{1,0:T(8,128)(2,1)S(1)}, bf16[8,3584]{1,0:T(8,128)(2,1)S(1)}, u32[]{:S(2)}, u32[]{:S(2)}) collective-permute-start(bf16[8,3584]{1,0:T(8,128)(2,1)S(1)} %slice.86), channel_id=1, source_target_pairs={{0,4},{1,5},{2,6},{3,7},{4,0},{5,1},{6,2},{7,3},{8,12},{9,13},{10,... | collective-permute-start | bytes 172040 | tf_op jit(solution)/shard_map/ppermute | solution.py:58
  51.2 1.5 %collective-permute-done.11 = bf16[8,3584]{1,0:T(8,128)(2,1)S(1)} collective-permute-done((bf16[8,3584]{1,0:T(8,128)(2,1)S(1)}, bf16[8,3584]{1,0:T(8,128)(2,1)S(1)}, u32[]{:S(2)}, u32[]{:S(2)}) %collective-permute-start.11) | collective-permute-done | bytes 57376 | tf_op jit(solution)/shard_map/ppermute | solution.py:58
  52.7 2.1 %collective-permute-done.15 = bf16[8,3584]{1,0:T(8,128)(2,1)S(1)} collective-permute-done((bf16[8,3584]{1,0:T(8,128)(2,1)S(1)}, bf16[8,3584]{1,0:T(8,128)(2,1)S(1)}, u32[]{:S(2)}, u32[]{:S(2)}) %collective-permute-start.15) | collective-permute-done | bytes 57376 | tf_op jit(solution)/shard_map/ppermute | solution.py:58
  (57 shorter events, 3.7 us)
Async XLA Ops:
  0.0 25.9 %slice-start.8 = ((s8[14680064]{0:T(1024)(128)(4,1)}), s8[4194304]{0:T(1024)(128)(4,1)S(1)}, s32[]{:S(2)}) async-start(s8[14680064]{0:T(1024)(128)(4,1)} %bitcast.5), calls=%async_computation.8 | async-start | bytes 8388608
  0.0 25.9 %slice-start.9 = ((s8[14680064]{0:T(1024)(128)(4,1)}), s8[4194304]{0:T(1024)(128)(4,1)S(1)}, s32[]{:S(2)}) async-start(s8[14680064]{0:T(1024)(128)(4,1)} %bitcast.5), calls=%async_computation.9 | async-start | bytes 8388608
  1.2 24.7 %slice-start.4 = ((s8[14680064]{0:T(1024)(128)(4,1)}), s8[4194304]{0:T(1024)(128)(4,1)S(1)}, s32[]{:S(2)}) async-start(s8[14680064]{0:T(1024)(128)(4,1)} %bitcast.3), calls=%async_computation.4 | async-start | bytes 8388608
  1.2 24.7 %slice-start.5 = ((s8[14680064]{0:T(1024)(128)(4,1)}), s8[4194304]{0:T(1024)(128)(4,1)S(1)}, s32[]{:S(2)}) async-start(s8[14680064]{0:T(1024)(128)(4,1)} %bitcast.3), calls=%async_computation.5 | async-start | bytes 8388608
  1.2 24.7 %slice-start.10 = ((s8[14680064]{0:T(1024)(128)(4,1)}), s8[4194304]{0:T(1024)(128)(4,1)S(1)}, s32[]{:S(2)}) async-start(s8[14680064]{0:T(1024)(128)(4,1)} %bitcast.5), calls=%async_computation.10 | async-start | bytes 8388608
  1.2 9.8 %collective-permute-start = (bf16[8,7296]{1,0:T(8,128)(2,1)S(1)}, bf16[8,7296]{1,0:T(8,128)(2,1)S(1)}, u32[]{:S(2)}, u32[]{:S(2)}) collective-permute-start(bf16[8,7296]{1,0:T(8,128)(2,1)S(1)} %shard_map.64.refs_1_), channel_id=1, source_target_pairs={{0,4},{1,5},{2,6},{3,7},{4,0},{5,1},{6,2},{7,3},{8,12},{9,13},{10,... | collective-permute-start | bytes 350216 | tf_op jit(solution)/shard_map/ppermute | solution.py:58
  11.0 14.9 %slice-start.6 = ((s8[14680064]{0:T(1024)(128)(4,1)}), s8[4194304]{0:T(1024)(128)(4,1)S(1)}, s32[]{:S(2)}) async-start(s8[14680064]{0:T(1024)(128)(4,1)} %bitcast.3), calls=%async_computation.6 | async-start | bytes 8388608
  11.1 14.9 %slice-start.7 = ((s8[14680064]{0:T(1024)(128)(4,1)}), s8[2097152]{0:T(1024)(128)(4,1)S(1)}, s32[]{:S(2)}) async-start(s8[14680064]{0:T(1024)(128)(4,1)} %bitcast.3), calls=%async_computation.7 | async-start | bytes 4194304
  11.1 14.9 %slice-start.11 = ((s8[14680064]{0:T(1024)(128)(4,1)}), s8[2097152]{0:T(1024)(128)(4,1)S(1)}, s32[]{:S(2)}) async-start(s8[14680064]{0:T(1024)(128)(4,1)} %bitcast.5), calls=%async_computation.11 | async-start | bytes 4194304
  11.1 6.1 %collective-permute-start.1 = (bf16[16,7296]{1,0:T(8,128)(2,1)S(1)}, bf16[16,7296]{1,0:T(8,128)(2,1)S(1)}, u32[]{:S(2)}, u32[]{:S(2)}) collective-permute-start(bf16[16,7296]{1,0:T(8,128)(2,1)S(1)} %shard_map.65.refs_1_), channel_id=1, source_target_pairs={{0,2},{1,3},{2,0},{3,1},{4,6},{5,7},{6,4},{7,5},{8,9},{9,8},{10,11... | collective-permute-start | bytes 700424 | tf_op jit(solution)/shard_map/ppermute | solution.py:58
  17.2 6.1 %collective-permute-start.5 = (bf16[32,3584]{1,0:T(8,128)(2,1)S(1)}, bf16[32,3584]{1,0:T(8,128)(2,1)S(1)}, u32[]{:S(2)}, u32[]{:S(2)}) collective-permute-start(bf16[32,3584]{1,0:T(8,128)(2,1)S(1)} %get-tuple-element.14.refs_2_), channel_id=1, source_target_pairs={{0,1},{1,0},{2,3},{3,2},{4,5},{5,4},{6,7},{7,6},{8,10},{9,11},{10,... | collective-permute-start | bytes 688136 | tf_op jit(solution)/shard_map/ppermute | solution.py:58
  18.9 7.0 %collective-permute-start.2 = (bf16[32,3712]{1,0:T(8,128)(2,1)S(1)}, bf16[32,3712]{1,0:T(8,128)(2,1)S(1)}, u32[]{:S(2)}, u32[]{:S(2)}) collective-permute-start(bf16[32,3712]{1,0:T(8,128)(2,1)S(1)} %get-tuple-element.13.refs_2_.refs_3_), channel_id=1, source_target_pairs={{0,1},{1,0},{2,3},{3,2},{4,5},{5,4},{6,7},{7,6},{8,10},{9,11},{10,... | collective-permute-start | bytes 712712 | tf_op jit(solution)/shard_map/ppermute | solution.py:58
  19.3 6.5 %collective-permute-start.6 = (bf16[32,3584]{1,0:T(8,128)(2,1)S(1)}, bf16[32,3584]{1,0:T(8,128)(2,1)S(1)}, u32[]{:S(2)}, u32[]{:S(2)}) collective-permute-start(bf16[32,3584]{1,0:T(8,128)(2,1)S(1)} %get-tuple-element.14.refs_2_), channel_id=1, source_target_pairs={{0,8},{8,0},{1,9},{9,1},{2,10},{10,2},{3,11},{11,3},{4,12},{12,4},... | collective-permute-start | bytes 688136 | tf_op jit(solution)/shard_map/ppermute | solution.py:62
  23.3 2.6 %collective-permute-start.7 = (bf16[32,3584]{1,0:T(8,128)(2,1)S(1)}, bf16[32,3584]{1,0:T(8,128)(2,1)S(1)}, u32[]{:S(2)}, u32[]{:S(2)}) collective-permute-start(bf16[32,3584]{1,0:T(8,128)(2,1)S(1)} %collective-permute-done.5.refs_3_), channel_id=1, source_target_pairs={{0,8},{8,0},{1,9},{9,1},{2,10},{10,2},{3,11},{11,3},{4,12},{12,4},... | collective-permute-start | bytes 688136 | tf_op jit(solution)/shard_map/ppermute | solution.py:62
  23.3 5.0 %collective-permute-start.3 = (bf16[32,3712]{1,0:T(8,128)(2,1)S(1)}, bf16[32,3712]{1,0:T(8,128)(2,1)S(1)}, u32[]{:S(2)}, u32[]{:S(2)}) collective-permute-start(bf16[32,3712]{1,0:T(8,128)(2,1)S(1)} %get-tuple-element.13.refs_2_.refs_3_), channel_id=1, source_target_pairs={{0,8},{8,0},{1,9},{9,1},{2,10},{10,2},{3,11},{11,3},{4,12},{12,4},... | collective-permute-start | bytes 712712 | tf_op jit(solution)/shard_map/ppermute | solution.py:62
  25.9 2.5 %collective-permute-start.4 = (bf16[32,3712]{1,0:T(8,128)(2,1)S(1)}, bf16[32,3712]{1,0:T(8,128)(2,1)S(1)}, u32[]{:S(2)}, u32[]{:S(2)}) collective-permute-start(bf16[32,3712]{1,0:T(8,128)(2,1)S(1)} %collective-permute-done.2.refs_3_.refs_4_), channel_id=1, source_target_pairs={{0,8},{8,0},{1,9},{9,1},{2,10},{10,2},{3,11},{11,3},{4,12},{12,4},... | collective-permute-start | bytes 712712 | tf_op jit(solution)/shard_map/ppermute | solution.py:62
  32.6 2.0 %collective-permute-start.8 = (bf16[64,3584]{1,0:T(8,128)(2,1)S(1)}, bf16[64,3584]{1,0:T(8,128)(2,1)S(1)}, u32[]{:S(2)}, u32[]{:S(2)}) collective-permute-start(bf16[64,3584]{1,0:T(8,128)(2,1)S(1)} %get-tuple-element.18), channel_id=1, source_target_pairs={{0,8},{8,0},{1,9},{9,1},{2,10},{10,2},{3,11},{11,3},{4,12},{12,4},... | collective-permute-start | bytes 1376264 | tf_op jit(solution)/shard_map/ppermute | solution.py:62
  34.3 2.1 %collective-permute-start.12 = (bf16[64,3584]{1,0:T(8,128)(2,1)S(1)}, bf16[64,3584]{1,0:T(8,128)(2,1)S(1)}, u32[]{:S(2)}, u32[]{:S(2)}) collective-permute-start(bf16[64,3584]{1,0:T(8,128)(2,1)S(1)} %get-tuple-element.20), channel_id=1, source_target_pairs={{0,8},{8,0},{1,9},{9,1},{2,10},{10,2},{3,11},{11,3},{4,12},{12,4},... | collective-permute-start | bytes 1376264 | tf_op jit(solution)/shard_map/ppermute | solution.py:62
  34.7 6.1 %collective-permute-start.9 = (bf16[32,3584]{1,0:T(8,128)(2,1)S(1)}, bf16[32,3584]{1,0:T(8,128)(2,1)S(1)}, u32[]{:S(2)}, u32[]{:S(2)}) collective-permute-start(bf16[32,3584]{1,0:T(8,128)(2,1)S(1)} %slice.83), channel_id=1, source_target_pairs={{0,1},{1,0},{2,3},{3,2},{4,5},{5,4},{6,7},{7,6},{8,10},{9,11},{10,... | collective-permute-start | bytes 688136 | tf_op jit(solution)/shard_map/ppermute | solution.py:58
  36.5 6.9 %collective-permute-start.13 = (bf16[32,3584]{1,0:T(8,128)(2,1)S(1)}, bf16[32,3584]{1,0:T(8,128)(2,1)S(1)}, u32[]{:S(2)}, u32[]{:S(2)}) collective-permute-start(bf16[32,3584]{1,0:T(8,128)(2,1)S(1)} %slice.82), channel_id=1, source_target_pairs={{0,1},{1,0},{2,3},{3,2},{4,5},{5,4},{6,7},{7,6},{8,10},{9,11},{10,... | collective-permute-start | bytes 688136 | tf_op jit(solution)/shard_map/ppermute | solution.py:58
  40.9 4.9 %collective-permute-start.10 = (bf16[16,3584]{1,0:T(8,128)(2,1)S(1)}, bf16[16,3584]{1,0:T(8,128)(2,1)S(1)}, u32[]{:S(2)}, u32[]{:S(2)}) collective-permute-start(bf16[16,3584]{1,0:T(8,128)(2,1)S(1)} %slice.85), channel_id=1, source_target_pairs={{0,2},{1,3},{2,0},{3,1},{4,6},{5,7},{6,4},{7,5},{8,9},{9,8},{10,11... | collective-permute-start | bytes 344072 | tf_op jit(solution)/shard_map/ppermute | solution.py:58
  43.5 5.5 %collective-permute-start.14 = (bf16[16,3584]{1,0:T(8,128)(2,1)S(1)}, bf16[16,3584]{1,0:T(8,128)(2,1)S(1)}, u32[]{:S(2)}, u32[]{:S(2)}) collective-permute-start(bf16[16,3584]{1,0:T(8,128)(2,1)S(1)} %slice.84), channel_id=1, source_target_pairs={{0,2},{1,3},{2,0},{3,1},{4,6},{5,7},{6,4},{7,5},{8,9},{9,8},{10,11... | collective-permute-start | bytes 344072 | tf_op jit(solution)/shard_map/ppermute | solution.py:58
  45.8 6.9 %collective-permute-start.11 = (bf16[8,3584]{1,0:T(8,128)(2,1)S(1)}, bf16[8,3584]{1,0:T(8,128)(2,1)S(1)}, u32[]{:S(2)}, u32[]{:S(2)}) collective-permute-start(bf16[8,3584]{1,0:T(8,128)(2,1)S(1)} %slice.87), channel_id=1, source_target_pairs={{0,4},{1,5},{2,6},{3,7},{4,0},{5,1},{6,2},{7,3},{8,12},{9,13},{10,... | collective-permute-start | bytes 172040 | tf_op jit(solution)/shard_map/ppermute | solution.py:58
  49.0 5.8 %collective-permute-start.15 = (bf16[8,3584]{1,0:T(8,128)(2,1)S(1)}, bf16[8,3584]{1,0:T(8,128)(2,1)S(1)}, u32[]{:S(2)}, u32[]{:S(2)}) collective-permute-start(bf16[8,3584]{1,0:T(8,128)(2,1)S(1)} %slice.86), channel_id=1, source_target_pairs={{0,4},{1,5},{2,6},{3,7},{4,0},{5,1},{6,2},{7,3},{8,12},{9,13},{10,... | collective-permute-start | bytes 172040 | tf_op jit(solution)/shard_map/ppermute | solution.py:58
  (4 other events, 15.3 us)

commit v4 on v3

v4 whole, which is shorter than its diff:
```python
import functools

import jax
import jax.numpy as jnp
from jax import lax
from jax.experimental import pallas as pl
from jax.experimental.pallas import tpu as pltpu
from jax.sharding import PartitionSpec as P

EXPERTS = 16
LANES = 128
VM = pltpu.VMEM
F32 = jnp.float32
BF16 = jnp.bfloat16


def in_vmem(array):
    return pltpu.with_memory_space_constraint(array, VM)


def in_hbm(array):
    return pltpu.with_memory_space_constraint(array, pltpu.HBM)


def call(kernel, outs, *args, limit, flops, nbytes, scalars=(), far=()):
    def body(*refs):
        kernel(*refs[: len(scalars)], *refs[len(scalars) + len(far) :])


    return pl.pallas_call(
        body,
        out_shape=outs,
        in_specs=[pl.BlockSpec(memory_space=pltpu.SMEM)] * len(scalars)
        + [pl.BlockSpec(memory_space=pltpu.HBM)] * len(far)
        + [pl.BlockSpec(memory_space=VM)] * len(args),
        out_specs=[pl.BlockSpec(memory_space=VM)] * len(outs),
        compiler_params=pltpu.CompilerParams(vmem_limit_bytes=limit * 2**20),
        cost_estimate=pl.CostEstimate(
            flops=flops, bytes_accessed=nbytes, transcendentals=0
        ),
    )(*scalars, *[in_hbm(x) for x in far], *args)


def level_bits(node_count, bits):
    even = list(range(bits - 1, -1, -1))
    odd = even[:-2] + even[-2:][::-1]
    return [[(even, odd)[n % 2][k] for n in range(node_count)] for k in range(bits)]


def swap(array, level, local_count):
    perm = [
        (n * local_count + i, n * local_count + (i ^ (1 << bit)))
        for n, bit in enumerate(level)
        for i in range(local_count)
    ]
    return lax.ppermute(array, ("node", "local"), perm)


def swap_core(array, node_count):
    return lax.ppermute(array, "node", [(n, n ^ 1) for n in range(node_count)])


def prepare_kernel(_, tokens_far, ids_far, weights_far, __, out, tokens, ids, weights, sems):
    pairs = ((tokens_far, tokens), (ids_far, ids), (weights_far, weights))
    copies = [
        pltpu.make_async_copy(src, dst, sems.at[i]) for i, (src, dst) in enumerate(pairs)
    ]
    for copy in copies:
        copy.start()
    for copy in copies[::-1]:
        copy.wait()
    lane = lax.broadcasted_iota(jnp.int32, (tokens.shape[0], LANES), 1)
    coef = jnp.zeros((tokens.shape[0], LANES), F32)
    for k in range(ids.shape[1]):
        named = weights[:, k : k + 1].astype(F32)
        coef = coef + jnp.where(lane == ids[:, k : k + 1], named, 0.0)
    width = tokens.shape[1]
    out[:, :width] = tokens[...]
    out[:, width:] = coef.astype(BF16)


def prepare(expert, tokens, expert_ids, route_weights, far):
    held = (tokens, expert_ids, route_weights)
    return pl.pallas_call(
        prepare_kernel,
        out_shape=VM((tokens.shape[0], tokens.shape[1] + LANES), BF16),
        in_specs=[pl.BlockSpec(memory_space=pltpu.SMEM)]
        + [pl.BlockSpec(memory_space=pltpu.HBM)] * 4,
        out_specs=pl.BlockSpec(memory_space=VM),
        scratch_shapes=[VM(x.shape, x.dtype) for x in held]
        + [pltpu.SemaphoreType.DMA((3,))],
        compiler_params=pltpu.CompilerParams(vmem_limit_bytes=2**20),
        cost_estimate=pl.CostEstimate(
            flops=0, bytes_accessed=200_000, transcendentals=0
        ),
    )(expert, *[in_hbm(x) for x in (*held, far)])


def stacked(refs, columns=slice(None)):
    if any(ref.shape[0] % 16 for ref in refs):
        rows = [ref[:, columns].astype(F32) for ref in refs]
        return jnp.concatenate(rows, axis=0).astype(BF16)
    return jnp.concatenate([ref[:, columns] for ref in refs], axis=0)


def join_kernel(*refs):
    refs[-1][...] = stacked(refs[:-1])


def join(parts, far):
    rows = sum(p.shape[0] for p in parts)
    return call(
        join_kernel,
        [VM((rows, parts[0].shape[1]), BF16)],
        *parts,
        far=far,
        limit=1,
        flops=0,
        nbytes=200_000,
    )[0]


def proj_kernel(w_gate, w_up, *refs):
    parts, hidden = refs[:-1], refs[-1]
    width = w_gate.shape[1]
    step = max(n for n in range(LANES, 1025, LANES) if width % n == 0)
    gate = up = None
    for c in range(0, width, step):
        rows = stacked(parts, slice(c, c + step))
        g = jnp.dot(rows, w_gate[0, c : c + step, :], preferred_element_type=F32)
        u = jnp.dot(rows, w_up[0, c : c + step, :], preferred_element_type=F32)
        gate = g if gate is None else gate + g
        up = u if up is None else up + u
    hidden[...] = (gate / (1.0 + jnp.exp(-gate)) * up).astype(BF16)


def down_kernel(expert, w_down, hidden, *refs):
    parts, outs = refs[:-4], refs[-4:]
    low = outs[0].shape[0]
    coef = stacked(parts, slice(-LANES, None)).astype(F32)
    lane = lax.broadcasted_iota(jnp.int32, coef.shape, 1)
    coef = jnp.sum(jnp.where(lane == expert[0], coef, 0.0), axis=1, keepdims=True)
    width = w_down.shape[2]
    step = max(n for n in range(LANES, 1025, LANES) if width % n == 0)
    h = hidden[...]
    for c in range(0, width, step):
        part = coef * jnp.dot(
            h, w_down[0, :, c : c + step], preferred_element_type=F32
        )
        for i, out in enumerate(outs):
            out[:, c : c + step] = part[i * low : (i + 1) * low].astype(out.dtype)


def shards(tokens, expert_ids, route_weights, w_gate, w_up, w_down):
    tok_rows, width = tokens.shape
    hid = w_gate.shape[2]
    node_count = lax.axis_size("node")
    local_count = lax.axis_size("local")
    split_count = node_count * local_count // EXPERTS
    bits = local_count.bit_length() - 1
    dims = level_bits(node_count, bits)[::-1]
    half = tok_rows * local_count
    rows = 2 * half
    me = lax.axis_index("node") * local_count + lax.axis_index("local")
    expert = (me // split_count).astype(jnp.int32).reshape(1)

    block = prepare(expert, tokens, expert_ids, route_weights, w_down)
    mine = []
    far = swap(block, dims[-1], local_count)
    for k, half_block in enumerate((block, far)):
        for dim in dims[-2:0:-1]:
            other = swap(half_block, dim, local_count)
            half_block = join([half_block, other], (w_down,))
        other = swap(half_block, dims[0], local_count)
        if k == 0:
            mine.append(join([half_block, other], (w_down,)))
        else:
            mine += [half_block, other]
    parts = mine + [swap_core(m, node_count) for m in mine]

    w_gate, w_up, w_down = in_vmem(w_gate), in_vmem(w_up), in_vmem(w_down)
    hidden = call(
        proj_kernel,
        [VM((rows, hid), BF16)],
        w_gate,
        w_up,
        *parts,
        limit=4,
        flops=4 * rows * hid * width,
        nbytes=4 * hid * width,
    )[0]
    low = half // 2
    own_low, own_high, other_low, other_high = call(
        down_kernel,
        [VM((low, width), kind) for kind in (F32, F32, BF16, BF16)],
        w_down,
        hidden,
        *parts,
        scalars=(expert,),
        limit=4,
        flops=2 * rows * hid * width,
        nbytes=2 * hid * width,
    )
    totals = [
        own_high + swap_core(other_high, node_count).astype(F32),
        own_low + swap_core(other_low, node_count).astype(F32),
    ]
    for dim in dims[:-1]:
        n = totals[0].shape[0] // 2
        totals = [
            t[:n] + swap(t[n:].astype(BF16), dim, local_count).astype(F32)
            for t in totals
        ]
    far = swap(totals[0].astype(BF16), dims[-1], local_count)
    return (totals[1] + far.astype(F32)).astype(BF16)


def solution(mesh):
    return jax.shard_map(
        shards,
        mesh=mesh,
        in_specs=(
            P(("groups", "node", "local"), None),
            P(("groups", "node", "local"), None),
            P(("groups", "node", "local"), None),
            P(("node", "local"), None, None),
            P(("node", "local"), None, None),
            P(("node", "local"), None, None),
        ),
        out_specs=P(("groups", "node", "local"), None),
        check_vma=False,
    )
```

time: 55.6 us -> 52.2 us (0.939)
  waiting for transfers between devices: 28 us -> 22.3 us
  starting transfers between devices: 17.1 us -> 21 us
  Pallas kernels: 8.29 us -> 7.33 us
  local copies, waits for them, and re-layouts: 0.75 us -> 0.15 us
    ppermute x10, waiting for transfers between devices: 27.7 us -> 19.5 us  [swap(): return lax.ppermute(array, ('node', 'local'), perm)]
    ppermute x10, starting transfers between devices: 15.9 us -> 19.8 us  [swap(): return lax.ppermute(array, ('node', 'local'), perm)]
    ppermute x6 -> x5, waiting for transfers between devices: 0.23 us -> 2.8 us  [swap_core(): return lax.ppermute(array, 'node', [(n, n ^ 1) for n in range(node_count)])]
    pallas_call x6 -> x5, Pallas kernels: 7.12 us -> 6.3 us  [call(): pl.pallas_call(body, out_shape=outs, in_specs=[pl.BlockSpec(memory_space=...]
    convert_element_type x2, other arithmetic: 0.03 us -> 0.71 us  [the longest x1 0.68 us: shards(): return (totals[1] + far.astype(F32)).astype(BF16)]
    concatenate x1 -> x0, other arithmetic: 0.65 us -> none  [shards(): return jnp.concatenate(results, axis=1)]
    unnamed x24, local copies, waits for them, and re-layouts: 0.65 us -> 0.07 us
    ppermute x6 -> x5, starting transfers between devices: 1.16 us -> 1.15 us  [swap_core(): return lax.ppermute(array, 'node', [(n, n ^ 1) for n in range(node_count)])]
  transfers between devices with their start and end apart: 16 -> 15, of which waited for: 11 -> 11; matrix products, arithmetic and copies ran while one was open for 1% -> 1% of each run, Pallas kernels for 6% -> 0%
where the time goes in v4:
time: 52.2 us; the launch traced here: 52 us
  waiting for transfers between devices  22.3 us (43%)
  starting transfers between devices  21 us (40%)
  Pallas kernels  7.33 us (14%)
  other arithmetic  0.95 us (2%)
    ppermute x10, starting transfers between devices, swap(): return lax.ppermute(array, ('node', 'local'), perm)  19.8 us
    ppermute x10, waiting for transfers between devices, swap(): return lax.ppermute(array, ('node', 'local'), perm)  19.5 us
    pallas_call x5, Pallas kernels, call(): pl.pallas_call(body, out_shape=outs, in_specs=[pl.BlockSpec(memory_space=...  6.3 us
    ppermute x5, waiting for transfers between devices, swap_core(): return lax.ppermute(array, 'node', [(n, n ^ 1) for n in range(node_count)])  2.8 us
    ppermute x5, starting transfers between devices, swap_core(): return lax.ppermute(array, 'node', [(n, n ^ 1) for n in range(node_count)])  1.15 us
  transfers between devices with their start and end apart: 15, of which 11 were waited for; matrix products, arithmetic and copies ran while one was open for 1% of the time, Pallas kernels for 0%

profile of v4, /device:TPU:0, one launch (start us, length us, event | category | flops | bytes accessed | tf_op | source)
XLA Modules:
  0.0 52.0 jit_solution(13885855632261978052)
XLA Ops:
  0.0 1.0 %shard_map.64.refs_1_ = bf16[8,7296]{1,0:T(8,128)(2,1)S(1)} custom-call(s32[1]{0:T(128)} %bitcast._.refs_0_, bf16[8,7168]{1,0:T(8,128)(2,1)} %tokens_far.1, s32[8,8]{1,0:T(8,128)} %ids_far.1, bf16[8,8]{1,0:T(8,128)(2,1)} %weights_far.1, bf16[1,1024,7168]{2,1,0:T(8,128)(2,1)} %refs_1_.3), custom_call_target="tpu_custom_call" | custom-call | bytes 200000 | tf_op jit(solution)/shard_map/pallas_call | solution.py:84
  1.0 3.1 %collective-permute-start = (bf16[8,7296]{1,0:T(8,128)(2,1)S(1)}, bf16[8,7296]{1,0:T(8,128)(2,1)S(1)}, u32[]{:S(2)}, u32[]{:S(2)}) collective-permute-start(bf16[8,7296]{1,0:T(8,128)(2,1)S(1)} %shard_map.64.refs_1_), channel_id=1, source_target_pairs={{0,2},{1,3},{2,0},{3,1},{4,6},{5,7},{6,4},{7,5},{8,9},{9,8},{10,11... | collective-permute-start | bytes 350216 | tf_op jit(solution)/shard_map/ppermute | solution.py:56
  4.1 2.6 %collective-permute-start.2 = (bf16[8,7296]{1,0:T(8,128)(2,1)S(1)}, bf16[8,7296]{1,0:T(8,128)(2,1)S(1)}, u32[]{:S(2)}, u32[]{:S(2)}) collective-permute-start(bf16[8,7296]{1,0:T(8,128)(2,1)S(1)} %shard_map.64.refs_1_), channel_id=1, source_target_pairs={{0,4},{1,5},{2,6},{3,7},{4,0},{5,1},{6,2},{7,3},{8,12},{9,13},{10,... | collective-permute-start | bytes 350216 | tf_op jit(solution)/shard_map/ppermute | solution.py:56
  7.0 3.2 %collective-permute-start.1 = (bf16[16,7296]{1,0:T(8,128)(2,1)S(1)}, bf16[16,7296]{1,0:T(8,128)(2,1)S(1)}, u32[]{:S(2)}, u32[]{:S(2)}) collective-permute-start(bf16[16,7296]{1,0:T(8,128)(2,1)S(1)} %shard_map.65.refs_1_), channel_id=1, source_target_pairs={{0,1},{1,0},{2,3},{3,2},{4,5},{5,4},{6,7},{7,6},{8,10},{9,11},{10,... | collective-permute-start | bytes 700424 | tf_op jit(solution)/shard_map/ppermute | solution.py:56
  10.2 1.4 %collective-permute-done.2.refs_1_ = bf16[8,7296]{1,0:T(8,128)(2,1)S(1)} collective-permute-done((bf16[8,7296]{1,0:T(8,128)(2,1)S(1)}, bf16[8,7296]{1,0:T(8,128)(2,1)S(1)}, u32[]{:S(2)}, u32[]{:S(2)}) %collective-permute-start.2) | collective-permute-done | bytes 116768 | tf_op jit(solution)/shard_map/ppermute | solution.py:56
  11.6 1.5 %collective-permute-start.3 = (bf16[8,7296]{1,0:T(8,128)(2,1)S(1)}, bf16[8,7296]{1,0:T(8,128)(2,1)S(1)}, u32[]{:S(2)}, u32[]{:S(2)}) collective-permute-start(bf16[8,7296]{1,0:T(8,128)(2,1)S(1)} %collective-permute-done.2.refs_1_), channel_id=1, source_target_pairs={{0,2},{1,3},{2,0},{3,1},{4,6},{5,7},{6,4},{7,5},{8,9},{9,8},{10,11... | collective-permute-start | bytes 350216 | tf_op jit(solution)/shard_map/ppermute | solution.py:56
  13.2 3.3 %collective-permute-done.3.refs_2_ = bf16[8,7296]{1,0:T(8,128)(2,1)S(1)} collective-permute-done((bf16[8,7296]{1,0:T(8,128)(2,1)S(1)}, bf16[8,7296]{1,0:T(8,128)(2,1)S(1)}, u32[]{:S(2)}, u32[]{:S(2)}) %collective-permute-start.3) | collective-permute-done | bytes 116768 | tf_op jit(solution)/shard_map/ppermute | solution.py:56
  16.5 1.2 %collective-permute-start.4 = (bf16[16,7296]{1,0:T(8,128)(2,1)S(1)}, bf16[16,7296]{1,0:T(8,128)(2,1)S(1)}, u32[]{:S(2)}, u32[]{:S(2)}) collective-permute-start(bf16[16,7296]{1,0:T(8,128)(2,1)S(1)} %shard_map.67.refs_3_.refs_4_), channel_id=1, source_target_pairs={{0,1},{1,0},{2,3},{3,2},{4,5},{5,4},{6,7},{7,6},{8,10},{9,11},{10,... | collective-permute-start | bytes 700424 | tf_op jit(solution)/shard_map/ppermute | solution.py:56
  17.8 0.5 collective-permute-start.6
  18.3 4.3 %collective-permute-done.4.refs_4_.refs_5_ = bf16[16,7296]{1,0:T(8,128)(2,1)S(1)} collective-permute-done((bf16[16,7296]{1,0:T(8,128)(2,1)S(1)}, bf16[16,7296]{1,0:T(8,128)(2,1)S(1)}, u32[]{:S(2)}, u32[]{:S(2)}) %collective-permute-start.4) | collective-permute-done | bytes 233504 | tf_op jit(solution)/shard_map/ppermute | solution.py:56
  22.6 1.5 %collective-permute-done.7.refs_7_.refs_8_ = bf16[16,7296]{1,0:T(8,128)(2,1)S(1)} collective-permute-done((bf16[16,7296]{1,0:T(8,128)(2,1)S(1)}, bf16[16,7296]{1,0:T(8,128)(2,1)S(1)}, u32[]{:S(2)}, u32[]{:S(2)}) %collective-permute-start.7) | collective-permute-done | bytes 233504 | tf_op jit(solution)/shard_map/ppermute | solution.py:60
  24.2 4.1 %shard_map.68.refs_2_ = bf16[128,1024]{1,0:T(8,128)(2,1)S(1)} custom-call(bf16[1,7168,1024]{2,1,0:T(8,128)(2,1)S(1)} %bitcast.4, bf16[1,7168,1024]{2,1,0:T(8,128)(2,1)S(1)} %bitcast.6, bf16[32,7296]{1,0:T(8,128)(2,1)S(1)} %shard_map.66.refs_2_.refs_3_, bf16[16,7296]{1,0:T(8,128)(2,1)S(1)} %shard_map.67.refs_3_.refs_4_, ...), custom_call_target="tpu_custom_call" | custom-call | flops 3758096384 | bytes 29360128 | tf_op jit(solution)/shard_map/pallas_call | solution.py:30
  28.4 2.1 %shard_map.69 = (f32[32,7168]{1,0:T(8,128)S(1)}, f32[32,7168]{1,0:T(8,128)S(1)}, bf16[32,7168]{1,0:T(8,128)(2,1)S(1)}, bf16[32,7168]{1,0:T(8,128)(2,1)S(1)}) custom-call(s32[1]{0:T(128)} %bitcast._.refs_0_, bf16[1,1024,7168]{2,1,0:T(8,128)(2,1)S(1)} %bitcast.2, bf16[128,1024]{1,0:T(8,128)(2,1)S(1)} %shard_map.68.refs_2_, ...), custom_call_target="tpu_custom_call" | custom-call | flops 1879048192 | bytes 14680064 | tf_op jit(solution)/shard_map/pallas_call | solution.py:30
  31.1 1.3 %collective-permute-done.11 = bf16[32,7168]{1,0:T(8,128)(2,1)S(1)} collective-permute-done((bf16[32,7168]{1,0:T(8,128)(2,1)S(1)}, bf16[32,7168]{1,0:T(8,128)(2,1)S(1)}, u32[]{:S(2)}, u32[]{:S(2)}) %collective-permute-start.11) | collective-permute-done | bytes 458784 | tf_op jit(solution)/shard_map/ppermute | solution.py:60
  32.5 1.2 %collective-permute-start.12 = (bf16[16,7168]{1,0:T(8,128)(2,1)S(1)}, bf16[16,7168]{1,0:T(8,128)(2,1)S(1)}, u32[]{:S(2)}, u32[]{:S(2)}) collective-permute-start(bf16[16,7168]{1,0:T(8,128)(2,1)S(1)} %slice.58), channel_id=1, source_target_pairs={{0,1},{1,0},{2,3},{3,2},{4,5},{5,4},{6,7},{7,6},{8,10},{9,11},{10,... | collective-permute-start | bytes 688136 | tf_op jit(solution)/shard_map/ppermute | solution.py:56
  33.8 1.0 %collective-permute-start.9 = (bf16[16,7168]{1,0:T(8,128)(2,1)S(1)}, bf16[16,7168]{1,0:T(8,128)(2,1)S(1)}, u32[]{:S(2)}, u32[]{:S(2)}) collective-permute-start(bf16[16,7168]{1,0:T(8,128)(2,1)S(1)} %slice.59), channel_id=1, source_target_pairs={{0,1},{1,0},{2,3},{3,2},{4,5},{5,4},{6,7},{7,6},{8,10},{9,11},{10,... | collective-permute-start | bytes 688136 | tf_op jit(solution)/shard_map/ppermute | solution.py:56
  34.8 3.8 %collective-permute-done.12 = bf16[16,7168]{1,0:T(8,128)(2,1)S(1)} collective-permute-done((bf16[16,7168]{1,0:T(8,128)(2,1)S(1)}, bf16[16,7168]{1,0:T(8,128)(2,1)S(1)}, u32[]{:S(2)}, u32[]{:S(2)}) %collective-permute-start.12) | collective-permute-done | bytes 229408 | tf_op jit(solution)/shard_map/ppermute | solution.py:56
  38.7 1.6 %collective-permute-start.13 = (bf16[8,7168]{1,0:T(8,128)(2,1)S(1)}, bf16[8,7168]{1,0:T(8,128)(2,1)S(1)}, u32[]{:S(2)}, u32[]{:S(2)}) collective-permute-start(bf16[8,7168]{1,0:T(8,128)(2,1)S(1)} %slice.60), channel_id=1, source_target_pairs={{0,2},{1,3},{2,0},{3,1},{4,6},{5,7},{6,4},{7,5},{8,9},{9,8},{10,11... | collective-permute-start | bytes 344072 | tf_op jit(solution)/shard_map/ppermute | solution.py:56
  40.3 1.2 %collective-permute-done.9 = bf16[16,7168]{1,0:T(8,128)(2,1)S(1)} collective-permute-done((bf16[16,7168]{1,0:T(8,128)(2,1)S(1)}, bf16[16,7168]{1,0:T(8,128)(2,1)S(1)}, u32[]{:S(2)}, u32[]{:S(2)}) %collective-permute-start.9) | collective-permute-done | bytes 229408 | tf_op jit(solution)/shard_map/ppermute | solution.py:56
  41.5 1.6 %collective-permute-start.10 = (bf16[8,7168]{1,0:T(8,128)(2,1)S(1)}, bf16[8,7168]{1,0:T(8,128)(2,1)S(1)}, u32[]{:S(2)}, u32[]{:S(2)}) collective-permute-start(bf16[8,7168]{1,0:T(8,128)(2,1)S(1)} %slice.61), channel_id=1, source_target_pairs={{0,2},{1,3},{2,0},{3,1},{4,6},{5,7},{6,4},{7,5},{8,9},{9,8},{10,11... | collective-permute-start | bytes 344072 | tf_op jit(solution)/shard_map/ppermute | solution.py:56
  43.6 2.8 %collective-permute-start.14 = (bf16[8,7168]{1,0:T(8,128)(2,1)S(1)}, bf16[8,7168]{1,0:T(8,128)(2,1)S(1)}, u32[]{:S(2)}, u32[]{:S(2)}) collective-permute-start(bf16[8,7168]{1,0:T(8,128)(2,1)S(1)} %fusion), channel_id=1, source_target_pairs={{0,4},{1,5},{2,6},{3,7},{4,0},{5,1},{6,2},{7,3},{8,12},{9,13},{10,... | collective-permute-start | bytes 344072 | tf_op jit(solution)/shard_map/ppermute | solution.py:56
  46.4 1.2 %collective-permute-done.10 = bf16[8,7168]{1,0:T(8,128)(2,1)S(1)} collective-permute-done((bf16[8,7168]{1,0:T(8,128)(2,1)S(1)}, bf16[8,7168]{1,0:T(8,128)(2,1)S(1)}, u32[]{:S(2)}, u32[]{:S(2)}) %collective-permute-start.10) | collective-permute-done | bytes 114720 | tf_op jit(solution)/shard_map/ppermute | solution.py:56
  47.6 3.7 %collective-permute-done.14 = bf16[8,7168]{1,0:T(8,128)(2,1)S(1)} collective-permute-done((bf16[8,7168]{1,0:T(8,128)(2,1)S(1)}, bf16[8,7168]{1,0:T(8,128)(2,1)S(1)}, u32[]{:S(2)}, u32[]{:S(2)}) %collective-permute-start.14) | collective-permute-done | bytes 114720 | tf_op jit(solution)/shard_map/ppermute | solution.py:56
  51.3 0.7 %fusion.2 = bf16[8,7168]{1,0:T(8,128)(2,1)} fusion(f32[16,7168]{1,0:T(8,128)S(1)} %slice_add_fusion.1, bf16[8,7168]{1,0:T(8,128)(2,1)S(1)} %collective-permute-done.14, bf16[8,7168]{1,0:T(8,128)(2,1)S(1)} %collective-permute-done.10), kind=kLoop, calls=%fused_computation.12 | loop fusion | flops 286720 | bytes 573440 | tf_op jit(solution)/shard_map/convert_element_type | solution.py:215
  (49 shorter events, 1.7 us)
Async XLA Ops:
  1.0 5.9 %collective-permute-start = (bf16[8,7296]{1,0:T(8,128)(2,1)S(1)}, bf16[8,7296]{1,0:T(8,128)(2,1)S(1)}, u32[]{:S(2)}, u32[]{:S(2)}) collective-permute-start(bf16[8,7296]{1,0:T(8,128)(2,1)S(1)} %shard_map.64.refs_1_), channel_id=1, source_target_pairs={{0,2},{1,3},{2,0},{3,1},{4,6},{5,7},{6,4},{7,5},{8,9},{9,8},{10,11... | collective-permute-start | bytes 350216 | tf_op jit(solution)/shard_map/ppermute | solution.py:56
  4.1 7.5 %collective-permute-start.2 = (bf16[8,7296]{1,0:T(8,128)(2,1)S(1)}, bf16[8,7296]{1,0:T(8,128)(2,1)S(1)}, u32[]{:S(2)}, u32[]{:S(2)}) collective-permute-start(bf16[8,7296]{1,0:T(8,128)(2,1)S(1)} %shard_map.64.refs_1_), channel_id=1, source_target_pairs={{0,4},{1,5},{2,6},{3,7},{4,0},{5,1},{6,2},{7,3},{8,12},{9,13},{10,... | collective-permute-start | bytes 350216 | tf_op jit(solution)/shard_map/ppermute | solution.py:56
  6.9 17.2 %slice-start.8 = ((s8[14680064]{0:T(1024)(128)(4,1)}), s8[4194304]{0:T(1024)(128)(4,1)S(1)}, s32[]{:S(2)}) async-start(s8[14680064]{0:T(1024)(128)(4,1)} %bitcast.5), calls=%async_computation.8 | async-start | bytes 8388608
  6.9 17.2 %slice-start.9 = ((s8[14680064]{0:T(1024)(128)(4,1)}), s8[4194304]{0:T(1024)(128)(4,1)S(1)}, s32[]{:S(2)}) async-start(s8[14680064]{0:T(1024)(128)(4,1)} %bitcast.5), calls=%async_computation.9 | async-start | bytes 8388608
  6.9 17.2 %slice-start.4 = ((s8[14680064]{0:T(1024)(128)(4,1)}), s8[4194304]{0:T(1024)(128)(4,1)S(1)}, s32[]{:S(2)}) async-start(s8[14680064]{0:T(1024)(128)(4,1)} %bitcast.3), calls=%async_computation.4 | async-start | bytes 8388608
  7.0 17.2 %slice-start.5 = ((s8[14680064]{0:T(1024)(128)(4,1)}), s8[4194304]{0:T(1024)(128)(4,1)S(1)}, s32[]{:S(2)}) async-start(s8[14680064]{0:T(1024)(128)(4,1)} %bitcast.3), calls=%async_computation.5 | async-start | bytes 8388608
  7.0 17.2 %slice-start.10 = ((s8[14680064]{0:T(1024)(128)(4,1)}), s8[4194304]{0:T(1024)(128)(4,1)S(1)}, s32[]{:S(2)}) async-start(s8[14680064]{0:T(1024)(128)(4,1)} %bitcast.5), calls=%async_computation.10 | async-start | bytes 8388608
  7.0 10.7 %collective-permute-start.1 = (bf16[16,7296]{1,0:T(8,128)(2,1)S(1)}, bf16[16,7296]{1,0:T(8,128)(2,1)S(1)}, u32[]{:S(2)}, u32[]{:S(2)}) collective-permute-start(bf16[16,7296]{1,0:T(8,128)(2,1)S(1)} %shard_map.65.refs_1_), channel_id=1, source_target_pairs={{0,1},{1,0},{2,3},{3,2},{4,5},{5,4},{6,7},{7,6},{8,10},{9,11},{10,... | collective-permute-start | bytes 700424 | tf_op jit(solution)/shard_map/ppermute | solution.py:56
  11.6 4.8 %collective-permute-start.3 = (bf16[8,7296]{1,0:T(8,128)(2,1)S(1)}, bf16[8,7296]{1,0:T(8,128)(2,1)S(1)}, u32[]{:S(2)}, u32[]{:S(2)}) collective-permute-start(bf16[8,7296]{1,0:T(8,128)(2,1)S(1)} %collective-permute-done.2.refs_1_), channel_id=1, source_target_pairs={{0,2},{1,3},{2,0},{3,1},{4,6},{5,7},{6,4},{7,5},{8,9},{9,8},{10,11... | collective-permute-start | bytes 350216 | tf_op jit(solution)/shard_map/ppermute | solution.py:56
  16.5 6.1 %collective-permute-start.4 = (bf16[16,7296]{1,0:T(8,128)(2,1)S(1)}, bf16[16,7296]{1,0:T(8,128)(2,1)S(1)}, u32[]{:S(2)}, u32[]{:S(2)}) collective-permute-start(bf16[16,7296]{1,0:T(8,128)(2,1)S(1)} %shard_map.67.refs_3_.refs_4_), channel_id=1, source_target_pairs={{0,1},{1,0},{2,3},{3,2},{4,5},{5,4},{6,7},{7,6},{8,10},{9,11},{10,... | collective-permute-start | bytes 700424 | tf_op jit(solution)/shard_map/ppermute | solution.py:56
  17.7 10.7 %slice-start = ((s8[14680064]{0:T(1024)(128)(4,1)}), s8[4194304]{0:T(1024)(128)(4,1)S(1)}, s32[]{:S(2)}) async-start(s8[14680064]{0:T(1024)(128)(4,1)} %bitcast.1), calls=%async_computation | async-start | bytes 8388608
  17.7 10.7 %slice-start.1 = ((s8[14680064]{0:T(1024)(128)(4,1)}), s8[4194304]{0:T(1024)(128)(4,1)S(1)}, s32[]{:S(2)}) async-start(s8[14680064]{0:T(1024)(128)(4,1)} %bitcast.1), calls=%async_computation.1 | async-start | bytes 8388608
  17.7 10.6 %slice-start.2 = ((s8[14680064]{0:T(1024)(128)(4,1)}), s8[4194304]{0:T(1024)(128)(4,1)S(1)}, s32[]{:S(2)}) async-start(s8[14680064]{0:T(1024)(128)(4,1)} %bitcast.1), calls=%async_computation.2 | async-start | bytes 8388608
  17.8 10.6 %slice-start.3 = ((s8[14680064]{0:T(1024)(128)(4,1)}), s8[2097152]{0:T(1024)(128)(4,1)S(1)}, s32[]{:S(2)}) async-start(s8[14680064]{0:T(1024)(128)(4,1)} %bitcast.1), calls=%async_computation.3 | async-start | bytes 4194304
  17.8 6.4 %collective-permute-start.5 = (bf16[32,7296]{1,0:T(8,128)(2,1)S(1)}, bf16[32,7296]{1,0:T(8,128)(2,1)S(1)}, u32[]{:S(2)}, u32[]{:S(2)}) collective-permute-start(bf16[32,7296]{1,0:T(8,128)(2,1)S(1)} %shard_map.66.refs_2_.refs_3_), channel_id=1, source_target_pairs={{0,8},{8,0},{1,9},{9,1},{2,10},{10,2},{3,11},{11,3},{4,12},{12,4},... | collective-permute-start | bytes 1400840 | tf_op jit(solution)/shard_map/ppermute | solution.py:60
  17.8 4.8 %collective-permute-start.6 = (bf16[16,7296]{1,0:T(8,128)(2,1)S(1)}, bf16[16,7296]{1,0:T(8,128)(2,1)S(1)}, u32[]{:S(2)}, u32[]{:S(2)}) collective-permute-start(bf16[16,7296]{1,0:T(8,128)(2,1)S(1)} %shard_map.67.refs_3_.refs_4_), channel_id=1, source_target_pairs={{0,8},{8,0},{1,9},{9,1},{2,10},{10,2},{3,11},{11,3},{4,12},{12,4},... | collective-permute-start | bytes 700424 | tf_op jit(solution)/shard_map/ppermute | solution.py:60
  22.6 1.5 %collective-permute-start.7 = (bf16[16,7296]{1,0:T(8,128)(2,1)S(1)}, bf16[16,7296]{1,0:T(8,128)(2,1)S(1)}, u32[]{:S(2)}, u32[]{:S(2)}) collective-permute-start(bf16[16,7296]{1,0:T(8,128)(2,1)S(1)} %collective-permute-done.4.refs_4_.refs_5_), channel_id=1, source_target_pairs={{0,8},{8,0},{1,9},{9,1},{2,10},{10,2},{3,11},{11,3},{4,12},{12,4},... | collective-permute-start | bytes 700424 | tf_op jit(solution)/shard_map/ppermute | solution.py:60
  30.5 1.9 %collective-permute-start.11 = (bf16[32,7168]{1,0:T(8,128)(2,1)S(1)}, bf16[32,7168]{1,0:T(8,128)(2,1)S(1)}, u32[]{:S(2)}, u32[]{:S(2)}) collective-permute-start(bf16[32,7168]{1,0:T(8,128)(2,1)S(1)} %get-tuple-element.12), channel_id=1, source_target_pairs={{0,8},{8,0},{1,9},{9,1},{2,10},{10,2},{3,11},{11,3},{4,12},{12,4},... | collective-permute-start | bytes 1376264 | tf_op jit(solution)/shard_map/ppermute | solution.py:60
  30.7 3.0 %collective-permute-start.8 = (bf16[32,7168]{1,0:T(8,128)(2,1)S(1)}, bf16[32,7168]{1,0:T(8,128)(2,1)S(1)}, u32[]{:S(2)}, u32[]{:S(2)}) collective-permute-start(bf16[32,7168]{1,0:T(8,128)(2,1)S(1)} %get-tuple-element.10), channel_id=1, source_target_pairs={{0,8},{8,0},{1,9},{9,1},{2,10},{10,2},{3,11},{11,3},{4,12},{12,4},... | collective-permute-start | bytes 1376264 | tf_op jit(solution)/shard_map/ppermute | solution.py:60
  32.5 6.1 %collective-permute-start.12 = (bf16[16,7168]{1,0:T(8,128)(2,1)S(1)}, bf16[16,7168]{1,0:T(8,128)(2,1)S(1)}, u32[]{:S(2)}, u32[]{:S(2)}) collective-permute-start(bf16[16,7168]{1,0:T(8,128)(2,1)S(1)} %slice.58), channel_id=1, source_target_pairs={{0,1},{1,0},{2,3},{3,2},{4,5},{5,4},{6,7},{7,6},{8,10},{9,11},{10,... | collective-permute-start | bytes 688136 | tf_op jit(solution)/shard_map/ppermute | solution.py:56
  33.8 7.6 %collective-permute-start.9 = (bf16[16,7168]{1,0:T(8,128)(2,1)S(1)}, bf16[16,7168]{1,0:T(8,128)(2,1)S(1)}, u32[]{:S(2)}, u32[]{:S(2)}) collective-permute-start(bf16[16,7168]{1,0:T(8,128)(2,1)S(1)} %slice.59), channel_id=1, source_target_pairs={{0,1},{1,0},{2,3},{3,2},{4,5},{5,4},{6,7},{7,6},{8,10},{9,11},{10,... | collective-permute-start | bytes 688136 | tf_op jit(solution)/shard_map/ppermute | solution.py:56
  38.7 4.9 %collective-permute-start.13 = (bf16[8,7168]{1,0:T(8,128)(2,1)S(1)}, bf16[8,7168]{1,0:T(8,128)(2,1)S(1)}, u32[]{:S(2)}, u32[]{:S(2)}) collective-permute-start(bf16[8,7168]{1,0:T(8,128)(2,1)S(1)} %slice.60), channel_id=1, source_target_pairs={{0,2},{1,3},{2,0},{3,1},{4,6},{5,7},{6,4},{7,5},{8,9},{9,8},{10,11... | collective-permute-start | bytes 344072 | tf_op jit(solution)/shard_map/ppermute | solution.py:56
  41.5 6.1 %collective-permute-start.10 = (bf16[8,7168]{1,0:T(8,128)(2,1)S(1)}, bf16[8,7168]{1,0:T(8,128)(2,1)S(1)}, u32[]{:S(2)}, u32[]{:S(2)}) collective-permute-start(bf16[8,7168]{1,0:T(8,128)(2,1)S(1)} %slice.61), channel_id=1, source_target_pairs={{0,2},{1,3},{2,0},{3,1},{4,6},{5,7},{6,4},{7,5},{8,9},{9,8},{10,11... | collective-permute-start | bytes 344072 | tf_op jit(solution)/shard_map/ppermute | solution.py:56
  43.6 7.7 %collective-permute-start.14 = (bf16[8,7168]{1,0:T(8,128)(2,1)S(1)}, bf16[8,7168]{1,0:T(8,128)(2,1)S(1)}, u32[]{:S(2)}, u32[]{:S(2)}) collective-permute-start(bf16[8,7168]{1,0:T(8,128)(2,1)S(1)} %fusion), channel_id=1, source_target_pairs={{0,4},{1,5},{2,6},{3,7},{4,0},{5,1},{6,2},{7,3},{8,12},{9,13},{10,... | collective-permute-start | bytes 344072 | tf_op jit(solution)/shard_map/ppermute | solution.py:56
  (3 other events, 23.1 us)

commit v5 on v4

--- a/solution.py
+++ b/solution.py
@@ -47,13 +47,19 @@
     return [[(even, odd)[n % 2][k] for n in range(node_count)] for k in range(bits)]
 
 
-def swap(array, level, local_count):
-    perm = [
-        (n * local_count + i, n * local_count + (i ^ (1 << bit)))
-        for n, bit in enumerate(level)
-        for i in range(local_count)
-    ]
+def swap_across(array, dims, mask, local_count):
+    perm = []
+    for n in range(len(dims[0])):
+        across = sum(1 << level[n] for k, level in enumerate(dims) if mask >> k & 1)
+        perm += [
+            (n * local_count + i, n * local_count + (i ^ across))
+            for i in range(local_count)
+        ]
     return lax.ppermute(array, ("node", "local"), perm)
+
+
+def swap(array, dim, local_count):
+    return swap_across(array, [dim], 1, local_count)
 
 
 def swap_core(array, node_count):
@@ -164,18 +170,17 @@
     me = lax.axis_index("node") * local_count + lax.axis_index("local")
     expert = (me // split_count).astype(jnp.int32).reshape(1)
 
-    block = prepare(expert, tokens, expert_ids, route_weights, w_down)
-    mine = []
-    far = swap(block, dims[-1], local_count)
-    for k, half_block in enumerate((block, far)):
-        for dim in dims[-2:0:-1]:
-            other = swap(half_block, dim, local_count)
-            half_block = join([half_block, other], (w_down,))
-        other = swap(half_block, dims[0], local_count)
-        if k == 0:
-            mine.append(join([half_block, other], (w_down,)))
-        else:
-            mine += [half_block, other]
+    side = local_count // 2
+    masks = [
+        sum(1 << k for k in range(bits - 1) if i >> (bits - 2 - k) & 1)
+        for i in range(side)
+    ]
+    near = prepare(expert, tokens, expert_ids, route_weights, w_down)
+    far = [swap(near, dims[-1], local_count)]
+    far += [swap_across(far[0], dims, m, local_count) for m in masks[1:]]
+    for dim in dims[-2::-1]:
+        near = join([near, swap(near, dim, local_count)], (w_down,))
+    mine = [near, join(far, (w_down,))]
     parts = mine + [swap_core(m, node_count) for m in mine]
 
     w_gate, w_up, w_down = in_vmem(w_gate), in_vmem(w_up), in_vmem(w_down)
@@ -201,18 +206,25 @@
         flops=2 * rows * hid * width,
         nbytes=2 * hid * width,
     )
-    totals = [
-        own_high + swap_core(other_high, node_count).astype(F32),
-        own_low + swap_core(other_low, node_count).astype(F32),
-    ]
+    def halve(total, dim):
+        n = total.shape[0] // 2
+        return total[:n] + swap(total[n:].astype(BF16), dim, local_count).astype(F32)
+
+    def gather_side(rows):
+        total = rows[:tok_rows]
+        for i in range(1, local_count // 2):
+            part = rows[i * tok_rows : (i + 1) * tok_rows].astype(BF16)
+            mask = sum(1 << k for k in range(bits - 1) if i >> (bits - 2 - k) & 1)
+            total = total + swap_across(part, dims, mask, local_count).astype(F32)
+        return total
+
+    far = own_high + swap_core(other_high, node_count).astype(F32)
+    near = own_low + swap_core(other_low, node_count).astype(F32)
+    far = gather_side(far)
     for dim in dims[:-1]:
-        n = totals[0].shape[0] // 2
-        totals = [
-            t[:n] + swap(t[n:].astype(BF16), dim, local_count).astype(F32)
-            for t in totals
-        ]
-    far = swap(totals[0].astype(BF16), dims[-1], local_count)
-    return (totals[1] + far.astype(F32)).astype(BF16)
+        near = halve(near, dim)
+    far = swap(far.astype(BF16), dims[-1], local_count)
+    return (near + far.astype(F32)).astype(BF16)
 
 
 def solution(mesh):

time: 52.2 us -> 49.8 us (0.954)
  waiting for transfers between devices: 22.3 us -> 17.6 us
  starting transfers between devices: 21 us -> 23.3 us
    ppermute x10 -> x12, waiting for transfers between devices: 19.5 us -> 14.4 us  [swap_across(): return lax.ppermute(array, ('node', 'local'), perm)]
    ppermute x10 -> x12, starting transfers between devices: 19.8 us -> 22.2 us  [swap_across(): return lax.ppermute(array, ('node', 'local'), perm)]
    ppermute x5 -> x4, waiting for transfers between devices: 2.8 us -> 3.16 us  [swap_core(): return lax.ppermute(array, 'node', [(n, n ^ 1) for n in range(node_count)])]
    ppermute x5 -> x4, starting transfers between devices: 1.15 us -> 1.18 us  [swap_core(): return lax.ppermute(array, 'node', [(n, n ^ 1) for n in range(node_count)])]
  transfers between devices with their start and end apart: 15 -> 16, of which waited for: 11 -> 12; matrix products, arithmetic and copies ran while one was open for 1% -> 1% of each run, Pallas kernels for 0% -> 0%
where the time goes in v5:
time: 49.8 us; the launch traced here: 49.6 us
  starting transfers between devices  23.3 us (47%)
  waiting for transfers between devices  17.6 us (35%)
  Pallas kernels  7.31 us (15%)
  other arithmetic  0.97 us (2%)
    ppermute x12, starting transfers between devices, swap_across(): return lax.ppermute(array, ('node', 'local'), perm)  22.2 us
    ppermute x12, waiting for transfers between devices, swap_across(): return lax.ppermute(array, ('node', 'local'), perm)  14.4 us
    pallas_call x5, Pallas kernels, call(): pl.pallas_call(body, out_shape=outs, in_specs=[pl.BlockSpec(memory_space=...  6.29 us
    ppermute x4, waiting for transfers between devices, swap_core(): return lax.ppermute(array, 'node', [(n, n ^ 1) for n in range(node_count)])  3.16 us
    ppermute x4, starting transfers between devices, swap_core(): return lax.ppermute(array, 'node', [(n, n ^ 1) for n in range(node_count)])  1.18 us
    pallas_call x1, Pallas kernels, prepare(): pl.pallas_call(prepare_kernel, out_shape=VM((tokens.shape[0], tokens.shap...  1.02 us
  transfers between devices with their start and end apart: 16, of which 12 were waited for; matrix products, arithmetic and copies ran while one was open for 1% of the time, Pallas kernels for 0%

profile of v5, /device:TPU:0, one launch (start us, length us, event | category | flops | bytes accessed | tf_op | source)
XLA Modules:
  0.0 49.6 jit_solution(15323710237301931588)
XLA Ops:
  0.0 1.0 %shard_map.64.refs_1_ = bf16[8,7296]{1,0:T(8,128)(2,1)S(1)} custom-call(s32[1]{0:T(128)} %bitcast._.refs_0_, bf16[8,7168]{1,0:T(8,128)(2,1)} %tokens_far.1, s32[8,8]{1,0:T(8,128)} %ids_far.1, bf16[8,8]{1,0:T(8,128)(2,1)} %weights_far.1, bf16[1,1024,7168]{2,1,0:T(8,128)(2,1)} %refs_1_.3), custom_call_target="tpu_custom_call" | custom-call | bytes 200000 | tf_op jit(solution)/shard_map/pallas_call | solution.py:90
  1.0 3.1 %collective-permute-start = (bf16[8,7296]{1,0:T(8,128)(2,1)S(1)}, bf16[8,7296]{1,0:T(8,128)(2,1)S(1)}, u32[]{:S(2)}, u32[]{:S(2)}) collective-permute-start(bf16[8,7296]{1,0:T(8,128)(2,1)S(1)} %shard_map.64.refs_1_), channel_id=1, source_target_pairs={{0,2},{1,3},{2,0},{3,1},{4,6},{5,7},{6,4},{7,5},{8,9},{9,8},{10,11... | collective-permute-start | bytes 350216 | tf_op jit(solution)/shard_map/ppermute | solution.py:58
  4.1 2.6 %collective-permute-start.2 = (bf16[8,7296]{1,0:T(8,128)(2,1)S(1)}, bf16[8,7296]{1,0:T(8,128)(2,1)S(1)}, u32[]{:S(2)}, u32[]{:S(2)}) collective-permute-start(bf16[8,7296]{1,0:T(8,128)(2,1)S(1)} %shard_map.64.refs_1_), channel_id=1, source_target_pairs={{0,4},{1,5},{2,6},{3,7},{4,0},{5,1},{6,2},{7,3},{8,12},{9,13},{10,... | collective-permute-start | bytes 350216 | tf_op jit(solution)/shard_map/ppermute | solution.py:58
  7.0 3.2 %collective-permute-start.1 = (bf16[16,7296]{1,0:T(8,128)(2,1)S(1)}, bf16[16,7296]{1,0:T(8,128)(2,1)S(1)}, u32[]{:S(2)}, u32[]{:S(2)}) collective-permute-start(bf16[16,7296]{1,0:T(8,128)(2,1)S(1)} %shard_map.65.refs_1_), channel_id=1, source_target_pairs={{0,1},{1,0},{2,3},{3,2},{4,5},{5,4},{6,7},{7,6},{8,10},{9,11},{10,... | collective-permute-start | bytes 700424 | tf_op jit(solution)/shard_map/ppermute | solution.py:58
  10.2 1.4 %collective-permute-done.2.refs_1_ = bf16[8,7296]{1,0:T(8,128)(2,1)S(1)} collective-permute-done((bf16[8,7296]{1,0:T(8,128)(2,1)S(1)}, bf16[8,7296]{1,0:T(8,128)(2,1)S(1)}, u32[]{:S(2)}, u32[]{:S(2)}) %collective-permute-start.2) | collective-permute-done | bytes 116768 | tf_op jit(solution)/shard_map/ppermute | solution.py:58
  11.6 1.2 %collective-permute-start.5 = (bf16[8,7296]{1,0:T(8,128)(2,1)S(1)}, bf16[8,7296]{1,0:T(8,128)(2,1)S(1)}, u32[]{:S(2)}, u32[]{:S(2)}) collective-permute-start(bf16[8,7296]{1,0:T(8,128)(2,1)S(1)} %collective-permute-done.2.refs_1_), channel_id=1, source_target_pairs={{0,3},{1,2},{2,1},{3,0},{4,7},{5,6},{6,5},{7,4},{8,11},{9,10},{10,... | collective-permute-start | bytes 350216 | tf_op jit(solution)/shard_map/ppermute | solution.py:58
  12.8 1.8 %collective-permute-start.4 = (bf16[8,7296]{1,0:T(8,128)(2,1)S(1)}, bf16[8,7296]{1,0:T(8,128)(2,1)S(1)}, u32[]{:S(2)}, u32[]{:S(2)}) collective-permute-start(bf16[8,7296]{1,0:T(8,128)(2,1)S(1)} %collective-permute-done.2.refs_1_), channel_id=1, source_target_pairs={{0,1},{1,0},{2,3},{3,2},{4,5},{5,4},{6,7},{7,6},{8,10},{9,11},{10,... | collective-permute-start | bytes 350216 | tf_op jit(solution)/shard_map/ppermute | solution.py:58
  14.6 0.5 %collective-permute-start.3 = (bf16[8,7296]{1,0:T(8,128)(2,1)S(1)}, bf16[8,7296]{1,0:T(8,128)(2,1)S(1)}, u32[]{:S(2)}, u32[]{:S(2)}) collective-permute-start(bf16[8,7296]{1,0:T(8,128)(2,1)S(1)} %collective-permute-done.2.refs_1_), channel_id=1, source_target_pairs={{0,2},{1,3},{2,0},{3,1},{4,6},{5,7},{6,4},{7,5},{8,9},{9,8},{10,11... | collective-permute-start | bytes 350216 | tf_op jit(solution)/shard_map/ppermute | solution.py:58
  15.1 3.5 %collective-permute-done.5.refs_4_ = bf16[8,7296]{1,0:T(8,128)(2,1)S(1)} collective-permute-done((bf16[8,7296]{1,0:T(8,128)(2,1)S(1)}, bf16[8,7296]{1,0:T(8,128)(2,1)S(1)}, u32[]{:S(2)}, u32[]{:S(2)}) %collective-permute-start.5) | collective-permute-done | bytes 116768 | tf_op jit(solution)/shard_map/ppermute | solution.py:58
  18.7 0.6 %collective-permute-done.4.refs_3_ = bf16[8,7296]{1,0:T(8,128)(2,1)S(1)} collective-permute-done((bf16[8,7296]{1,0:T(8,128)(2,1)S(1)}, bf16[8,7296]{1,0:T(8,128)(2,1)S(1)}, u32[]{:S(2)}, u32[]{:S(2)}) %collective-permute-start.4) | collective-permute-done | bytes 116768 | tf_op jit(solution)/shard_map/ppermute | solution.py:58
  19.7 0.5 %collective-permute-start.6 = (bf16[32,7296]{1,0:T(8,128)(2,1)S(1)}, bf16[32,7296]{1,0:T(8,128)(2,1)S(1)}, u32[]{:S(2)}, u32[]{:S(2)}) collective-permute-start(bf16[32,7296]{1,0:T(8,128)(2,1)S(1)} %shard_map.66.refs_2_.refs_3_), channel_id=1, source_target_pairs={{0,8},{8,0},{1,9},{9,1},{2,10},{10,2},{3,11},{11,3},{4,12},{12,4},... | collective-permute-start | bytes 1400840 | tf_op jit(solution)/shard_map/ppermute | solution.py:66
  20.2 1.2 %collective-permute-done.7.refs_5_.refs_6_ = bf16[32,7296]{1,0:T(8,128)(2,1)S(1)} collective-permute-done((bf16[32,7296]{1,0:T(8,128)(2,1)S(1)}, bf16[32,7296]{1,0:T(8,128)(2,1)S(1)}, u32[]{:S(2)}, u32[]{:S(2)}) %collective-permute-start.7) | collective-permute-done | bytes 466976 | tf_op jit(solution)/shard_map/ppermute | solution.py:66
  21.4 0.7 %collective-permute-done.6.refs_4_.refs_5_ = bf16[32,7296]{1,0:T(8,128)(2,1)S(1)} collective-permute-done((bf16[32,7296]{1,0:T(8,128)(2,1)S(1)}, bf16[32,7296]{1,0:T(8,128)(2,1)S(1)}, u32[]{:S(2)}, u32[]{:S(2)}) %collective-permute-start.6) | collective-permute-done | bytes 466976 | tf_op jit(solution)/shard_map/ppermute | solution.py:66
  22.1 4.1 %shard_map.68.refs_2_ = bf16[128,1024]{1,0:T(8,128)(2,1)S(1)} custom-call(bf16[1,7168,1024]{2,1,0:T(8,128)(2,1)S(1)} %bitcast.4, bf16[1,7168,1024]{2,1,0:T(8,128)(2,1)S(1)} %bitcast.6, bf16[32,7296]{1,0:T(8,128)(2,1)S(1)} %shard_map.66.refs_2_.refs_3_, bf16[32,7296]{1,0:T(8,128)(2,1)S(1)} %shard_map.67.refs_3_.refs_4_, ...), custom_call_target="tpu_custom_call" | custom-call | flops 3758096384 | bytes 29360128 | tf_op jit(solution)/shard_map/pallas_call | solution.py:30
  26.3 2.1 %shard_map.69 = (f32[32,7168]{1,0:T(8,128)S(1)}, f32[32,7168]{1,0:T(8,128)S(1)}, bf16[32,7168]{1,0:T(8,128)(2,1)S(1)}, bf16[32,7168]{1,0:T(8,128)(2,1)S(1)}) custom-call(s32[1]{0:T(128)} %bitcast._.refs_0_, bf16[1,1024,7168]{2,1,0:T(8,128)(2,1)S(1)} %bitcast.2, bf16[128,1024]{1,0:T(8,128)(2,1)S(1)} %shard_map.68.refs_2_, ...), custom_call_target="tpu_custom_call" | custom-call | flops 1879048192 | bytes 14680064 | tf_op jit(solution)/shard_map/pallas_call | solution.py:30
  29.0 1.3 %collective-permute-done.11 = bf16[32,7168]{1,0:T(8,128)(2,1)S(1)} collective-permute-done((bf16[32,7168]{1,0:T(8,128)(2,1)S(1)}, bf16[32,7168]{1,0:T(8,128)(2,1)S(1)}, u32[]{:S(2)}, u32[]{:S(2)}) %collective-permute-start.11) | collective-permute-done | bytes 458784 | tf_op jit(solution)/shard_map/ppermute | solution.py:66
  30.4 2.0 %collective-permute-start.12 = (bf16[8,7168]{1,0:T(8,128)(2,1)S(1)}, bf16[8,7168]{1,0:T(8,128)(2,1)S(1)}, u32[]{:S(2)}, u32[]{:S(2)}) collective-permute-start(bf16[8,7168]{1,0:T(8,128)(2,1)S(1)} %get-tuple-element.15), channel_id=1, source_target_pairs={{0,2},{1,3},{2,0},{3,1},{4,6},{5,7},{6,4},{7,5},{8,9},{9,8},{10,11... | collective-permute-start | bytes 344072 | tf_op jit(solution)/shard_map/ppermute | solution.py:58
  32.4 1.4 %collective-permute-start.14 = (bf16[8,7168]{1,0:T(8,128)(2,1)S(1)}, bf16[8,7168]{1,0:T(8,128)(2,1)S(1)}, u32[]{:S(2)}, u32[]{:S(2)}) collective-permute-start(bf16[8,7168]{1,0:T(8,128)(2,1)S(1)} %get-tuple-element.16), channel_id=1, source_target_pairs={{0,3},{1,2},{2,1},{3,0},{4,7},{5,6},{6,5},{7,4},{8,11},{9,10},{10,... | collective-permute-start | bytes 344072 | tf_op jit(solution)/shard_map/ppermute | solution.py:58
  34.1 1.9 %collective-permute-start.9 = (bf16[16,7168]{1,0:T(8,128)(2,1)S(1)}, bf16[16,7168]{1,0:T(8,128)(2,1)S(1)}, u32[]{:S(2)}, u32[]{:S(2)}) collective-permute-start(bf16[16,7168]{1,0:T(8,128)(2,1)S(1)} %slice.60), channel_id=1, source_target_pairs={{0,1},{1,0},{2,3},{3,2},{4,5},{5,4},{6,7},{7,6},{8,10},{9,11},{10,... | collective-permute-start | bytes 688136 | tf_op jit(solution)/shard_map/ppermute | solution.py:58
  36.0 3.9 %collective-permute-done.14 = bf16[8,7168]{1,0:T(8,128)(2,1)S(1)} collective-permute-done((bf16[8,7168]{1,0:T(8,128)(2,1)S(1)}, bf16[8,7168]{1,0:T(8,128)(2,1)S(1)}, u32[]{:S(2)}, u32[]{:S(2)}) %collective-permute-start.14) | collective-permute-done | bytes 114720 | tf_op jit(solution)/shard_map/ppermute | solution.py:58
  40.2 2.7 %collective-permute-start.15 = (bf16[8,7168]{1,0:T(8,128)(2,1)S(1)}, bf16[8,7168]{1,0:T(8,128)(2,1)S(1)}, u32[]{:S(2)}, u32[]{:S(2)}) collective-permute-start(bf16[8,7168]{1,0:T(8,128)(2,1)S(1)} %fusion.2), channel_id=1, source_target_pairs={{0,4},{1,5},{2,6},{3,7},{4,0},{5,1},{6,2},{7,3},{8,12},{9,13},{10,... | collective-permute-start | bytes 344072 | tf_op jit(solution)/shard_map/ppermute | solution.py:58
  43.0 1.6 %collective-permute-start.10 = (bf16[8,7168]{1,0:T(8,128)(2,1)S(1)}, bf16[8,7168]{1,0:T(8,128)(2,1)S(1)}, u32[]{:S(2)}, u32[]{:S(2)}) collective-permute-start(bf16[8,7168]{1,0:T(8,128)(2,1)S(1)} %slice.61), channel_id=1, source_target_pairs={{0,2},{1,3},{2,0},{3,1},{4,6},{5,7},{6,4},{7,5},{8,9},{9,8},{10,11... | collective-permute-start | bytes 344072 | tf_op jit(solution)/shard_map/ppermute | solution.py:58
  44.6 3.9 %collective-permute-done.15 = bf16[8,7168]{1,0:T(8,128)(2,1)S(1)} collective-permute-done((bf16[8,7168]{1,0:T(8,128)(2,1)S(1)}, bf16[8,7168]{1,0:T(8,128)(2,1)S(1)}, u32[]{:S(2)}, u32[]{:S(2)}) %collective-permute-start.15) | collective-permute-done | bytes 114720 | tf_op jit(solution)/shard_map/ppermute | solution.py:58
  48.9 0.7 %fusion.4 = bf16[8,7168]{1,0:T(8,128)(2,1)} fusion(f32[16,7168]{1,0:T(8,128)S(1)} %slice_add_fusion, bf16[8,7168]{1,0:T(8,128)(2,1)S(1)} %collective-permute-done.15, bf16[8,7168]{1,0:T(8,128)(2,1)S(1)} %collective-permute-done.10), kind=kLoop, calls=%fused_computation.11 | loop fusion | flops 286720 | bytes 573440 | tf_op jit(solution)/shard_map/convert_element_type | solution.py:227
  (49 shorter events, 2.3 us)
Async XLA Ops:
  1.0 5.9 %collective-permute-start = (bf16[8,7296]{1,0:T(8,128)(2,1)S(1)}, bf16[8,7296]{1,0:T(8,128)(2,1)S(1)}, u32[]{:S(2)}, u32[]{:S(2)}) collective-permute-start(bf16[8,7296]{1,0:T(8,128)(2,1)S(1)} %shard_map.64.refs_1_), channel_id=1, source_target_pairs={{0,2},{1,3},{2,0},{3,1},{4,6},{5,7},{6,4},{7,5},{8,9},{9,8},{10,11... | collective-permute-start | bytes 350216 | tf_op jit(solution)/shard_map/ppermute | solution.py:58
  4.1 7.5 %collective-permute-start.2 = (bf16[8,7296]{1,0:T(8,128)(2,1)S(1)}, bf16[8,7296]{1,0:T(8,128)(2,1)S(1)}, u32[]{:S(2)}, u32[]{:S(2)}) collective-permute-start(bf16[8,7296]{1,0:T(8,128)(2,1)S(1)} %shard_map.64.refs_1_), channel_id=1, source_target_pairs={{0,4},{1,5},{2,6},{3,7},{4,0},{5,1},{6,2},{7,3},{8,12},{9,13},{10,... | collective-permute-start | bytes 350216 | tf_op jit(solution)/shard_map/ppermute | solution.py:58
  6.9 15.1 %slice-start.8 = ((s8[14680064]{0:T(1024)(128)(4,1)}), s8[4194304]{0:T(1024)(128)(4,1)S(1)}, s32[]{:S(2)}) async-start(s8[14680064]{0:T(1024)(128)(4,1)} %bitcast.5), calls=%async_computation.8 | async-start | bytes 8388608
  6.9 15.1 %slice-start.9 = ((s8[14680064]{0:T(1024)(128)(4,1)}), s8[4194304]{0:T(1024)(128)(4,1)S(1)}, s32[]{:S(2)}) async-start(s8[14680064]{0:T(1024)(128)(4,1)} %bitcast.5), calls=%async_computation.9 | async-start | bytes 8388608
  6.9 15.1 %slice-start.4 = ((s8[14680064]{0:T(1024)(128)(4,1)}), s8[4194304]{0:T(1024)(128)(4,1)S(1)}, s32[]{:S(2)}) async-start(s8[14680064]{0:T(1024)(128)(4,1)} %bitcast.3), calls=%async_computation.4 | async-start | bytes 8388608
  7.0 15.1 %slice-start.5 = ((s8[14680064]{0:T(1024)(128)(4,1)}), s8[4194304]{0:T(1024)(128)(4,1)S(1)}, s32[]{:S(2)}) async-start(s8[14680064]{0:T(1024)(128)(4,1)} %bitcast.3), calls=%async_computation.5 | async-start | bytes 8388608
  7.0 15.1 %slice-start.6 = ((s8[14680064]{0:T(1024)(128)(4,1)}), s8[4194304]{0:T(1024)(128)(4,1)S(1)}, s32[]{:S(2)}) async-start(s8[14680064]{0:T(1024)(128)(4,1)} %bitcast.3), calls=%async_computation.6 | async-start | bytes 8388608
  7.0 15.1 %slice-start.10 = ((s8[14680064]{0:T(1024)(128)(4,1)}), s8[4194304]{0:T(1024)(128)(4,1)S(1)}, s32[]{:S(2)}) async-start(s8[14680064]{0:T(1024)(128)(4,1)} %bitcast.5), calls=%async_computation.10 | async-start | bytes 8388608
  7.0 12.6 %collective-permute-start.1 = (bf16[16,7296]{1,0:T(8,128)(2,1)S(1)}, bf16[16,7296]{1,0:T(8,128)(2,1)S(1)}, u32[]{:S(2)}, u32[]{:S(2)}) collective-permute-start(bf16[16,7296]{1,0:T(8,128)(2,1)S(1)} %shard_map.65.refs_1_), channel_id=1, source_target_pairs={{0,1},{1,0},{2,3},{3,2},{4,5},{5,4},{6,7},{7,6},{8,10},{9,11},{10,... | collective-permute-start | bytes 700424 | tf_op jit(solution)/shard_map/ppermute | solution.py:58
  11.6 7.0 %collective-permute-start.5 = (bf16[8,7296]{1,0:T(8,128)(2,1)S(1)}, bf16[8,7296]{1,0:T(8,128)(2,1)S(1)}, u32[]{:S(2)}, u32[]{:S(2)}) collective-permute-start(bf16[8,7296]{1,0:T(8,128)(2,1)S(1)} %collective-permute-done.2.refs_1_), channel_id=1, source_target_pairs={{0,3},{1,2},{2,1},{3,0},{4,7},{5,6},{6,5},{7,4},{8,11},{9,10},{10,... | collective-permute-start | bytes 350216 | tf_op jit(solution)/shard_map/ppermute | solution.py:58
  12.8 6.4 %collective-permute-start.4 = (bf16[8,7296]{1,0:T(8,128)(2,1)S(1)}, bf16[8,7296]{1,0:T(8,128)(2,1)S(1)}, u32[]{:S(2)}, u32[]{:S(2)}) collective-permute-start(bf16[8,7296]{1,0:T(8,128)(2,1)S(1)} %collective-permute-done.2.refs_1_), channel_id=1, source_target_pairs={{0,1},{1,0},{2,3},{3,2},{4,5},{5,4},{6,7},{7,6},{8,10},{9,11},{10,... | collective-permute-start | bytes 350216 | tf_op jit(solution)/shard_map/ppermute | solution.py:58
  14.6 4.8 %collective-permute-start.3 = (bf16[8,7296]{1,0:T(8,128)(2,1)S(1)}, bf16[8,7296]{1,0:T(8,128)(2,1)S(1)}, u32[]{:S(2)}, u32[]{:S(2)}) collective-permute-start(bf16[8,7296]{1,0:T(8,128)(2,1)S(1)} %collective-permute-done.2.refs_1_), channel_id=1, source_target_pairs={{0,2},{1,3},{2,0},{3,1},{4,6},{5,7},{6,4},{7,5},{8,9},{9,8},{10,11... | collective-permute-start | bytes 350216 | tf_op jit(solution)/shard_map/ppermute | solution.py:58
  19.5 1.9 %collective-permute-start.7 = (bf16[32,7296]{1,0:T(8,128)(2,1)S(1)}, bf16[32,7296]{1,0:T(8,128)(2,1)S(1)}, u32[]{:S(2)}, u32[]{:S(2)}) collective-permute-start(bf16[32,7296]{1,0:T(8,128)(2,1)S(1)} %shard_map.67.refs_3_.refs_4_), channel_id=1, source_target_pairs={{0,8},{8,0},{1,9},{9,1},{2,10},{10,2},{3,11},{11,3},{4,12},{12,4},... | collective-permute-start | bytes 1400840 | tf_op jit(solution)/shard_map/ppermute | solution.py:66
  19.6 6.7 %slice-start = ((s8[14680064]{0:T(1024)(128)(4,1)}), s8[4194304]{0:T(1024)(128)(4,1)S(1)}, s32[]{:S(2)}) async-start(s8[14680064]{0:T(1024)(128)(4,1)} %bitcast.1), calls=%async_computation | async-start | bytes 8388608
  19.6 6.7 %slice-start.1 = ((s8[14680064]{0:T(1024)(128)(4,1)}), s8[4194304]{0:T(1024)(128)(4,1)S(1)}, s32[]{:S(2)}) async-start(s8[14680064]{0:T(1024)(128)(4,1)} %bitcast.1), calls=%async_computation.1 | async-start | bytes 8388608
  19.7 2.4 %collective-permute-start.6 = (bf16[32,7296]{1,0:T(8,128)(2,1)S(1)}, bf16[32,7296]{1,0:T(8,128)(2,1)S(1)}, u32[]{:S(2)}, u32[]{:S(2)}) collective-permute-start(bf16[32,7296]{1,0:T(8,128)(2,1)S(1)} %shard_map.66.refs_2_.refs_3_), channel_id=1, source_target_pairs={{0,8},{8,0},{1,9},{9,1},{2,10},{10,2},{3,11},{11,3},{4,12},{12,4},... | collective-permute-start | bytes 1400840 | tf_op jit(solution)/shard_map/ppermute | solution.py:66
  28.4 1.9 %collective-permute-start.11 = (bf16[32,7168]{1,0:T(8,128)(2,1)S(1)}, bf16[32,7168]{1,0:T(8,128)(2,1)S(1)}, u32[]{:S(2)}, u32[]{:S(2)}) collective-permute-start(bf16[32,7168]{1,0:T(8,128)(2,1)S(1)} %get-tuple-element.12), channel_id=1, source_target_pairs={{0,8},{8,0},{1,9},{9,1},{2,10},{10,2},{3,11},{11,3},{4,12},{12,4},... | collective-permute-start | bytes 1376264 | tf_op jit(solution)/shard_map/ppermute | solution.py:66
  28.6 5.4 %collective-permute-start.8 = (bf16[32,7168]{1,0:T(8,128)(2,1)S(1)}, bf16[32,7168]{1,0:T(8,128)(2,1)S(1)}, u32[]{:S(2)}, u32[]{:S(2)}) collective-permute-start(bf16[32,7168]{1,0:T(8,128)(2,1)S(1)} %get-tuple-element.10), channel_id=1, source_target_pairs={{0,8},{8,0},{1,9},{9,1},{2,10},{10,2},{3,11},{11,3},{4,12},{12,4},... | collective-permute-start | bytes 1376264 | tf_op jit(solution)/shard_map/ppermute | solution.py:66
  30.4 5.6 %collective-permute-start.12 = (bf16[8,7168]{1,0:T(8,128)(2,1)S(1)}, bf16[8,7168]{1,0:T(8,128)(2,1)S(1)}, u32[]{:S(2)}, u32[]{:S(2)}) collective-permute-start(bf16[8,7168]{1,0:T(8,128)(2,1)S(1)} %get-tuple-element.15), channel_id=1, source_target_pairs={{0,2},{1,3},{2,0},{3,1},{4,6},{5,7},{6,4},{7,5},{8,9},{9,8},{10,11... | collective-permute-start | bytes 344072 | tf_op jit(solution)/shard_map/ppermute | solution.py:58
  32.4 7.6 %collective-permute-start.14 = (bf16[8,7168]{1,0:T(8,128)(2,1)S(1)}, bf16[8,7168]{1,0:T(8,128)(2,1)S(1)}, u32[]{:S(2)}, u32[]{:S(2)}) collective-permute-start(bf16[8,7168]{1,0:T(8,128)(2,1)S(1)} %get-tuple-element.16), channel_id=1, source_target_pairs={{0,3},{1,2},{2,1},{3,0},{4,7},{5,6},{6,5},{7,4},{8,11},{9,10},{10,... | collective-permute-start | bytes 344072 | tf_op jit(solution)/shard_map/ppermute | solution.py:58
  33.8 6.4 %collective-permute-start.13 = (bf16[8,7168]{1,0:T(8,128)(2,1)S(1)}, bf16[8,7168]{1,0:T(8,128)(2,1)S(1)}, u32[]{:S(2)}, u32[]{:S(2)}) collective-permute-start(bf16[8,7168]{1,0:T(8,128)(2,1)S(1)} %get-tuple-element.17), channel_id=1, source_target_pairs={{0,1},{1,0},{2,3},{3,2},{4,5},{5,4},{6,7},{7,6},{8,10},{9,11},{10,... | collective-permute-start | bytes 344072 | tf_op jit(solution)/shard_map/ppermute | solution.py:58
  34.1 8.8 %collective-permute-start.9 = (bf16[16,7168]{1,0:T(8,128)(2,1)S(1)}, bf16[16,7168]{1,0:T(8,128)(2,1)S(1)}, u32[]{:S(2)}, u32[]{:S(2)}) collective-permute-start(bf16[16,7168]{1,0:T(8,128)(2,1)S(1)} %slice.60), channel_id=1, source_target_pairs={{0,1},{1,0},{2,3},{3,2},{4,5},{5,4},{6,7},{7,6},{8,10},{9,11},{10,... | collective-permute-start | bytes 688136 | tf_op jit(solution)/shard_map/ppermute | solution.py:58
  40.2 8.3 %collective-permute-start.15 = (bf16[8,7168]{1,0:T(8,128)(2,1)S(1)}, bf16[8,7168]{1,0:T(8,128)(2,1)S(1)}, u32[]{:S(2)}, u32[]{:S(2)}) collective-permute-start(bf16[8,7168]{1,0:T(8,128)(2,1)S(1)} %fusion.2), channel_id=1, source_target_pairs={{0,4},{1,5},{2,6},{3,7},{4,0},{5,1},{6,2},{7,3},{8,12},{9,13},{10,... | collective-permute-start | bytes 344072 | tf_op jit(solution)/shard_map/ppermute | solution.py:58
  43.0 5.9 %collective-permute-start.10 = (bf16[8,7168]{1,0:T(8,128)(2,1)S(1)}, bf16[8,7168]{1,0:T(8,128)(2,1)S(1)}, u32[]{:S(2)}, u32[]{:S(2)}) collective-permute-start(bf16[8,7168]{1,0:T(8,128)(2,1)S(1)} %slice.61), channel_id=1, source_target_pairs={{0,2},{1,3},{2,0},{3,1},{4,6},{5,7},{6,4},{7,5},{8,9},{9,8},{10,11... | collective-permute-start | bytes 344072 | tf_op jit(solution)/shard_map/ppermute | solution.py:58
  (4 other events, 18.5 us)

commit v6 on v5

--- a/solution.py
+++ b/solution.py
@@ -22,9 +22,9 @@
     return pltpu.with_memory_space_constraint(array, pltpu.HBM)
 
 
-def call(kernel, outs, *args, limit, flops, nbytes, scalars=(), far=()):
+def call(kernel, outs, *args, limit, flops, nbytes, scalars=(), far=(), after=()):
     def body(*refs):
-        kernel(*refs[: len(scalars)], *refs[len(scalars) + len(far) :])
+        kernel(*refs[: len(scalars)], *refs[len(scalars) + len(far) + len(after) :])
 
 
     return pl.pallas_call(
@@ -32,13 +32,14 @@
         out_shape=outs,
         in_specs=[pl.BlockSpec(memory_space=pltpu.SMEM)] * len(scalars)
         + [pl.BlockSpec(memory_space=pltpu.HBM)] * len(far)
+        + [pl.BlockSpec(memory_space=pl.ANY)] * len(after)
         + [pl.BlockSpec(memory_space=VM)] * len(args),
         out_specs=[pl.BlockSpec(memory_space=VM)] * len(outs),
         compiler_params=pltpu.CompilerParams(vmem_limit_bytes=limit * 2**20),
         cost_estimate=pl.CostEstimate(
             flops=flops, bytes_accessed=nbytes, transcendentals=0
         ),
-    )(*scalars, *[in_hbm(x) for x in far], *args)
+    )(*scalars, *[in_hbm(x) for x in far], *after, *args)
 
 
 def level_bits(node_count, bits):
@@ -113,13 +114,14 @@
     refs[-1][...] = stacked(refs[:-1])
 
 
-def join(parts, far):
+def join(parts, far, after=()):
     rows = sum(p.shape[0] for p in parts)
     return call(
         join_kernel,
         [VM((rows, parts[0].shape[1]), BF16)],
         *parts,
         far=far,
+        after=after,
         limit=1,
         flops=0,
         nbytes=200_000,
@@ -175,12 +177,13 @@
         sum(1 << k for k in range(bits - 1) if i >> (bits - 2 - k) & 1)
         for i in range(side)
     ]
-    near = prepare(expert, tokens, expert_ids, route_weights, w_down)
-    far = [swap(near, dims[-1], local_count)]
+    block = prepare(expert, tokens, expert_ids, route_weights, w_down)
+    far = [swap(block, dims[-1], local_count)]
+    near = [block] + [swap_across(block, dims, m, local_count) for m in masks[1:]]
     far += [swap_across(far[0], dims, m, local_count) for m in masks[1:]]
-    for dim in dims[-2::-1]:
-        near = join([near, swap(near, dim, local_count)], (w_down,))
-    mine = [near, join(far, (w_down,))]
+    near = join(near, (w_down,), ())
+    far = join(far, (w_down,))
+    mine = [near, far]
     parts = mine + [swap_core(m, node_count) for m in mine]
 
     w_gate, w_up, w_down = in_vmem(w_gate), in_vmem(w_up), in_vmem(w_down)

time: 49.8 us -> 48.8 us (0.980)
  starting transfers between devices: 23.3 us -> 20.8 us
  waiting for transfers between devices: 17.6 us -> 19.1 us
    ppermute x12 -> x13, starting transfers between devices: 22.2 us -> 20.1 us  [swap_across(): return lax.ppermute(array, ('node', 'local'), perm)]
    ppermute x12 -> x13, waiting for transfers between devices: 14.4 us -> 16 us  [swap_across(): return lax.ppermute(array, ('node', 'local'), perm)]
    pallas_call x5 -> x4, Pallas kernels: 6.29 us -> 6.22 us  [call(): pl.pallas_call(body, out_shape=outs, in_specs=[pl.BlockSpec(memory_space=...]
  transfers between devices with their start and end apart: 16 -> 17, of which waited for: 12 -> 13; matrix products, arithmetic and copies ran while one was open for 1% -> 1% of each run, Pallas kernels for 0% -> 0%
where the time goes in v6:
time: 48.8 us; the launch traced here: 48.7 us
  starting transfers between devices  20.8 us (43%)
  waiting for transfers between devices  19.1 us (39%)
  Pallas kernels  7.39 us (15%)
  other arithmetic  0.97 us (2%)
    ppermute x13, starting transfers between devices, swap_across(): return lax.ppermute(array, ('node', 'local'), perm)  20.1 us
    ppermute x13, waiting for transfers between devices, swap_across(): return lax.ppermute(array, ('node', 'local'), perm)  16 us
    pallas_call x4, Pallas kernels, call(): pl.pallas_call(body, out_shape=outs, in_specs=[pl.BlockSpec(memory_space=...  6.22 us
    ppermute x4, waiting for transfers between devices, swap_core(): return lax.ppermute(array, 'node', [(n, n ^ 1) for n in range(node_count)])  3.12 us
    pallas_call x1, Pallas kernels, prepare(): pl.pallas_call(prepare_kernel, out_shape=VM((tokens.shape[0], tokens.shap...  1.17 us
  transfers between devices with their start and end apart: 17, of which 13 were waited for; matrix products, arithmetic and copies ran while one was open for 1% of the time, Pallas kernels for 0%

profile of v6, /device:TPU:0, one launch (start us, length us, event | category | flops | bytes accessed | tf_op | source)
XLA Modules:
  0.0 48.7 jit_solution(11258613355740194584)
XLA Ops:
  0.0 1.2 %shard_map.64.refs_1_ = bf16[8,7296]{1,0:T(8,128)(2,1)S(1)} custom-call(s32[1]{0:T(128)} %bitcast._.refs_0_, bf16[8,7168]{1,0:T(8,128)(2,1)} %tokens_far.1, s32[8,8]{1,0:T(8,128)} %ids_far.1, bf16[8,8]{1,0:T(8,128)(2,1)} %weights_far.1, bf16[1,1024,7168]{2,1,0:T(8,128)(2,1)} %refs_1_.3), custom_call_target="tpu_custom_call" | custom-call | bytes 200000 | tf_op jit(solution)/shard_map/pallas_call | solution.py:91
  1.2 4.1 %collective-permute-start.3 = (bf16[8,7296]{1,0:T(8,128)(2,1)S(1)}, bf16[8,7296]{1,0:T(8,128)(2,1)S(1)}, u32[]{:S(2)}, u32[]{:S(2)}) collective-permute-start(bf16[8,7296]{1,0:T(8,128)(2,1)S(1)} %shard_map.64.refs_1_), channel_id=1, source_target_pairs={{0,4},{1,5},{2,6},{3,7},{4,0},{5,1},{6,2},{7,3},{8,12},{9,13},{10,... | collective-permute-start | bytes 350216 | tf_op jit(solution)/shard_map/ppermute | solution.py:59
  5.3 2.5 %collective-permute-start.2 = (bf16[8,7296]{1,0:T(8,128)(2,1)S(1)}, bf16[8,7296]{1,0:T(8,128)(2,1)S(1)}, u32[]{:S(2)}, u32[]{:S(2)}) collective-permute-start(bf16[8,7296]{1,0:T(8,128)(2,1)S(1)} %shard_map.64.refs_1_), channel_id=1, source_target_pairs={{0,3},{1,2},{2,1},{3,0},{4,7},{5,6},{6,5},{7,4},{8,11},{9,10},{10,... | collective-permute-start | bytes 350216 | tf_op jit(solution)/shard_map/ppermute | solution.py:59
  8.8 2.3 %collective-permute-done.3.refs_1_ = bf16[8,7296]{1,0:T(8,128)(2,1)S(1)} collective-permute-done((bf16[8,7296]{1,0:T(8,128)(2,1)S(1)}, bf16[8,7296]{1,0:T(8,128)(2,1)S(1)}, u32[]{:S(2)}, u32[]{:S(2)}) %collective-permute-start.3) | collective-permute-done | bytes 116768 | tf_op jit(solution)/shard_map/ppermute | solution.py:59
  11.1 1.6 %collective-permute-start.6 = (bf16[8,7296]{1,0:T(8,128)(2,1)S(1)}, bf16[8,7296]{1,0:T(8,128)(2,1)S(1)}, u32[]{:S(2)}, u32[]{:S(2)}) collective-permute-start(bf16[8,7296]{1,0:T(8,128)(2,1)S(1)} %collective-permute-done.3.refs_1_), channel_id=1, source_target_pairs={{0,3},{1,2},{2,1},{3,0},{4,7},{5,6},{6,5},{7,4},{8,11},{9,10},{10,... | collective-permute-start | bytes 350216 | tf_op jit(solution)/shard_map/ppermute | solution.py:59
  13.6 1.2 %collective-permute-start.4 = (bf16[8,7296]{1,0:T(8,128)(2,1)S(1)}, bf16[8,7296]{1,0:T(8,128)(2,1)S(1)}, u32[]{:S(2)}, u32[]{:S(2)}) collective-permute-start(bf16[8,7296]{1,0:T(8,128)(2,1)S(1)} %collective-permute-done.3.refs_1_), channel_id=1, source_target_pairs={{0,2},{1,3},{2,0},{3,1},{4,6},{5,7},{6,4},{7,5},{8,9},{9,8},{10,11... | collective-permute-start | bytes 350216 | tf_op jit(solution)/shard_map/ppermute | solution.py:59
  14.9 0.8 %collective-permute-done.refs_2_ = bf16[8,7296]{1,0:T(8,128)(2,1)S(1)} collective-permute-done((bf16[8,7296]{1,0:T(8,128)(2,1)S(1)}, bf16[8,7296]{1,0:T(8,128)(2,1)S(1)}, u32[]{:S(2)}, u32[]{:S(2)}) %collective-permute-start) | collective-permute-done | bytes 116768 | tf_op jit(solution)/shard_map/ppermute | solution.py:59
  15.8 2.6 %collective-permute-done.6.refs_4_ = bf16[8,7296]{1,0:T(8,128)(2,1)S(1)} collective-permute-done((bf16[8,7296]{1,0:T(8,128)(2,1)S(1)}, bf16[8,7296]{1,0:T(8,128)(2,1)S(1)}, u32[]{:S(2)}, u32[]{:S(2)}) %collective-permute-start.6) | collective-permute-done | bytes 116768 | tf_op jit(solution)/shard_map/ppermute | solution.py:59
  18.4 1.0 %collective-permute-done.5.refs_3_ = bf16[8,7296]{1,0:T(8,128)(2,1)S(1)} collective-permute-done((bf16[8,7296]{1,0:T(8,128)(2,1)S(1)}, bf16[8,7296]{1,0:T(8,128)(2,1)S(1)}, u32[]{:S(2)}, u32[]{:S(2)}) %collective-permute-start.5) | collective-permute-done | bytes 116768 | tf_op jit(solution)/shard_map/ppermute | solution.py:59
  19.9 1.8 %collective-permute-done.8.refs_5_.refs_6_ = bf16[32,7296]{1,0:T(8,128)(2,1)S(1)} collective-permute-done((bf16[32,7296]{1,0:T(8,128)(2,1)S(1)}, bf16[32,7296]{1,0:T(8,128)(2,1)S(1)}, u32[]{:S(2)}, u32[]{:S(2)}) %collective-permute-start.8) | collective-permute-done | bytes 466976 | tf_op jit(solution)/shard_map/ppermute | solution.py:67
  21.8 4.0 %shard_map.67.refs_2_ = bf16[128,1024]{1,0:T(8,128)(2,1)S(1)} custom-call(bf16[1,7168,1024]{2,1,0:T(8,128)(2,1)S(1)} %bitcast.4, bf16[1,7168,1024]{2,1,0:T(8,128)(2,1)S(1)} %bitcast.6, bf16[32,7296]{1,0:T(8,128)(2,1)S(1)} %shard_map.65.refs_2_.refs_3_, bf16[32,7296]{1,0:T(8,128)(2,1)S(1)} %shard_map.66.refs_3_.refs_4_, ...), custom_call_target="tpu_custom_call" | custom-call | flops 3758096384 | bytes 29360128 | tf_op jit(solution)/shard_map/pallas_call | solution.py:30
  25.9 2.1 %shard_map.68 = (f32[32,7168]{1,0:T(8,128)S(1)}, f32[32,7168]{1,0:T(8,128)S(1)}, bf16[32,7168]{1,0:T(8,128)(2,1)S(1)}, bf16[32,7168]{1,0:T(8,128)(2,1)S(1)}) custom-call(s32[1]{0:T(128)} %bitcast._.refs_0_, bf16[1,1024,7168]{2,1,0:T(8,128)(2,1)S(1)} %bitcast.2, bf16[128,1024]{1,0:T(8,128)(2,1)S(1)} %shard_map.67.refs_2_, ...), custom_call_target="tpu_custom_call" | custom-call | flops 1879048192 | bytes 14680064 | tf_op jit(solution)/shard_map/pallas_call | solution.py:30
  28.6 1.3 %collective-permute-done.12 = bf16[32,7168]{1,0:T(8,128)(2,1)S(1)} collective-permute-done((bf16[32,7168]{1,0:T(8,128)(2,1)S(1)}, bf16[32,7168]{1,0:T(8,128)(2,1)S(1)}, u32[]{:S(2)}, u32[]{:S(2)}) %collective-permute-start.12) | collective-permute-done | bytes 458784 | tf_op jit(solution)/shard_map/ppermute | solution.py:67
  30.0 1.4 %collective-permute-start.13 = (bf16[8,7168]{1,0:T(8,128)(2,1)S(1)}, bf16[8,7168]{1,0:T(8,128)(2,1)S(1)}, u32[]{:S(2)}, u32[]{:S(2)}) collective-permute-start(bf16[8,7168]{1,0:T(8,128)(2,1)S(1)} %get-tuple-element.15), channel_id=1, source_target_pairs={{0,2},{1,3},{2,0},{3,1},{4,6},{5,7},{6,4},{7,5},{8,9},{9,8},{10,11... | collective-permute-start | bytes 344072 | tf_op jit(solution)/shard_map/ppermute | solution.py:59
  31.4 0.9 %collective-permute-start.15 = (bf16[8,7168]{1,0:T(8,128)(2,1)S(1)}, bf16[8,7168]{1,0:T(8,128)(2,1)S(1)}, u32[]{:S(2)}, u32[]{:S(2)}) collective-permute-start(bf16[8,7168]{1,0:T(8,128)(2,1)S(1)} %get-tuple-element.16), channel_id=1, source_target_pairs={{0,3},{1,2},{2,1},{3,0},{4,7},{5,6},{6,5},{7,4},{8,11},{9,10},{10,... | collective-permute-start | bytes 344072 | tf_op jit(solution)/shard_map/ppermute | solution.py:59
  32.3 1.3 %collective-permute-start.14 = (bf16[8,7168]{1,0:T(8,128)(2,1)S(1)}, bf16[8,7168]{1,0:T(8,128)(2,1)S(1)}, u32[]{:S(2)}, u32[]{:S(2)}) collective-permute-start(bf16[8,7168]{1,0:T(8,128)(2,1)S(1)} %get-tuple-element.17), channel_id=1, source_target_pairs={{0,1},{1,0},{2,3},{3,2},{4,5},{5,4},{6,7},{7,6},{8,10},{9,11},{10,... | collective-permute-start | bytes 344072 | tf_op jit(solution)/shard_map/ppermute | solution.py:59
  33.7 0.8 %collective-permute-start.10 = (bf16[16,7168]{1,0:T(8,128)(2,1)S(1)}, bf16[16,7168]{1,0:T(8,128)(2,1)S(1)}, u32[]{:S(2)}, u32[]{:S(2)}) collective-permute-start(bf16[16,7168]{1,0:T(8,128)(2,1)S(1)} %slice.60), channel_id=1, source_target_pairs={{0,1},{1,0},{2,3},{3,2},{4,5},{5,4},{6,7},{7,6},{8,10},{9,11},{10,... | collective-permute-start | bytes 688136 | tf_op jit(solution)/shard_map/ppermute | solution.py:59
  34.5 1.3 %collective-permute-done.13 = bf16[8,7168]{1,0:T(8,128)(2,1)S(1)} collective-permute-done((bf16[8,7168]{1,0:T(8,128)(2,1)S(1)}, bf16[8,7168]{1,0:T(8,128)(2,1)S(1)}, u32[]{:S(2)}, u32[]{:S(2)}) %collective-permute-start.13) | collective-permute-done | bytes 114720 | tf_op jit(solution)/shard_map/ppermute | solution.py:59
  35.9 2.6 %collective-permute-done.15 = bf16[8,7168]{1,0:T(8,128)(2,1)S(1)} collective-permute-done((bf16[8,7168]{1,0:T(8,128)(2,1)S(1)}, bf16[8,7168]{1,0:T(8,128)(2,1)S(1)}, u32[]{:S(2)}, u32[]{:S(2)}) %collective-permute-start.15) | collective-permute-done | bytes 114720 | tf_op jit(solution)/shard_map/ppermute | solution.py:59
  38.7 2.7 %collective-permute-start.16 = (bf16[8,7168]{1,0:T(8,128)(2,1)S(1)}, bf16[8,7168]{1,0:T(8,128)(2,1)S(1)}, u32[]{:S(2)}, u32[]{:S(2)}) collective-permute-start(bf16[8,7168]{1,0:T(8,128)(2,1)S(1)} %fusion.2), channel_id=1, source_target_pairs={{0,4},{1,5},{2,6},{3,7},{4,0},{5,1},{6,2},{7,3},{8,12},{9,13},{10,... | collective-permute-start | bytes 344072 | tf_op jit(solution)/shard_map/ppermute | solution.py:59
  41.5 2.1 %collective-permute-start.11 = (bf16[8,7168]{1,0:T(8,128)(2,1)S(1)}, bf16[8,7168]{1,0:T(8,128)(2,1)S(1)}, u32[]{:S(2)}, u32[]{:S(2)}) collective-permute-start(bf16[8,7168]{1,0:T(8,128)(2,1)S(1)} %slice.61), channel_id=1, source_target_pairs={{0,2},{1,3},{2,0},{3,1},{4,6},{5,7},{6,4},{7,5},{8,9},{9,8},{10,11... | collective-permute-start | bytes 344072 | tf_op jit(solution)/shard_map/ppermute | solution.py:59
  43.6 3.7 %collective-permute-done.16 = bf16[8,7168]{1,0:T(8,128)(2,1)S(1)} collective-permute-done((bf16[8,7168]{1,0:T(8,128)(2,1)S(1)}, bf16[8,7168]{1,0:T(8,128)(2,1)S(1)}, u32[]{:S(2)}, u32[]{:S(2)}) %collective-permute-start.16) | collective-permute-done | bytes 114720 | tf_op jit(solution)/shard_map/ppermute | solution.py:59
  47.3 0.6 %collective-permute-done.11 = bf16[8,7168]{1,0:T(8,128)(2,1)S(1)} collective-permute-done((bf16[8,7168]{1,0:T(8,128)(2,1)S(1)}, bf16[8,7168]{1,0:T(8,128)(2,1)S(1)}, u32[]{:S(2)}, u32[]{:S(2)}) %collective-permute-start.11) | collective-permute-done | bytes 114720 | tf_op jit(solution)/shard_map/ppermute | solution.py:59
  48.0 0.7 %fusion.4 = bf16[8,7168]{1,0:T(8,128)(2,1)} fusion(f32[16,7168]{1,0:T(8,128)S(1)} %slice_add_fusion, bf16[8,7168]{1,0:T(8,128)(2,1)S(1)} %collective-permute-done.16, bf16[8,7168]{1,0:T(8,128)(2,1)S(1)} %collective-permute-done.11), kind=kLoop, calls=%fused_computation.11 | loop fusion | flops 286720 | bytes 573440 | tf_op jit(solution)/shard_map/convert_element_type | solution.py:230
  (50 shorter events, 3.6 us)
Async XLA Ops:
  0.0 21.7 %slice-start.8 = ((s8[14680064]{0:T(1024)(128)(4,1)}), s8[4194304]{0:T(1024)(128)(4,1)S(1)}, s32[]{:S(2)}) async-start(s8[14680064]{0:T(1024)(128)(4,1)} %bitcast.5), calls=%async_computation.8 | async-start | bytes 8388608
  0.0 21.7 %slice-start.9 = ((s8[14680064]{0:T(1024)(128)(4,1)}), s8[4194304]{0:T(1024)(128)(4,1)S(1)}, s32[]{:S(2)}) async-start(s8[14680064]{0:T(1024)(128)(4,1)} %bitcast.5), calls=%async_computation.9 | async-start | bytes 8388608
  1.2 20.6 %slice-start.4 = ((s8[14680064]{0:T(1024)(128)(4,1)}), s8[4194304]{0:T(1024)(128)(4,1)S(1)}, s32[]{:S(2)}) async-start(s8[14680064]{0:T(1024)(128)(4,1)} %bitcast.3), calls=%async_computation.4 | async-start | bytes 8388608
  1.2 20.5 %slice-start.5 = ((s8[14680064]{0:T(1024)(128)(4,1)}), s8[4194304]{0:T(1024)(128)(4,1)S(1)}, s32[]{:S(2)}) async-start(s8[14680064]{0:T(1024)(128)(4,1)} %bitcast.3), calls=%async_computation.5 | async-start | bytes 8388608
  1.2 20.5 %slice-start.10 = ((s8[14680064]{0:T(1024)(128)(4,1)}), s8[4194304]{0:T(1024)(128)(4,1)S(1)}, s32[]{:S(2)}) async-start(s8[14680064]{0:T(1024)(128)(4,1)} %bitcast.5), calls=%async_computation.10 | async-start | bytes 8388608
  1.2 9.9 %collective-permute-start.3 = (bf16[8,7296]{1,0:T(8,128)(2,1)S(1)}, bf16[8,7296]{1,0:T(8,128)(2,1)S(1)}, u32[]{:S(2)}, u32[]{:S(2)}) collective-permute-start(bf16[8,7296]{1,0:T(8,128)(2,1)S(1)} %shard_map.64.refs_1_), channel_id=1, source_target_pairs={{0,4},{1,5},{2,6},{3,7},{4,0},{5,1},{6,2},{7,3},{8,12},{9,13},{10,... | collective-permute-start | bytes 350216 | tf_op jit(solution)/shard_map/ppermute | solution.py:59
  5.3 8.3 %collective-permute-start.2 = (bf16[8,7296]{1,0:T(8,128)(2,1)S(1)}, bf16[8,7296]{1,0:T(8,128)(2,1)S(1)}, u32[]{:S(2)}, u32[]{:S(2)}) collective-permute-start(bf16[8,7296]{1,0:T(8,128)(2,1)S(1)} %shard_map.64.refs_1_), channel_id=1, source_target_pairs={{0,3},{1,2},{2,1},{3,0},{4,7},{5,6},{6,5},{7,4},{8,11},{9,10},{10,... | collective-permute-start | bytes 350216 | tf_op jit(solution)/shard_map/ppermute | solution.py:59
  7.9 7.0 %collective-permute-start.1 = (bf16[8,7296]{1,0:T(8,128)(2,1)S(1)}, bf16[8,7296]{1,0:T(8,128)(2,1)S(1)}, u32[]{:S(2)}, u32[]{:S(2)}) collective-permute-start(bf16[8,7296]{1,0:T(8,128)(2,1)S(1)} %shard_map.64.refs_1_), channel_id=1, source_target_pairs={{0,1},{1,0},{2,3},{3,2},{4,5},{5,4},{6,7},{7,6},{8,10},{9,11},{10,... | collective-permute-start | bytes 350216 | tf_op jit(solution)/shard_map/ppermute | solution.py:59
  8.4 7.3 %collective-permute-start = (bf16[8,7296]{1,0:T(8,128)(2,1)S(1)}, bf16[8,7296]{1,0:T(8,128)(2,1)S(1)}, u32[]{:S(2)}, u32[]{:S(2)}) collective-permute-start(bf16[8,7296]{1,0:T(8,128)(2,1)S(1)} %shard_map.64.refs_1_), channel_id=1, source_target_pairs={{0,2},{1,3},{2,0},{3,1},{4,6},{5,7},{6,4},{7,5},{8,9},{9,8},{10,11... | collective-permute-start | bytes 350216 | tf_op jit(solution)/shard_map/ppermute | solution.py:59
  11.1 7.2 %collective-permute-start.6 = (bf16[8,7296]{1,0:T(8,128)(2,1)S(1)}, bf16[8,7296]{1,0:T(8,128)(2,1)S(1)}, u32[]{:S(2)}, u32[]{:S(2)}) collective-permute-start(bf16[8,7296]{1,0:T(8,128)(2,1)S(1)} %collective-permute-done.3.refs_1_), channel_id=1, source_target_pairs={{0,3},{1,2},{2,1},{3,0},{4,7},{5,6},{6,5},{7,4},{8,11},{9,10},{10,... | collective-permute-start | bytes 350216 | tf_op jit(solution)/shard_map/ppermute | solution.py:59
  12.7 6.6 %collective-permute-start.5 = (bf16[8,7296]{1,0:T(8,128)(2,1)S(1)}, bf16[8,7296]{1,0:T(8,128)(2,1)S(1)}, u32[]{:S(2)}, u32[]{:S(2)}) collective-permute-start(bf16[8,7296]{1,0:T(8,128)(2,1)S(1)} %collective-permute-done.3.refs_1_), channel_id=1, source_target_pairs={{0,1},{1,0},{2,3},{3,2},{4,5},{5,4},{6,7},{7,6},{8,10},{9,11},{10,... | collective-permute-start | bytes 350216 | tf_op jit(solution)/shard_map/ppermute | solution.py:59
  13.6 6.2 %collective-permute-start.4 = (bf16[8,7296]{1,0:T(8,128)(2,1)S(1)}, bf16[8,7296]{1,0:T(8,128)(2,1)S(1)}, u32[]{:S(2)}, u32[]{:S(2)}) collective-permute-start(bf16[8,7296]{1,0:T(8,128)(2,1)S(1)} %collective-permute-done.3.refs_1_), channel_id=1, source_target_pairs={{0,2},{1,3},{2,0},{3,1},{4,6},{5,7},{6,4},{7,5},{8,9},{9,8},{10,11... | collective-permute-start | bytes 350216 | tf_op jit(solution)/shard_map/ppermute | solution.py:59
  15.7 6.1 %slice-start.6 = ((s8[14680064]{0:T(1024)(128)(4,1)}), s8[4194304]{0:T(1024)(128)(4,1)S(1)}, s32[]{:S(2)}) async-start(s8[14680064]{0:T(1024)(128)(4,1)} %bitcast.3), calls=%async_computation.6 | async-start | bytes 8388608
  15.7 4.2 %collective-permute-start.7 = (bf16[32,7296]{1,0:T(8,128)(2,1)S(1)}, bf16[32,7296]{1,0:T(8,128)(2,1)S(1)}, u32[]{:S(2)}, u32[]{:S(2)}) collective-permute-start(bf16[32,7296]{1,0:T(8,128)(2,1)S(1)} %shard_map.65.refs_2_.refs_3_), channel_id=1, source_target_pairs={{0,8},{8,0},{1,9},{9,1},{2,10},{10,2},{3,11},{11,3},{4,12},{12,4},... | collective-permute-start | bytes 1400840 | tf_op jit(solution)/shard_map/ppermute | solution.py:67
  19.8 6.1 %slice-start.1 = ((s8[14680064]{0:T(1024)(128)(4,1)}), s8[4194304]{0:T(1024)(128)(4,1)S(1)}, s32[]{:S(2)}) async-start(s8[14680064]{0:T(1024)(128)(4,1)} %bitcast.1), calls=%async_computation.1 | async-start | bytes 8388608
  19.8 1.9 %collective-permute-start.8 = (bf16[32,7296]{1,0:T(8,128)(2,1)S(1)}, bf16[32,7296]{1,0:T(8,128)(2,1)S(1)}, u32[]{:S(2)}, u32[]{:S(2)}) collective-permute-start(bf16[32,7296]{1,0:T(8,128)(2,1)S(1)} %shard_map.66.refs_3_.refs_4_), channel_id=1, source_target_pairs={{0,8},{8,0},{1,9},{9,1},{2,10},{10,2},{3,11},{11,3},{4,12},{12,4},... | collective-permute-start | bytes 1400840 | tf_op jit(solution)/shard_map/ppermute | solution.py:67
  28.0 1.9 %collective-permute-start.12 = (bf16[32,7168]{1,0:T(8,128)(2,1)S(1)}, bf16[32,7168]{1,0:T(8,128)(2,1)S(1)}, u32[]{:S(2)}, u32[]{:S(2)}) collective-permute-start(bf16[32,7168]{1,0:T(8,128)(2,1)S(1)} %get-tuple-element.12), channel_id=1, source_target_pairs={{0,8},{8,0},{1,9},{9,1},{2,10},{10,2},{3,11},{11,3},{4,12},{12,4},... | collective-permute-start | bytes 1376264 | tf_op jit(solution)/shard_map/ppermute | solution.py:67
  28.2 5.4 %collective-permute-start.9 = (bf16[32,7168]{1,0:T(8,128)(2,1)S(1)}, bf16[32,7168]{1,0:T(8,128)(2,1)S(1)}, u32[]{:S(2)}, u32[]{:S(2)}) collective-permute-start(bf16[32,7168]{1,0:T(8,128)(2,1)S(1)} %get-tuple-element.10), channel_id=1, source_target_pairs={{0,8},{8,0},{1,9},{9,1},{2,10},{10,2},{3,11},{11,3},{4,12},{12,4},... | collective-permute-start | bytes 1376264 | tf_op jit(solution)/shard_map/ppermute | solution.py:67
  30.0 5.8 %collective-permute-start.13 = (bf16[8,7168]{1,0:T(8,128)(2,1)S(1)}, bf16[8,7168]{1,0:T(8,128)(2,1)S(1)}, u32[]{:S(2)}, u32[]{:S(2)}) collective-permute-start(bf16[8,7168]{1,0:T(8,128)(2,1)S(1)} %get-tuple-element.15), channel_id=1, source_target_pairs={{0,2},{1,3},{2,0},{3,1},{4,6},{5,7},{6,4},{7,5},{8,9},{9,8},{10,11... | collective-permute-start | bytes 344072 | tf_op jit(solution)/shard_map/ppermute | solution.py:59
  31.4 7.1 %collective-permute-start.15 = (bf16[8,7168]{1,0:T(8,128)(2,1)S(1)}, bf16[8,7168]{1,0:T(8,128)(2,1)S(1)}, u32[]{:S(2)}, u32[]{:S(2)}) collective-permute-start(bf16[8,7168]{1,0:T(8,128)(2,1)S(1)} %get-tuple-element.16), channel_id=1, source_target_pairs={{0,3},{1,2},{2,1},{3,0},{4,7},{5,6},{6,5},{7,4},{8,11},{9,10},{10,... | collective-permute-start | bytes 344072 | tf_op jit(solution)/shard_map/ppermute | solution.py:59
  32.3 6.4 %collective-permute-start.14 = (bf16[8,7168]{1,0:T(8,128)(2,1)S(1)}, bf16[8,7168]{1,0:T(8,128)(2,1)S(1)}, u32[]{:S(2)}, u32[]{:S(2)}) collective-permute-start(bf16[8,7168]{1,0:T(8,128)(2,1)S(1)} %get-tuple-element.17), channel_id=1, source_target_pairs={{0,1},{1,0},{2,3},{3,2},{4,5},{5,4},{6,7},{7,6},{8,10},{9,11},{10,... | collective-permute-start | bytes 344072 | tf_op jit(solution)/shard_map/ppermute | solution.py:59
  33.7 7.7 %collective-permute-start.10 = (bf16[16,7168]{1,0:T(8,128)(2,1)S(1)}, bf16[16,7168]{1,0:T(8,128)(2,1)S(1)}, u32[]{:S(2)}, u32[]{:S(2)}) collective-permute-start(bf16[16,7168]{1,0:T(8,128)(2,1)S(1)} %slice.60), channel_id=1, source_target_pairs={{0,1},{1,0},{2,3},{3,2},{4,5},{5,4},{6,7},{7,6},{8,10},{9,11},{10,... | collective-permute-start | bytes 688136 | tf_op jit(solution)/shard_map/ppermute | solution.py:59
  38.7 8.6 %collective-permute-start.16 = (bf16[8,7168]{1,0:T(8,128)(2,1)S(1)}, bf16[8,7168]{1,0:T(8,128)(2,1)S(1)}, u32[]{:S(2)}, u32[]{:S(2)}) collective-permute-start(bf16[8,7168]{1,0:T(8,128)(2,1)S(1)} %fusion.2), channel_id=1, source_target_pairs={{0,4},{1,5},{2,6},{3,7},{4,0},{5,1},{6,2},{7,3},{8,12},{9,13},{10,... | collective-permute-start | bytes 344072 | tf_op jit(solution)/shard_map/ppermute | solution.py:59
  41.5 6.4 %collective-permute-start.11 = (bf16[8,7168]{1,0:T(8,128)(2,1)S(1)}, bf16[8,7168]{1,0:T(8,128)(2,1)S(1)}, u32[]{:S(2)}, u32[]{:S(2)}) collective-permute-start(bf16[8,7168]{1,0:T(8,128)(2,1)S(1)} %slice.61), channel_id=1, source_target_pairs={{0,2},{1,3},{2,0},{3,1},{4,6},{5,7},{6,4},{7,5},{8,9},{9,8},{10,11... | collective-permute-start | bytes 344072 | tf_op jit(solution)/shard_map/ppermute | solution.py:59
  (5 other events, 30.4 us)

commit v7 on v6

--- a/solution.py
+++ b/solution.py
@@ -179,7 +179,7 @@
     ]
     block = prepare(expert, tokens, expert_ids, route_weights, w_down)
     far = [swap(block, dims[-1], local_count)]
-    near = [block] + [swap_across(block, dims, m, local_count) for m in masks[1:]]
+    near = [block] + [swap_across(block, dims, m, local_count) for m in range(1, side)]
     far += [swap_across(far[0], dims, m, local_count) for m in masks[1:]]
     near = join(near, (w_down,), ())
     far = join(far, (w_down,))
@@ -215,7 +215,7 @@
 
     def gather_side(rows):
         total = rows[:tok_rows]
-        for i in range(1, local_count // 2):
+        for i in range(local_count // 2 - 1, 0, -1):
             part = rows[i * tok_rows : (i + 1) * tok_rows].astype(BF16)
             mask = sum(1 << k for k in range(bits - 1) if i >> (bits - 2 - k) & 1)
             total = total + swap_across(part, dims, mask, local_count).astype(F32)
@@ -224,7 +224,7 @@
     far = own_high + swap_core(other_high, node_count).astype(F32)
     near = own_low + swap_core(other_low, node_count).astype(F32)
     far = gather_side(far)
-    for dim in dims[:-1]:
+    for dim in dims[-2::-1]:
         near = halve(near, dim)
     far = swap(far.astype(BF16), dims[-1], local_count)
     return (near + far.astype(F32)).astype(BF16)

time: 48.8 us -> 47.9 us (0.982)
  starting transfers between devices: 20.8 us -> 20.2 us
    ppermute x13, starting transfers between devices: 20.1 us -> 19.5 us  [swap_across(): return lax.ppermute(array, ('node', 'local'), perm)]
  transfers between devices with their start and end apart: 17 -> 17, of which waited for: 13 -> 11; matrix products, arithmetic and copies ran while one was open for 1% -> 1% of each run, Pallas kernels for 0% -> 0%
where the time goes in v7:
time: 47.9 us; the launch traced here: 47.7 us
  starting transfers between devices  20.2 us (42%)
  waiting for transfers between devices  18.8 us (39%)
  Pallas kernels  7.39 us (15%)
  other arithmetic  0.97 us (2%)
    ppermute x13, starting transfers between devices, swap_across(): return lax.ppermute(array, ('node', 'local'), perm)  19.5 us
    ppermute x13, waiting for transfers between devices, swap_across(): return lax.ppermute(array, ('node', 'local'), perm)  15.6 us
    pallas_call x4, Pallas kernels, call(): pl.pallas_call(body, out_shape=outs, in_specs=[pl.BlockSpec(memory_space=...  6.22 us
    ppermute x4, waiting for transfers between devices, swap_core(): return lax.ppermute(array, 'node', [(n, n ^ 1) for n in range(node_count)])  3.12 us
    pallas_call x1, Pallas kernels, prepare(): pl.pallas_call(prepare_kernel, out_shape=VM((tokens.shape[0], tokens.shap...  1.17 us
  transfers between devices with their start and end apart: 17, of which 11 were waited for; matrix products, arithmetic and copies ran while one was open for 1% of the time, Pallas kernels for 0%

profile of v7, /device:TPU:0, one launch (start us, length us, event | category | flops | bytes accessed | tf_op | source)
XLA Modules:
  0.0 47.7 jit_solution(294988450244937402)
XLA Ops:
  0.0 1.2 %shard_map.64.refs_1_ = bf16[8,7296]{1,0:T(8,128)(2,1)S(1)} custom-call(s32[1]{0:T(128)} %bitcast._.refs_0_, bf16[8,7168]{1,0:T(8,128)(2,1)} %tokens_far.1, s32[8,8]{1,0:T(8,128)} %ids_far.1, bf16[8,8]{1,0:T(8,128)(2,1)} %weights_far.1, bf16[1,1024,7168]{2,1,0:T(8,128)(2,1)} %refs_1_.3), custom_call_target="tpu_custom_call" | custom-call | bytes 200000 | tf_op jit(solution)/shard_map/pallas_call | solution.py:91
  1.2 4.1 %collective-permute-start.3 = (bf16[8,7296]{1,0:T(8,128)(2,1)S(1)}, bf16[8,7296]{1,0:T(8,128)(2,1)S(1)}, u32[]{:S(2)}, u32[]{:S(2)}) collective-permute-start(bf16[8,7296]{1,0:T(8,128)(2,1)S(1)} %shard_map.64.refs_1_), channel_id=1, source_target_pairs={{0,4},{1,5},{2,6},{3,7},{4,0},{5,1},{6,2},{7,3},{8,12},{9,13},{10,... | collective-permute-start | bytes 350216 | tf_op jit(solution)/shard_map/ppermute | solution.py:59
  5.3 2.5 %collective-permute-start.2 = (bf16[8,7296]{1,0:T(8,128)(2,1)S(1)}, bf16[8,7296]{1,0:T(8,128)(2,1)S(1)}, u32[]{:S(2)}, u32[]{:S(2)}) collective-permute-start(bf16[8,7296]{1,0:T(8,128)(2,1)S(1)} %shard_map.64.refs_1_), channel_id=1, source_target_pairs={{0,3},{1,2},{2,1},{3,0},{4,7},{5,6},{6,5},{7,4},{8,11},{9,10},{10,... | collective-permute-start | bytes 350216 | tf_op jit(solution)/shard_map/ppermute | solution.py:59
  8.8 2.3 %collective-permute-done.3.refs_1_ = bf16[8,7296]{1,0:T(8,128)(2,1)S(1)} collective-permute-done((bf16[8,7296]{1,0:T(8,128)(2,1)S(1)}, bf16[8,7296]{1,0:T(8,128)(2,1)S(1)}, u32[]{:S(2)}, u32[]{:S(2)}) %collective-permute-start.3) | collective-permute-done | bytes 116768 | tf_op jit(solution)/shard_map/ppermute | solution.py:59
  11.1 1.6 %collective-permute-start.6 = (bf16[8,7296]{1,0:T(8,128)(2,1)S(1)}, bf16[8,7296]{1,0:T(8,128)(2,1)S(1)}, u32[]{:S(2)}, u32[]{:S(2)}) collective-permute-start(bf16[8,7296]{1,0:T(8,128)(2,1)S(1)} %collective-permute-done.3.refs_1_), channel_id=1, source_target_pairs={{0,3},{1,2},{2,1},{3,0},{4,7},{5,6},{6,5},{7,4},{8,11},{9,10},{10,... | collective-permute-start | bytes 350216 | tf_op jit(solution)/shard_map/ppermute | solution.py:59
  13.3 1.6 %collective-permute-start.4 = (bf16[8,7296]{1,0:T(8,128)(2,1)S(1)}, bf16[8,7296]{1,0:T(8,128)(2,1)S(1)}, u32[]{:S(2)}, u32[]{:S(2)}) collective-permute-start(bf16[8,7296]{1,0:T(8,128)(2,1)S(1)} %collective-permute-done.3.refs_1_), channel_id=1, source_target_pairs={{0,2},{1,3},{2,0},{3,1},{4,6},{5,7},{6,4},{7,5},{8,9},{9,8},{10,11... | collective-permute-start | bytes 350216 | tf_op jit(solution)/shard_map/ppermute | solution.py:59
  14.9 0.8 %collective-permute-done.1.refs_3_ = bf16[8,7296]{1,0:T(8,128)(2,1)S(1)} collective-permute-done((bf16[8,7296]{1,0:T(8,128)(2,1)S(1)}, bf16[8,7296]{1,0:T(8,128)(2,1)S(1)}, u32[]{:S(2)}, u32[]{:S(2)}) %collective-permute-start.1) | collective-permute-done | bytes 116768 | tf_op jit(solution)/shard_map/ppermute | solution.py:59
  15.8 2.4 %collective-permute-done.6.refs_4_ = bf16[8,7296]{1,0:T(8,128)(2,1)S(1)} collective-permute-done((bf16[8,7296]{1,0:T(8,128)(2,1)S(1)}, bf16[8,7296]{1,0:T(8,128)(2,1)S(1)}, u32[]{:S(2)}, u32[]{:S(2)}) %collective-permute-start.6) | collective-permute-done | bytes 116768 | tf_op jit(solution)/shard_map/ppermute | solution.py:59
  18.2 1.4 %collective-permute-done.5.refs_3_ = bf16[8,7296]{1,0:T(8,128)(2,1)S(1)} collective-permute-done((bf16[8,7296]{1,0:T(8,128)(2,1)S(1)}, bf16[8,7296]{1,0:T(8,128)(2,1)S(1)}, u32[]{:S(2)}, u32[]{:S(2)}) %collective-permute-start.5) | collective-permute-done | bytes 116768 | tf_op jit(solution)/shard_map/ppermute | solution.py:59
  19.9 1.8 %collective-permute-done.8.refs_5_.refs_6_ = bf16[32,7296]{1,0:T(8,128)(2,1)S(1)} collective-permute-done((bf16[32,7296]{1,0:T(8,128)(2,1)S(1)}, bf16[32,7296]{1,0:T(8,128)(2,1)S(1)}, u32[]{:S(2)}, u32[]{:S(2)}) %collective-permute-start.8) | collective-permute-done | bytes 466976 | tf_op jit(solution)/shard_map/ppermute | solution.py:67
  21.8 4.0 %shard_map.67.refs_2_ = bf16[128,1024]{1,0:T(8,128)(2,1)S(1)} custom-call(bf16[1,7168,1024]{2,1,0:T(8,128)(2,1)S(1)} %bitcast.4, bf16[1,7168,1024]{2,1,0:T(8,128)(2,1)S(1)} %bitcast.6, bf16[32,7296]{1,0:T(8,128)(2,1)S(1)} %shard_map.65.refs_2_.refs_3_, bf16[32,7296]{1,0:T(8,128)(2,1)S(1)} %shard_map.66.refs_3_.refs_4_, ...), custom_call_target="tpu_custom_call" | custom-call | flops 3758096384 | bytes 29360128 | tf_op jit(solution)/shard_map/pallas_call | solution.py:30
  25.9 2.1 %shard_map.68 = (f32[32,7168]{1,0:T(8,128)S(1)}, f32[32,7168]{1,0:T(8,128)S(1)}, bf16[32,7168]{1,0:T(8,128)(2,1)S(1)}, bf16[32,7168]{1,0:T(8,128)(2,1)S(1)}) custom-call(s32[1]{0:T(128)} %bitcast._.refs_0_, bf16[1,1024,7168]{2,1,0:T(8,128)(2,1)S(1)} %bitcast.2, bf16[128,1024]{1,0:T(8,128)(2,1)S(1)} %shard_map.67.refs_2_, ...), custom_call_target="tpu_custom_call" | custom-call | flops 1879048192 | bytes 14680064 | tf_op jit(solution)/shard_map/pallas_call | solution.py:30
  28.6 1.3 %collective-permute-done.12 = bf16[32,7168]{1,0:T(8,128)(2,1)S(1)} collective-permute-done((bf16[32,7168]{1,0:T(8,128)(2,1)S(1)}, bf16[32,7168]{1,0:T(8,128)(2,1)S(1)}, u32[]{:S(2)}, u32[]{:S(2)}) %collective-permute-start.12) | collective-permute-done | bytes 458784 | tf_op jit(solution)/shard_map/ppermute | solution.py:67
  30.0 1.5 %collective-permute-start.13 = (bf16[8,7168]{1,0:T(8,128)(2,1)S(1)}, bf16[8,7168]{1,0:T(8,128)(2,1)S(1)}, u32[]{:S(2)}, u32[]{:S(2)}) collective-permute-start(bf16[8,7168]{1,0:T(8,128)(2,1)S(1)} %get-tuple-element.15), channel_id=1, source_target_pairs={{0,3},{1,2},{2,1},{3,0},{4,7},{5,6},{6,5},{7,4},{8,11},{9,10},{10,... | collective-permute-start | bytes 344072 | tf_op jit(solution)/shard_map/ppermute | solution.py:59
  31.6 0.7 %collective-permute-start.15 = (bf16[8,7168]{1,0:T(8,128)(2,1)S(1)}, bf16[8,7168]{1,0:T(8,128)(2,1)S(1)}, u32[]{:S(2)}, u32[]{:S(2)}) collective-permute-start(bf16[8,7168]{1,0:T(8,128)(2,1)S(1)} %get-tuple-element.16), channel_id=1, source_target_pairs={{0,2},{1,3},{2,0},{3,1},{4,6},{5,7},{6,4},{7,5},{8,9},{9,8},{10,11... | collective-permute-start | bytes 344072 | tf_op jit(solution)/shard_map/ppermute | solution.py:59
  32.3 1.3 %collective-permute-start.14 = (bf16[8,7168]{1,0:T(8,128)(2,1)S(1)}, bf16[8,7168]{1,0:T(8,128)(2,1)S(1)}, u32[]{:S(2)}, u32[]{:S(2)}) collective-permute-start(bf16[8,7168]{1,0:T(8,128)(2,1)S(1)} %get-tuple-element.17), channel_id=1, source_target_pairs={{0,1},{1,0},{2,3},{3,2},{4,5},{5,4},{6,7},{7,6},{8,10},{9,11},{10,... | collective-permute-start | bytes 344072 | tf_op jit(solution)/shard_map/ppermute | solution.py:59
  33.7 1.4 %collective-permute-start.10 = (bf16[16,7168]{1,0:T(8,128)(2,1)S(1)}, bf16[16,7168]{1,0:T(8,128)(2,1)S(1)}, u32[]{:S(2)}, u32[]{:S(2)}) collective-permute-start(bf16[16,7168]{1,0:T(8,128)(2,1)S(1)} %slice.60), channel_id=1, source_target_pairs={{0,2},{1,3},{2,0},{3,1},{4,6},{5,7},{6,4},{7,5},{8,9},{9,8},{10,11... | collective-permute-start | bytes 688136 | tf_op jit(solution)/shard_map/ppermute | solution.py:59
  35.1 1.9 %collective-permute-done.13 = bf16[8,7168]{1,0:T(8,128)(2,1)S(1)} collective-permute-done((bf16[8,7168]{1,0:T(8,128)(2,1)S(1)}, bf16[8,7168]{1,0:T(8,128)(2,1)S(1)}, u32[]{:S(2)}, u32[]{:S(2)}) %collective-permute-start.13) | collective-permute-done | bytes 114720 | tf_op jit(solution)/shard_map/ppermute | solution.py:59
  37.0 0.9 %collective-permute-done.15 = bf16[8,7168]{1,0:T(8,128)(2,1)S(1)} collective-permute-done((bf16[8,7168]{1,0:T(8,128)(2,1)S(1)}, bf16[8,7168]{1,0:T(8,128)(2,1)S(1)}, u32[]{:S(2)}, u32[]{:S(2)}) %collective-permute-start.15) | collective-permute-done | bytes 114720 | tf_op jit(solution)/shard_map/ppermute | solution.py:59
  37.9 1.0 %collective-permute-done.14 = bf16[8,7168]{1,0:T(8,128)(2,1)S(1)} collective-permute-done((bf16[8,7168]{1,0:T(8,128)(2,1)S(1)}, bf16[8,7168]{1,0:T(8,128)(2,1)S(1)}, u32[]{:S(2)}, u32[]{:S(2)}) %collective-permute-start.14) | collective-permute-done | bytes 114720 | tf_op jit(solution)/shard_map/ppermute | solution.py:59
  39.0 2.1 %collective-permute-start.16 = (bf16[8,7168]{1,0:T(8,128)(2,1)S(1)}, bf16[8,7168]{1,0:T(8,128)(2,1)S(1)}, u32[]{:S(2)}, u32[]{:S(2)}) collective-permute-start(bf16[8,7168]{1,0:T(8,128)(2,1)S(1)} %fusion.2), channel_id=1, source_target_pairs={{0,4},{1,5},{2,6},{3,7},{4,0},{5,1},{6,2},{7,3},{8,12},{9,13},{10,... | collective-permute-start | bytes 344072 | tf_op jit(solution)/shard_map/ppermute | solution.py:59
  41.2 1.1 %collective-permute-start.11 = (bf16[8,7168]{1,0:T(8,128)(2,1)S(1)}, bf16[8,7168]{1,0:T(8,128)(2,1)S(1)}, u32[]{:S(2)}, u32[]{:S(2)}) collective-permute-start(bf16[8,7168]{1,0:T(8,128)(2,1)S(1)} %slice.61), channel_id=1, source_target_pairs={{0,1},{1,0},{2,3},{3,2},{4,5},{5,4},{6,7},{7,6},{8,10},{9,11},{10,... | collective-permute-start | bytes 344072 | tf_op jit(solution)/shard_map/ppermute | solution.py:59
  42.3 4.8 %collective-permute-done.16 = bf16[8,7168]{1,0:T(8,128)(2,1)S(1)} collective-permute-done((bf16[8,7168]{1,0:T(8,128)(2,1)S(1)}, bf16[8,7168]{1,0:T(8,128)(2,1)S(1)}, u32[]{:S(2)}, u32[]{:S(2)}) %collective-permute-start.16) | collective-permute-done | bytes 114720 | tf_op jit(solution)/shard_map/ppermute | solution.py:59
  47.1 0.7 %fusion.4 = bf16[8,7168]{1,0:T(8,128)(2,1)} fusion(f32[16,7168]{1,0:T(8,128)S(1)} %slice_add_fusion, bf16[8,7168]{1,0:T(8,128)(2,1)S(1)} %collective-permute-done.16, bf16[8,7168]{1,0:T(8,128)(2,1)S(1)} %collective-permute-done.11), kind=kLoop, calls=%fused_computation.11 | loop fusion | flops 286720 | bytes 573440 | tf_op jit(solution)/shard_map/convert_element_type | solution.py:230
  (50 shorter events, 2.8 us)
Async XLA Ops:
  0.0 21.7 %slice-start.8 = ((s8[14680064]{0:T(1024)(128)(4,1)}), s8[4194304]{0:T(1024)(128)(4,1)S(1)}, s32[]{:S(2)}) async-start(s8[14680064]{0:T(1024)(128)(4,1)} %bitcast.5), calls=%async_computation.8 | async-start | bytes 8388608
  0.0 21.7 %slice-start.9 = ((s8[14680064]{0:T(1024)(128)(4,1)}), s8[4194304]{0:T(1024)(128)(4,1)S(1)}, s32[]{:S(2)}) async-start(s8[14680064]{0:T(1024)(128)(4,1)} %bitcast.5), calls=%async_computation.9 | async-start | bytes 8388608
  1.2 20.6 %slice-start.4 = ((s8[14680064]{0:T(1024)(128)(4,1)}), s8[4194304]{0:T(1024)(128)(4,1)S(1)}, s32[]{:S(2)}) async-start(s8[14680064]{0:T(1024)(128)(4,1)} %bitcast.3), calls=%async_computation.4 | async-start | bytes 8388608
  1.2 20.5 %slice-start.5 = ((s8[14680064]{0:T(1024)(128)(4,1)}), s8[4194304]{0:T(1024)(128)(4,1)S(1)}, s32[]{:S(2)}) async-start(s8[14680064]{0:T(1024)(128)(4,1)} %bitcast.3), calls=%async_computation.5 | async-start | bytes 8388608
  1.2 20.5 %slice-start.10 = ((s8[14680064]{0:T(1024)(128)(4,1)}), s8[4194304]{0:T(1024)(128)(4,1)S(1)}, s32[]{:S(2)}) async-start(s8[14680064]{0:T(1024)(128)(4,1)} %bitcast.5), calls=%async_computation.10 | async-start | bytes 8388608
  1.2 9.9 %collective-permute-start.3 = (bf16[8,7296]{1,0:T(8,128)(2,1)S(1)}, bf16[8,7296]{1,0:T(8,128)(2,1)S(1)}, u32[]{:S(2)}, u32[]{:S(2)}) collective-permute-start(bf16[8,7296]{1,0:T(8,128)(2,1)S(1)} %shard_map.64.refs_1_), channel_id=1, source_target_pairs={{0,4},{1,5},{2,6},{3,7},{4,0},{5,1},{6,2},{7,3},{8,12},{9,13},{10,... | collective-permute-start | bytes 350216 | tf_op jit(solution)/shard_map/ppermute | solution.py:59
  5.3 7.9 %collective-permute-start.2 = (bf16[8,7296]{1,0:T(8,128)(2,1)S(1)}, bf16[8,7296]{1,0:T(8,128)(2,1)S(1)}, u32[]{:S(2)}, u32[]{:S(2)}) collective-permute-start(bf16[8,7296]{1,0:T(8,128)(2,1)S(1)} %shard_map.64.refs_1_), channel_id=1, source_target_pairs={{0,3},{1,2},{2,1},{3,0},{4,7},{5,6},{6,5},{7,4},{8,11},{9,10},{10,... | collective-permute-start | bytes 350216 | tf_op jit(solution)/shard_map/ppermute | solution.py:59
  7.9 7.8 %collective-permute-start.1 = (bf16[8,7296]{1,0:T(8,128)(2,1)S(1)}, bf16[8,7296]{1,0:T(8,128)(2,1)S(1)}, u32[]{:S(2)}, u32[]{:S(2)}) collective-permute-start(bf16[8,7296]{1,0:T(8,128)(2,1)S(1)} %shard_map.64.refs_1_), channel_id=1, source_target_pairs={{0,2},{1,3},{2,0},{3,1},{4,6},{5,7},{6,4},{7,5},{8,9},{9,8},{10,11... | collective-permute-start | bytes 350216 | tf_op jit(solution)/shard_map/ppermute | solution.py:59
  8.3 7.3 %collective-permute-start = (bf16[8,7296]{1,0:T(8,128)(2,1)S(1)}, bf16[8,7296]{1,0:T(8,128)(2,1)S(1)}, u32[]{:S(2)}, u32[]{:S(2)}) collective-permute-start(bf16[8,7296]{1,0:T(8,128)(2,1)S(1)} %shard_map.64.refs_1_), channel_id=1, source_target_pairs={{0,1},{1,0},{2,3},{3,2},{4,5},{5,4},{6,7},{7,6},{8,10},{9,11},{10,... | collective-permute-start | bytes 350216 | tf_op jit(solution)/shard_map/ppermute | solution.py:59
  11.1 7.1 %collective-permute-start.6 = (bf16[8,7296]{1,0:T(8,128)(2,1)S(1)}, bf16[8,7296]{1,0:T(8,128)(2,1)S(1)}, u32[]{:S(2)}, u32[]{:S(2)}) collective-permute-start(bf16[8,7296]{1,0:T(8,128)(2,1)S(1)} %collective-permute-done.3.refs_1_), channel_id=1, source_target_pairs={{0,3},{1,2},{2,1},{3,0},{4,7},{5,6},{6,5},{7,4},{8,11},{9,10},{10,... | collective-permute-start | bytes 350216 | tf_op jit(solution)/shard_map/ppermute | solution.py:59
  12.7 6.9 %collective-permute-start.5 = (bf16[8,7296]{1,0:T(8,128)(2,1)S(1)}, bf16[8,7296]{1,0:T(8,128)(2,1)S(1)}, u32[]{:S(2)}, u32[]{:S(2)}) collective-permute-start(bf16[8,7296]{1,0:T(8,128)(2,1)S(1)} %collective-permute-done.3.refs_1_), channel_id=1, source_target_pairs={{0,1},{1,0},{2,3},{3,2},{4,5},{5,4},{6,7},{7,6},{8,10},{9,11},{10,... | collective-permute-start | bytes 350216 | tf_op jit(solution)/shard_map/ppermute | solution.py:59
  13.3 6.5 %collective-permute-start.4 = (bf16[8,7296]{1,0:T(8,128)(2,1)S(1)}, bf16[8,7296]{1,0:T(8,128)(2,1)S(1)}, u32[]{:S(2)}, u32[]{:S(2)}) collective-permute-start(bf16[8,7296]{1,0:T(8,128)(2,1)S(1)} %collective-permute-done.3.refs_1_), channel_id=1, source_target_pairs={{0,2},{1,3},{2,0},{3,1},{4,6},{5,7},{6,4},{7,5},{8,9},{9,8},{10,11... | collective-permute-start | bytes 350216 | tf_op jit(solution)/shard_map/ppermute | solution.py:59
  15.7 6.1 %slice-start.6 = ((s8[14680064]{0:T(1024)(128)(4,1)}), s8[4194304]{0:T(1024)(128)(4,1)S(1)}, s32[]{:S(2)}) async-start(s8[14680064]{0:T(1024)(128)(4,1)} %bitcast.3), calls=%async_computation.6 | async-start | bytes 8388608
  15.7 4.2 %collective-permute-start.7 = (bf16[32,7296]{1,0:T(8,128)(2,1)S(1)}, bf16[32,7296]{1,0:T(8,128)(2,1)S(1)}, u32[]{:S(2)}, u32[]{:S(2)}) collective-permute-start(bf16[32,7296]{1,0:T(8,128)(2,1)S(1)} %shard_map.65.refs_2_.refs_3_), channel_id=1, source_target_pairs={{0,8},{8,0},{1,9},{9,1},{2,10},{10,2},{3,11},{11,3},{4,12},{12,4},... | collective-permute-start | bytes 1400840 | tf_op jit(solution)/shard_map/ppermute | solution.py:67
  19.8 6.1 %slice-start.1 = ((s8[14680064]{0:T(1024)(128)(4,1)}), s8[4194304]{0:T(1024)(128)(4,1)S(1)}, s32[]{:S(2)}) async-start(s8[14680064]{0:T(1024)(128)(4,1)} %bitcast.1), calls=%async_computation.1 | async-start | bytes 8388608
  19.8 1.9 %collective-permute-start.8 = (bf16[32,7296]{1,0:T(8,128)(2,1)S(1)}, bf16[32,7296]{1,0:T(8,128)(2,1)S(1)}, u32[]{:S(2)}, u32[]{:S(2)}) collective-permute-start(bf16[32,7296]{1,0:T(8,128)(2,1)S(1)} %shard_map.66.refs_3_.refs_4_), channel_id=1, source_target_pairs={{0,8},{8,0},{1,9},{9,1},{2,10},{10,2},{3,11},{11,3},{4,12},{12,4},... | collective-permute-start | bytes 1400840 | tf_op jit(solution)/shard_map/ppermute | solution.py:67
  28.0 1.9 %collective-permute-start.12 = (bf16[32,7168]{1,0:T(8,128)(2,1)S(1)}, bf16[32,7168]{1,0:T(8,128)(2,1)S(1)}, u32[]{:S(2)}, u32[]{:S(2)}) collective-permute-start(bf16[32,7168]{1,0:T(8,128)(2,1)S(1)} %get-tuple-element.12), channel_id=1, source_target_pairs={{0,8},{8,0},{1,9},{9,1},{2,10},{10,2},{3,11},{11,3},{4,12},{12,4},... | collective-permute-start | bytes 1376264 | tf_op jit(solution)/shard_map/ppermute | solution.py:67
  28.2 5.4 %collective-permute-start.9 = (bf16[32,7168]{1,0:T(8,128)(2,1)S(1)}, bf16[32,7168]{1,0:T(8,128)(2,1)S(1)}, u32[]{:S(2)}, u32[]{:S(2)}) collective-permute-start(bf16[32,7168]{1,0:T(8,128)(2,1)S(1)} %get-tuple-element.10), channel_id=1, source_target_pairs={{0,8},{8,0},{1,9},{9,1},{2,10},{10,2},{3,11},{11,3},{4,12},{12,4},... | collective-permute-start | bytes 1376264 | tf_op jit(solution)/shard_map/ppermute | solution.py:67
  30.0 7.0 %collective-permute-start.13 = (bf16[8,7168]{1,0:T(8,128)(2,1)S(1)}, bf16[8,7168]{1,0:T(8,128)(2,1)S(1)}, u32[]{:S(2)}, u32[]{:S(2)}) collective-permute-start(bf16[8,7168]{1,0:T(8,128)(2,1)S(1)} %get-tuple-element.15), channel_id=1, source_target_pairs={{0,3},{1,2},{2,1},{3,0},{4,7},{5,6},{6,5},{7,4},{8,11},{9,10},{10,... | collective-permute-start | bytes 344072 | tf_op jit(solution)/shard_map/ppermute | solution.py:59
  31.6 6.3 %collective-permute-start.15 = (bf16[8,7168]{1,0:T(8,128)(2,1)S(1)}, bf16[8,7168]{1,0:T(8,128)(2,1)S(1)}, u32[]{:S(2)}, u32[]{:S(2)}) collective-permute-start(bf16[8,7168]{1,0:T(8,128)(2,1)S(1)} %get-tuple-element.16), channel_id=1, source_target_pairs={{0,2},{1,3},{2,0},{3,1},{4,6},{5,7},{6,4},{7,5},{8,9},{9,8},{10,11... | collective-permute-start | bytes 344072 | tf_op jit(solution)/shard_map/ppermute | solution.py:59
  32.3 6.6 %collective-permute-start.14 = (bf16[8,7168]{1,0:T(8,128)(2,1)S(1)}, bf16[8,7168]{1,0:T(8,128)(2,1)S(1)}, u32[]{:S(2)}, u32[]{:S(2)}) collective-permute-start(bf16[8,7168]{1,0:T(8,128)(2,1)S(1)} %get-tuple-element.17), channel_id=1, source_target_pairs={{0,1},{1,0},{2,3},{3,2},{4,5},{5,4},{6,7},{7,6},{8,10},{9,11},{10,... | collective-permute-start | bytes 344072 | tf_op jit(solution)/shard_map/ppermute | solution.py:59
  33.7 7.4 %collective-permute-start.10 = (bf16[16,7168]{1,0:T(8,128)(2,1)S(1)}, bf16[16,7168]{1,0:T(8,128)(2,1)S(1)}, u32[]{:S(2)}, u32[]{:S(2)}) collective-permute-start(bf16[16,7168]{1,0:T(8,128)(2,1)S(1)} %slice.60), channel_id=1, source_target_pairs={{0,2},{1,3},{2,0},{3,1},{4,6},{5,7},{6,4},{7,5},{8,9},{9,8},{10,11... | collective-permute-start | bytes 688136 | tf_op jit(solution)/shard_map/ppermute | solution.py:59
  39.0 8.1 %collective-permute-start.16 = (bf16[8,7168]{1,0:T(8,128)(2,1)S(1)}, bf16[8,7168]{1,0:T(8,128)(2,1)S(1)}, u32[]{:S(2)}, u32[]{:S(2)}) collective-permute-start(bf16[8,7168]{1,0:T(8,128)(2,1)S(1)} %fusion.2), channel_id=1, source_target_pairs={{0,4},{1,5},{2,6},{3,7},{4,0},{5,1},{6,2},{7,3},{8,12},{9,13},{10,... | collective-permute-start | bytes 344072 | tf_op jit(solution)/shard_map/ppermute | solution.py:59
  41.2 5.9 %collective-permute-start.11 = (bf16[8,7168]{1,0:T(8,128)(2,1)S(1)}, bf16[8,7168]{1,0:T(8,128)(2,1)S(1)}, u32[]{:S(2)}, u32[]{:S(2)}) collective-permute-start(bf16[8,7168]{1,0:T(8,128)(2,1)S(1)} %slice.61), channel_id=1, source_target_pairs={{0,1},{1,0},{2,3},{3,2},{4,5},{5,4},{6,7},{7,6},{8,10},{9,11},{10,... | collective-permute-start | bytes 344072 | tf_op jit(solution)/shard_map/ppermute | solution.py:59
  (5 other events, 30.4 us)

commit v8 on v7

--- a/solution.py
+++ b/solution.py
@@ -215,7 +215,7 @@
 
     def gather_side(rows):
         total = rows[:tok_rows]
-        for i in range(local_count // 2 - 1, 0, -1):
+        for i in [*range(2, local_count // 2), 1]:
             part = rows[i * tok_rows : (i + 1) * tok_rows].astype(BF16)
             mask = sum(1 << k for k in range(bits - 1) if i >> (bits - 2 - k) & 1)
             total = total + swap_across(part, dims, mask, local_count).astype(F32)

time: 47.9 us -> 47.2 us (0.985)
  waiting for transfers between devices: 18.8 us -> 17.8 us
    ppermute x13, waiting for transfers between devices: 15.6 us -> 14.7 us  [swap_across(): return lax.ppermute(array, ('node', 'local'), perm)]
  transfers between devices with their start and end apart: 17 -> 17, of which waited for: 11 -> 10; matrix products, arithmetic and copies ran while one was open for 1% -> 1% of each run, Pallas kernels for 0% -> 0%
where the time goes in v8:
time: 47.2 us; the launch traced here: 47 us
  starting transfers between devices  20.4 us (43%)
  waiting for transfers between devices  17.8 us (38%)
  Pallas kernels  7.39 us (16%)
  other arithmetic  0.97 us (2%)
    ppermute x13, starting transfers between devices, swap_across(): return lax.ppermute(array, ('node', 'local'), perm)  19.7 us
    ppermute x13, waiting for transfers between devices, swap_across(): return lax.ppermute(array, ('node', 'local'), perm)  14.7 us
    pallas_call x4, Pallas kernels, call(): pl.pallas_call(body, out_shape=outs, in_specs=[pl.BlockSpec(memory_space=...  6.22 us
    ppermute x4, waiting for transfers between devices, swap_core(): return lax.ppermute(array, 'node', [(n, n ^ 1) for n in range(node_count)])  3.12 us
    pallas_call x1, Pallas kernels, prepare(): pl.pallas_call(prepare_kernel, out_shape=VM((tokens.shape[0], tokens.shap...  1.17 us
  transfers between devices with their start and end apart: 17, of which 10 were waited for; matrix products, arithmetic and copies ran while one was open for 1% of the time, Pallas kernels for 0%

profile of v8, /device:TPU:0, one launch (start us, length us, event | category | flops | bytes accessed | tf_op | source)
XLA Modules:
  0.0 47.0 jit_solution(10663429836607164754)
XLA Ops:
  0.0 1.2 %shard_map.64.refs_1_ = bf16[8,7296]{1,0:T(8,128)(2,1)S(1)} custom-call(s32[1]{0:T(128)} %bitcast._.refs_0_, bf16[8,7168]{1,0:T(8,128)(2,1)} %tokens_far.1, s32[8,8]{1,0:T(8,128)} %ids_far.1, bf16[8,8]{1,0:T(8,128)(2,1)} %weights_far.1, bf16[1,1024,7168]{2,1,0:T(8,128)(2,1)} %refs_1_.3), custom_call_target="tpu_custom_call" | custom-call | bytes 200000 | tf_op jit(solution)/shard_map/pallas_call | solution.py:91
  1.2 4.1 %collective-permute-start.3 = (bf16[8,7296]{1,0:T(8,128)(2,1)S(1)}, bf16[8,7296]{1,0:T(8,128)(2,1)S(1)}, u32[]{:S(2)}, u32[]{:S(2)}) collective-permute-start(bf16[8,7296]{1,0:T(8,128)(2,1)S(1)} %shard_map.64.refs_1_), channel_id=1, source_target_pairs={{0,4},{1,5},{2,6},{3,7},{4,0},{5,1},{6,2},{7,3},{8,12},{9,13},{10,... | collective-permute-start | bytes 350216 | tf_op jit(solution)/shard_map/ppermute | solution.py:59
  5.3 2.5 %collective-permute-start.2 = (bf16[8,7296]{1,0:T(8,128)(2,1)S(1)}, bf16[8,7296]{1,0:T(8,128)(2,1)S(1)}, u32[]{:S(2)}, u32[]{:S(2)}) collective-permute-start(bf16[8,7296]{1,0:T(8,128)(2,1)S(1)} %shard_map.64.refs_1_), channel_id=1, source_target_pairs={{0,3},{1,2},{2,1},{3,0},{4,7},{5,6},{6,5},{7,4},{8,11},{9,10},{10,... | collective-permute-start | bytes 350216 | tf_op jit(solution)/shard_map/ppermute | solution.py:59
  8.3 0.5 %collective-permute-start = (bf16[8,7296]{1,0:T(8,128)(2,1)S(1)}, bf16[8,7296]{1,0:T(8,128)(2,1)S(1)}, u32[]{:S(2)}, u32[]{:S(2)}) collective-permute-start(bf16[8,7296]{1,0:T(8,128)(2,1)S(1)} %shard_map.64.refs_1_), channel_id=1, source_target_pairs={{0,1},{1,0},{2,3},{3,2},{4,5},{5,4},{6,7},{7,6},{8,10},{9,11},{10,... | collective-permute-start | bytes 350216 | tf_op jit(solution)/shard_map/ppermute | solution.py:59
  8.8 2.3 %collective-permute-done.3.refs_1_ = bf16[8,7296]{1,0:T(8,128)(2,1)S(1)} collective-permute-done((bf16[8,7296]{1,0:T(8,128)(2,1)S(1)}, bf16[8,7296]{1,0:T(8,128)(2,1)S(1)}, u32[]{:S(2)}, u32[]{:S(2)}) %collective-permute-start.3) | collective-permute-done | bytes 116768 | tf_op jit(solution)/shard_map/ppermute | solution.py:59
  11.1 1.6 %collective-permute-start.6 = (bf16[8,7296]{1,0:T(8,128)(2,1)S(1)}, bf16[8,7296]{1,0:T(8,128)(2,1)S(1)}, u32[]{:S(2)}, u32[]{:S(2)}) collective-permute-start(bf16[8,7296]{1,0:T(8,128)(2,1)S(1)} %collective-permute-done.3.refs_1_), channel_id=1, source_target_pairs={{0,3},{1,2},{2,1},{3,0},{4,7},{5,6},{6,5},{7,4},{8,11},{9,10},{10,... | collective-permute-start | bytes 350216 | tf_op jit(solution)/shard_map/ppermute | solution.py:59
  13.3 1.6 %collective-permute-start.4 = (bf16[8,7296]{1,0:T(8,128)(2,1)S(1)}, bf16[8,7296]{1,0:T(8,128)(2,1)S(1)}, u32[]{:S(2)}, u32[]{:S(2)}) collective-permute-start(bf16[8,7296]{1,0:T(8,128)(2,1)S(1)} %collective-permute-done.3.refs_1_), channel_id=1, source_target_pairs={{0,2},{1,3},{2,0},{3,1},{4,6},{5,7},{6,4},{7,5},{8,9},{9,8},{10,11... | collective-permute-start | bytes 350216 | tf_op jit(solution)/shard_map/ppermute | solution.py:59
  14.9 0.8 %collective-permute-done.1.refs_3_ = bf16[8,7296]{1,0:T(8,128)(2,1)S(1)} collective-permute-done((bf16[8,7296]{1,0:T(8,128)(2,1)S(1)}, bf16[8,7296]{1,0:T(8,128)(2,1)S(1)}, u32[]{:S(2)}, u32[]{:S(2)}) %collective-permute-start.1) | collective-permute-done | bytes 116768 | tf_op jit(solution)/shard_map/ppermute | solution.py:59
  15.8 2.4 %collective-permute-done.6.refs_4_ = bf16[8,7296]{1,0:T(8,128)(2,1)S(1)} collective-permute-done((bf16[8,7296]{1,0:T(8,128)(2,1)S(1)}, bf16[8,7296]{1,0:T(8,128)(2,1)S(1)}, u32[]{:S(2)}, u32[]{:S(2)}) %collective-permute-start.6) | collective-permute-done | bytes 116768 | tf_op jit(solution)/shard_map/ppermute | solution.py:59
  18.2 1.4 %collective-permute-done.5.refs_3_ = bf16[8,7296]{1,0:T(8,128)(2,1)S(1)} collective-permute-done((bf16[8,7296]{1,0:T(8,128)(2,1)S(1)}, bf16[8,7296]{1,0:T(8,128)(2,1)S(1)}, u32[]{:S(2)}, u32[]{:S(2)}) %collective-permute-start.5) | collective-permute-done | bytes 116768 | tf_op jit(solution)/shard_map/ppermute | solution.py:59
  19.9 1.8 %collective-permute-done.8.refs_5_.refs_6_ = bf16[32,7296]{1,0:T(8,128)(2,1)S(1)} collective-permute-done((bf16[32,7296]{1,0:T(8,128)(2,1)S(1)}, bf16[32,7296]{1,0:T(8,128)(2,1)S(1)}, u32[]{:S(2)}, u32[]{:S(2)}) %collective-permute-start.8) | collective-permute-done | bytes 466976 | tf_op jit(solution)/shard_map/ppermute | solution.py:67
  21.8 4.0 %shard_map.67.refs_2_ = bf16[128,1024]{1,0:T(8,128)(2,1)S(1)} custom-call(bf16[1,7168,1024]{2,1,0:T(8,128)(2,1)S(1)} %bitcast.4, bf16[1,7168,1024]{2,1,0:T(8,128)(2,1)S(1)} %bitcast.6, bf16[32,7296]{1,0:T(8,128)(2,1)S(1)} %shard_map.65.refs_2_.refs_3_, bf16[32,7296]{1,0:T(8,128)(2,1)S(1)} %shard_map.66.refs_3_.refs_4_, ...), custom_call_target="tpu_custom_call" | custom-call | flops 3758096384 | bytes 29360128 | tf_op jit(solution)/shard_map/pallas_call | solution.py:30
  25.9 2.1 %shard_map.68 = (f32[32,7168]{1,0:T(8,128)S(1)}, f32[32,7168]{1,0:T(8,128)S(1)}, bf16[32,7168]{1,0:T(8,128)(2,1)S(1)}, bf16[32,7168]{1,0:T(8,128)(2,1)S(1)}) custom-call(s32[1]{0:T(128)} %bitcast._.refs_0_, bf16[1,1024,7168]{2,1,0:T(8,128)(2,1)S(1)} %bitcast.2, bf16[128,1024]{1,0:T(8,128)(2,1)S(1)} %shard_map.67.refs_2_, ...), custom_call_target="tpu_custom_call" | custom-call | flops 1879048192 | bytes 14680064 | tf_op jit(solution)/shard_map/pallas_call | solution.py:30
  28.6 1.3 %collective-permute-done.12 = bf16[32,7168]{1,0:T(8,128)(2,1)S(1)} collective-permute-done((bf16[32,7168]{1,0:T(8,128)(2,1)S(1)}, bf16[32,7168]{1,0:T(8,128)(2,1)S(1)}, u32[]{:S(2)}, u32[]{:S(2)}) %collective-permute-start.12) | collective-permute-done | bytes 458784 | tf_op jit(solution)/shard_map/ppermute | solution.py:67
  30.0 0.8 %collective-permute-start.13 = (bf16[8,7168]{1,0:T(8,128)(2,1)S(1)}, bf16[8,7168]{1,0:T(8,128)(2,1)S(1)}, u32[]{:S(2)}, u32[]{:S(2)}) collective-permute-start(bf16[8,7168]{1,0:T(8,128)(2,1)S(1)} %get-tuple-element.15), channel_id=1, source_target_pairs={{0,1},{1,0},{2,3},{3,2},{4,5},{5,4},{6,7},{7,6},{8,10},{9,11},{10,... | collective-permute-start | bytes 344072 | tf_op jit(solution)/shard_map/ppermute | solution.py:59
  30.9 1.3 %collective-permute-start.15 = (bf16[8,7168]{1,0:T(8,128)(2,1)S(1)}, bf16[8,7168]{1,0:T(8,128)(2,1)S(1)}, u32[]{:S(2)}, u32[]{:S(2)}) collective-permute-start(bf16[8,7168]{1,0:T(8,128)(2,1)S(1)} %get-tuple-element.16), channel_id=1, source_target_pairs={{0,2},{1,3},{2,0},{3,1},{4,6},{5,7},{6,4},{7,5},{8,9},{9,8},{10,11... | collective-permute-start | bytes 344072 | tf_op jit(solution)/shard_map/ppermute | solution.py:59
  32.2 1.4 %collective-permute-start.14 = (bf16[8,7168]{1,0:T(8,128)(2,1)S(1)}, bf16[8,7168]{1,0:T(8,128)(2,1)S(1)}, u32[]{:S(2)}, u32[]{:S(2)}) collective-permute-start(bf16[8,7168]{1,0:T(8,128)(2,1)S(1)} %get-tuple-element.17), channel_id=1, source_target_pairs={{0,3},{1,2},{2,1},{3,0},{4,7},{5,6},{6,5},{7,4},{8,11},{9,10},{10,... | collective-permute-start | bytes 344072 | tf_op jit(solution)/shard_map/ppermute | solution.py:59
  33.7 1.4 %collective-permute-start.10 = (bf16[16,7168]{1,0:T(8,128)(2,1)S(1)}, bf16[16,7168]{1,0:T(8,128)(2,1)S(1)}, u32[]{:S(2)}, u32[]{:S(2)}) collective-permute-start(bf16[16,7168]{1,0:T(8,128)(2,1)S(1)} %slice.60), channel_id=1, source_target_pairs={{0,2},{1,3},{2,0},{3,1},{4,6},{5,7},{6,4},{7,5},{8,9},{9,8},{10,11... | collective-permute-start | bytes 688136 | tf_op jit(solution)/shard_map/ppermute | solution.py:59
  35.1 1.5 %collective-permute-done.13 = bf16[8,7168]{1,0:T(8,128)(2,1)S(1)} collective-permute-done((bf16[8,7168]{1,0:T(8,128)(2,1)S(1)}, bf16[8,7168]{1,0:T(8,128)(2,1)S(1)}, u32[]{:S(2)}, u32[]{:S(2)}) %collective-permute-start.13) | collective-permute-done | bytes 114720 | tf_op jit(solution)/shard_map/ppermute | solution.py:59
  36.6 2.3 %collective-permute-done.14 = bf16[8,7168]{1,0:T(8,128)(2,1)S(1)} collective-permute-done((bf16[8,7168]{1,0:T(8,128)(2,1)S(1)}, bf16[8,7168]{1,0:T(8,128)(2,1)S(1)}, u32[]{:S(2)}, u32[]{:S(2)}) %collective-permute-start.14) | collective-permute-done | bytes 114720 | tf_op jit(solution)/shard_map/ppermute | solution.py:59
  39.0 2.4 %collective-permute-start.16 = (bf16[8,7168]{1,0:T(8,128)(2,1)S(1)}, bf16[8,7168]{1,0:T(8,128)(2,1)S(1)}, u32[]{:S(2)}, u32[]{:S(2)}) collective-permute-start(bf16[8,7168]{1,0:T(8,128)(2,1)S(1)} %fusion.2), channel_id=1, source_target_pairs={{0,4},{1,5},{2,6},{3,7},{4,0},{5,1},{6,2},{7,3},{8,12},{9,13},{10,... | collective-permute-start | bytes 344072 | tf_op jit(solution)/shard_map/ppermute | solution.py:59
  41.5 1.1 %collective-permute-start.11 = (bf16[8,7168]{1,0:T(8,128)(2,1)S(1)}, bf16[8,7168]{1,0:T(8,128)(2,1)S(1)}, u32[]{:S(2)}, u32[]{:S(2)}) collective-permute-start(bf16[8,7168]{1,0:T(8,128)(2,1)S(1)} %slice.61), channel_id=1, source_target_pairs={{0,1},{1,0},{2,3},{3,2},{4,5},{5,4},{6,7},{7,6},{8,10},{9,11},{10,... | collective-permute-start | bytes 344072 | tf_op jit(solution)/shard_map/ppermute | solution.py:59
  42.5 3.8 %collective-permute-done.16 = bf16[8,7168]{1,0:T(8,128)(2,1)S(1)} collective-permute-done((bf16[8,7168]{1,0:T(8,128)(2,1)S(1)}, bf16[8,7168]{1,0:T(8,128)(2,1)S(1)}, u32[]{:S(2)}, u32[]{:S(2)}) %collective-permute-start.16) | collective-permute-done | bytes 114720 | tf_op jit(solution)/shard_map/ppermute | solution.py:59
  46.3 0.7 %fusion.4 = bf16[8,7168]{1,0:T(8,128)(2,1)} fusion(f32[16,7168]{1,0:T(8,128)S(1)} %slice_add_fusion, bf16[8,7168]{1,0:T(8,128)(2,1)S(1)} %collective-permute-done.16, bf16[8,7168]{1,0:T(8,128)(2,1)S(1)} %collective-permute-done.11), kind=kLoop, calls=%fused_computation.11 | loop fusion | flops 286720 | bytes 573440 | tf_op jit(solution)/shard_map/convert_element_type | solution.py:230
  (50 shorter events, 2.3 us)
Async XLA Ops:
  0.0 21.7 %slice-start.8 = ((s8[14680064]{0:T(1024)(128)(4,1)}), s8[4194304]{0:T(1024)(128)(4,1)S(1)}, s32[]{:S(2)}) async-start(s8[14680064]{0:T(1024)(128)(4,1)} %bitcast.5), calls=%async_computation.8 | async-start | bytes 8388608
  0.0 21.7 %slice-start.9 = ((s8[14680064]{0:T(1024)(128)(4,1)}), s8[4194304]{0:T(1024)(128)(4,1)S(1)}, s32[]{:S(2)}) async-start(s8[14680064]{0:T(1024)(128)(4,1)} %bitcast.5), calls=%async_computation.9 | async-start | bytes 8388608
  1.2 20.6 %slice-start.4 = ((s8[14680064]{0:T(1024)(128)(4,1)}), s8[4194304]{0:T(1024)(128)(4,1)S(1)}, s32[]{:S(2)}) async-start(s8[14680064]{0:T(1024)(128)(4,1)} %bitcast.3), calls=%async_computation.4 | async-start | bytes 8388608
  1.2 20.5 %slice-start.5 = ((s8[14680064]{0:T(1024)(128)(4,1)}), s8[4194304]{0:T(1024)(128)(4,1)S(1)}, s32[]{:S(2)}) async-start(s8[14680064]{0:T(1024)(128)(4,1)} %bitcast.3), calls=%async_computation.5 | async-start | bytes 8388608
  1.2 20.5 %slice-start.10 = ((s8[14680064]{0:T(1024)(128)(4,1)}), s8[4194304]{0:T(1024)(128)(4,1)S(1)}, s32[]{:S(2)}) async-start(s8[14680064]{0:T(1024)(128)(4,1)} %bitcast.5), calls=%async_computation.10 | async-start | bytes 8388608
  1.2 9.9 %collective-permute-start.3 = (bf16[8,7296]{1,0:T(8,128)(2,1)S(1)}, bf16[8,7296]{1,0:T(8,128)(2,1)S(1)}, u32[]{:S(2)}, u32[]{:S(2)}) collective-permute-start(bf16[8,7296]{1,0:T(8,128)(2,1)S(1)} %shard_map.64.refs_1_), channel_id=1, source_target_pairs={{0,4},{1,5},{2,6},{3,7},{4,0},{5,1},{6,2},{7,3},{8,12},{9,13},{10,... | collective-permute-start | bytes 350216 | tf_op jit(solution)/shard_map/ppermute | solution.py:59
  5.3 7.9 %collective-permute-start.2 = (bf16[8,7296]{1,0:T(8,128)(2,1)S(1)}, bf16[8,7296]{1,0:T(8,128)(2,1)S(1)}, u32[]{:S(2)}, u32[]{:S(2)}) collective-permute-start(bf16[8,7296]{1,0:T(8,128)(2,1)S(1)} %shard_map.64.refs_1_), channel_id=1, source_target_pairs={{0,3},{1,2},{2,1},{3,0},{4,7},{5,6},{6,5},{7,4},{8,11},{9,10},{10,... | collective-permute-start | bytes 350216 | tf_op jit(solution)/shard_map/ppermute | solution.py:59
  7.9 7.8 %collective-permute-start.1 = (bf16[8,7296]{1,0:T(8,128)(2,1)S(1)}, bf16[8,7296]{1,0:T(8,128)(2,1)S(1)}, u32[]{:S(2)}, u32[]{:S(2)}) collective-permute-start(bf16[8,7296]{1,0:T(8,128)(2,1)S(1)} %shard_map.64.refs_1_), channel_id=1, source_target_pairs={{0,2},{1,3},{2,0},{3,1},{4,6},{5,7},{6,4},{7,5},{8,9},{9,8},{10,11... | collective-permute-start | bytes 350216 | tf_op jit(solution)/shard_map/ppermute | solution.py:59
  8.3 7.3 %collective-permute-start = (bf16[8,7296]{1,0:T(8,128)(2,1)S(1)}, bf16[8,7296]{1,0:T(8,128)(2,1)S(1)}, u32[]{:S(2)}, u32[]{:S(2)}) collective-permute-start(bf16[8,7296]{1,0:T(8,128)(2,1)S(1)} %shard_map.64.refs_1_), channel_id=1, source_target_pairs={{0,1},{1,0},{2,3},{3,2},{4,5},{5,4},{6,7},{7,6},{8,10},{9,11},{10,... | collective-permute-start | bytes 350216 | tf_op jit(solution)/shard_map/ppermute | solution.py:59
  11.1 7.1 %collective-permute-start.6 = (bf16[8,7296]{1,0:T(8,128)(2,1)S(1)}, bf16[8,7296]{1,0:T(8,128)(2,1)S(1)}, u32[]{:S(2)}, u32[]{:S(2)}) collective-permute-start(bf16[8,7296]{1,0:T(8,128)(2,1)S(1)} %collective-permute-done.3.refs_1_), channel_id=1, source_target_pairs={{0,3},{1,2},{2,1},{3,0},{4,7},{5,6},{6,5},{7,4},{8,11},{9,10},{10,... | collective-permute-start | bytes 350216 | tf_op jit(solution)/shard_map/ppermute | solution.py:59
  12.7 6.9 %collective-permute-start.5 = (bf16[8,7296]{1,0:T(8,128)(2,1)S(1)}, bf16[8,7296]{1,0:T(8,128)(2,1)S(1)}, u32[]{:S(2)}, u32[]{:S(2)}) collective-permute-start(bf16[8,7296]{1,0:T(8,128)(2,1)S(1)} %collective-permute-done.3.refs_1_), channel_id=1, source_target_pairs={{0,1},{1,0},{2,3},{3,2},{4,5},{5,4},{6,7},{7,6},{8,10},{9,11},{10,... | collective-permute-start | bytes 350216 | tf_op jit(solution)/shard_map/ppermute | solution.py:59
  13.3 6.5 %collective-permute-start.4 = (bf16[8,7296]{1,0:T(8,128)(2,1)S(1)}, bf16[8,7296]{1,0:T(8,128)(2,1)S(1)}, u32[]{:S(2)}, u32[]{:S(2)}) collective-permute-start(bf16[8,7296]{1,0:T(8,128)(2,1)S(1)} %collective-permute-done.3.refs_1_), channel_id=1, source_target_pairs={{0,2},{1,3},{2,0},{3,1},{4,6},{5,7},{6,4},{7,5},{8,9},{9,8},{10,11... | collective-permute-start | bytes 350216 | tf_op jit(solution)/shard_map/ppermute | solution.py:59
  15.7 6.1 %slice-start.6 = ((s8[14680064]{0:T(1024)(128)(4,1)}), s8[4194304]{0:T(1024)(128)(4,1)S(1)}, s32[]{:S(2)}) async-start(s8[14680064]{0:T(1024)(128)(4,1)} %bitcast.3), calls=%async_computation.6 | async-start | bytes 8388608
  15.7 4.2 %collective-permute-start.7 = (bf16[32,7296]{1,0:T(8,128)(2,1)S(1)}, bf16[32,7296]{1,0:T(8,128)(2,1)S(1)}, u32[]{:S(2)}, u32[]{:S(2)}) collective-permute-start(bf16[32,7296]{1,0:T(8,128)(2,1)S(1)} %shard_map.65.refs_2_.refs_3_), channel_id=1, source_target_pairs={{0,8},{8,0},{1,9},{9,1},{2,10},{10,2},{3,11},{11,3},{4,12},{12,4},... | collective-permute-start | bytes 1400840 | tf_op jit(solution)/shard_map/ppermute | solution.py:67
  19.8 6.1 %slice-start.1 = ((s8[14680064]{0:T(1024)(128)(4,1)}), s8[4194304]{0:T(1024)(128)(4,1)S(1)}, s32[]{:S(2)}) async-start(s8[14680064]{0:T(1024)(128)(4,1)} %bitcast.1), calls=%async_computation.1 | async-start | bytes 8388608
  19.8 1.9 %collective-permute-start.8 = (bf16[32,7296]{1,0:T(8,128)(2,1)S(1)}, bf16[32,7296]{1,0:T(8,128)(2,1)S(1)}, u32[]{:S(2)}, u32[]{:S(2)}) collective-permute-start(bf16[32,7296]{1,0:T(8,128)(2,1)S(1)} %shard_map.66.refs_3_.refs_4_), channel_id=1, source_target_pairs={{0,8},{8,0},{1,9},{9,1},{2,10},{10,2},{3,11},{11,3},{4,12},{12,4},... | collective-permute-start | bytes 1400840 | tf_op jit(solution)/shard_map/ppermute | solution.py:67
  28.0 1.9 %collective-permute-start.12 = (bf16[32,7168]{1,0:T(8,128)(2,1)S(1)}, bf16[32,7168]{1,0:T(8,128)(2,1)S(1)}, u32[]{:S(2)}, u32[]{:S(2)}) collective-permute-start(bf16[32,7168]{1,0:T(8,128)(2,1)S(1)} %get-tuple-element.12), channel_id=1, source_target_pairs={{0,8},{8,0},{1,9},{9,1},{2,10},{10,2},{3,11},{11,3},{4,12},{12,4},... | collective-permute-start | bytes 1376264 | tf_op jit(solution)/shard_map/ppermute | solution.py:67
  28.2 5.4 %collective-permute-start.9 = (bf16[32,7168]{1,0:T(8,128)(2,1)S(1)}, bf16[32,7168]{1,0:T(8,128)(2,1)S(1)}, u32[]{:S(2)}, u32[]{:S(2)}) collective-permute-start(bf16[32,7168]{1,0:T(8,128)(2,1)S(1)} %get-tuple-element.10), channel_id=1, source_target_pairs={{0,8},{8,0},{1,9},{9,1},{2,10},{10,2},{3,11},{11,3},{4,12},{12,4},... | collective-permute-start | bytes 1376264 | tf_op jit(solution)/shard_map/ppermute | solution.py:67
  30.0 6.6 %collective-permute-start.13 = (bf16[8,7168]{1,0:T(8,128)(2,1)S(1)}, bf16[8,7168]{1,0:T(8,128)(2,1)S(1)}, u32[]{:S(2)}, u32[]{:S(2)}) collective-permute-start(bf16[8,7168]{1,0:T(8,128)(2,1)S(1)} %get-tuple-element.15), channel_id=1, source_target_pairs={{0,1},{1,0},{2,3},{3,2},{4,5},{5,4},{6,7},{7,6},{8,10},{9,11},{10,... | collective-permute-start | bytes 344072 | tf_op jit(solution)/shard_map/ppermute | solution.py:59
  30.9 5.8 %collective-permute-start.15 = (bf16[8,7168]{1,0:T(8,128)(2,1)S(1)}, bf16[8,7168]{1,0:T(8,128)(2,1)S(1)}, u32[]{:S(2)}, u32[]{:S(2)}) collective-permute-start(bf16[8,7168]{1,0:T(8,128)(2,1)S(1)} %get-tuple-element.16), channel_id=1, source_target_pairs={{0,2},{1,3},{2,0},{3,1},{4,6},{5,7},{6,4},{7,5},{8,9},{9,8},{10,11... | collective-permute-start | bytes 344072 | tf_op jit(solution)/shard_map/ppermute | solution.py:59
  32.2 6.8 %collective-permute-start.14 = (bf16[8,7168]{1,0:T(8,128)(2,1)S(1)}, bf16[8,7168]{1,0:T(8,128)(2,1)S(1)}, u32[]{:S(2)}, u32[]{:S(2)}) collective-permute-start(bf16[8,7168]{1,0:T(8,128)(2,1)S(1)} %get-tuple-element.17), channel_id=1, source_target_pairs={{0,3},{1,2},{2,1},{3,0},{4,7},{5,6},{6,5},{7,4},{8,11},{9,10},{10,... | collective-permute-start | bytes 344072 | tf_op jit(solution)/shard_map/ppermute | solution.py:59
  33.7 7.7 %collective-permute-start.10 = (bf16[16,7168]{1,0:T(8,128)(2,1)S(1)}, bf16[16,7168]{1,0:T(8,128)(2,1)S(1)}, u32[]{:S(2)}, u32[]{:S(2)}) collective-permute-start(bf16[16,7168]{1,0:T(8,128)(2,1)S(1)} %slice.60), channel_id=1, source_target_pairs={{0,2},{1,3},{2,0},{3,1},{4,6},{5,7},{6,4},{7,5},{8,9},{9,8},{10,11... | collective-permute-start | bytes 688136 | tf_op jit(solution)/shard_map/ppermute | solution.py:59
  39.0 7.3 %collective-permute-start.16 = (bf16[8,7168]{1,0:T(8,128)(2,1)S(1)}, bf16[8,7168]{1,0:T(8,128)(2,1)S(1)}, u32[]{:S(2)}, u32[]{:S(2)}) collective-permute-start(bf16[8,7168]{1,0:T(8,128)(2,1)S(1)} %fusion.2), channel_id=1, source_target_pairs={{0,4},{1,5},{2,6},{3,7},{4,0},{5,1},{6,2},{7,3},{8,12},{9,13},{10,... | collective-permute-start | bytes 344072 | tf_op jit(solution)/shard_map/ppermute | solution.py:59
  41.5 4.9 %collective-permute-start.11 = (bf16[8,7168]{1,0:T(8,128)(2,1)S(1)}, bf16[8,7168]{1,0:T(8,128)(2,1)S(1)}, u32[]{:S(2)}, u32[]{:S(2)}) collective-permute-start(bf16[8,7168]{1,0:T(8,128)(2,1)S(1)} %slice.61), channel_id=1, source_target_pairs={{0,1},{1,0},{2,3},{3,2},{4,5},{5,4},{6,7},{7,6},{8,10},{9,11},{10,... | collective-permute-start | bytes 344072 | tf_op jit(solution)/shard_map/ppermute | solution.py:59
  (5 other events, 30.4 us)

commit v9 on v8

--- a/solution.py
+++ b/solution.py
@@ -215,7 +215,7 @@
 
     def gather_side(rows):
         total = rows[:tok_rows]
-        for i in [*range(2, local_count // 2), 1]:
+        for i in [*range(2, local_count // 2 - 1), 1, local_count // 2 - 1]:
             part = rows[i * tok_rows : (i + 1) * tok_rows].astype(BF16)
             mask = sum(1 << k for k in range(bits - 1) if i >> (bits - 2 - k) & 1)
             total = total + swap_across(part, dims, mask, local_count).astype(F32)

time: 47.2 us -> 48.1 us (1.019)
  starting transfers between devices: 20.4 us -> 21.1 us
    ppermute x13, starting transfers between devices: 19.7 us -> 20.3 us  [swap_across(): return lax.ppermute(array, ('node', 'local'), perm)]
  transfers between devices with their start and end apart: 17 -> 17, of which waited for: 10 -> 9; matrix products, arithmetic and copies ran while one was open for 1% -> 1% of each run, Pallas kernels for 0% -> 0%
where the time goes in v9:
time: 48.1 us; the launch traced here: 47.9 us
  starting transfers between devices  21.1 us (44%)
  waiting for transfers between devices  18.1 us (38%)
  Pallas kernels  7.39 us (15%)
  other arithmetic  0.97 us (2%)
    ppermute x13, starting transfers between devices, swap_across(): return lax.ppermute(array, ('node', 'local'), perm)  20.3 us
    ppermute x13, waiting for transfers between devices, swap_across(): return lax.ppermute(array, ('node', 'local'), perm)  15 us
    pallas_call x4, Pallas kernels, call(): pl.pallas_call(body, out_shape=outs, in_specs=[pl.BlockSpec(memory_space=...  6.22 us
    ppermute x4, waiting for transfers between devices, swap_core(): return lax.ppermute(array, 'node', [(n, n ^ 1) for n in range(node_count)])  3.12 us
    pallas_call x1, Pallas kernels, prepare(): pl.pallas_call(prepare_kernel, out_shape=VM((tokens.shape[0], tokens.shap...  1.17 us
  transfers between devices with their start and end apart: 17, of which 9 were waited for; matrix products, arithmetic and copies ran while one was open for 1% of the time, Pallas kernels for 0%

profile of v9, /device:TPU:0, one launch (start us, length us, event | category | flops | bytes accessed | tf_op | source)
XLA Modules:
  0.0 47.9 jit_solution(11854530388345336841)
XLA Ops:
  0.0 1.2 %shard_map.64.refs_1_ = bf16[8,7296]{1,0:T(8,128)(2,1)S(1)} custom-call(s32[1]{0:T(128)} %bitcast._.refs_0_, bf16[8,7168]{1,0:T(8,128)(2,1)} %tokens_far.1, s32[8,8]{1,0:T(8,128)} %ids_far.1, bf16[8,8]{1,0:T(8,128)(2,1)} %weights_far.1, bf16[1,1024,7168]{2,1,0:T(8,128)(2,1)} %refs_1_.3), custom_call_target="tpu_custom_call" | custom-call | bytes 200000 | tf_op jit(solution)/shard_map/pallas_call | solution.py:91
  1.2 4.1 %collective-permute-start.3 = (bf16[8,7296]{1,0:T(8,128)(2,1)S(1)}, bf16[8,7296]{1,0:T(8,128)(2,1)S(1)}, u32[]{:S(2)}, u32[]{:S(2)}) collective-permute-start(bf16[8,7296]{1,0:T(8,128)(2,1)S(1)} %shard_map.64.refs_1_), channel_id=1, source_target_pairs={{0,4},{1,5},{2,6},{3,7},{4,0},{5,1},{6,2},{7,3},{8,12},{9,13},{10,... | collective-permute-start | bytes 350216 | tf_op jit(solution)/shard_map/ppermute | solution.py:59
  5.3 2.5 %collective-permute-start.2 = (bf16[8,7296]{1,0:T(8,128)(2,1)S(1)}, bf16[8,7296]{1,0:T(8,128)(2,1)S(1)}, u32[]{:S(2)}, u32[]{:S(2)}) collective-permute-start(bf16[8,7296]{1,0:T(8,128)(2,1)S(1)} %shard_map.64.refs_1_), channel_id=1, source_target_pairs={{0,3},{1,2},{2,1},{3,0},{4,7},{5,6},{6,5},{7,4},{8,11},{9,10},{10,... | collective-permute-start | bytes 350216 | tf_op jit(solution)/shard_map/ppermute | solution.py:59
  8.3 0.5 %collective-permute-start = (bf16[8,7296]{1,0:T(8,128)(2,1)S(1)}, bf16[8,7296]{1,0:T(8,128)(2,1)S(1)}, u32[]{:S(2)}, u32[]{:S(2)}) collective-permute-start(bf16[8,7296]{1,0:T(8,128)(2,1)S(1)} %shard_map.64.refs_1_), channel_id=1, source_target_pairs={{0,1},{1,0},{2,3},{3,2},{4,5},{5,4},{6,7},{7,6},{8,10},{9,11},{10,... | collective-permute-start | bytes 350216 | tf_op jit(solution)/shard_map/ppermute | solution.py:59
  8.8 2.3 %collective-permute-done.3.refs_1_ = bf16[8,7296]{1,0:T(8,128)(2,1)S(1)} collective-permute-done((bf16[8,7296]{1,0:T(8,128)(2,1)S(1)}, bf16[8,7296]{1,0:T(8,128)(2,1)S(1)}, u32[]{:S(2)}, u32[]{:S(2)}) %collective-permute-start.3) | collective-permute-done | bytes 116768 | tf_op jit(solution)/shard_map/ppermute | solution.py:59
  11.1 1.6 %collective-permute-start.6 = (bf16[8,7296]{1,0:T(8,128)(2,1)S(1)}, bf16[8,7296]{1,0:T(8,128)(2,1)S(1)}, u32[]{:S(2)}, u32[]{:S(2)}) collective-permute-start(bf16[8,7296]{1,0:T(8,128)(2,1)S(1)} %collective-permute-done.3.refs_1_), channel_id=1, source_target_pairs={{0,3},{1,2},{2,1},{3,0},{4,7},{5,6},{6,5},{7,4},{8,11},{9,10},{10,... | collective-permute-start | bytes 350216 | tf_op jit(solution)/shard_map/ppermute | solution.py:59
  12.7 0.5 %collective-permute-start.5 = (bf16[8,7296]{1,0:T(8,128)(2,1)S(1)}, bf16[8,7296]{1,0:T(8,128)(2,1)S(1)}, u32[]{:S(2)}, u32[]{:S(2)}) collective-permute-start(bf16[8,7296]{1,0:T(8,128)(2,1)S(1)} %collective-permute-done.3.refs_1_), channel_id=1, source_target_pairs={{0,1},{1,0},{2,3},{3,2},{4,5},{5,4},{6,7},{7,6},{8,10},{9,11},{10,... | collective-permute-start | bytes 350216 | tf_op jit(solution)/shard_map/ppermute | solution.py:59
  13.3 1.6 %collective-permute-start.4 = (bf16[8,7296]{1,0:T(8,128)(2,1)S(1)}, bf16[8,7296]{1,0:T(8,128)(2,1)S(1)}, u32[]{:S(2)}, u32[]{:S(2)}) collective-permute-start(bf16[8,7296]{1,0:T(8,128)(2,1)S(1)} %collective-permute-done.3.refs_1_), channel_id=1, source_target_pairs={{0,2},{1,3},{2,0},{3,1},{4,6},{5,7},{6,4},{7,5},{8,9},{9,8},{10,11... | collective-permute-start | bytes 350216 | tf_op jit(solution)/shard_map/ppermute | solution.py:59
  14.9 0.8 %collective-permute-done.1.refs_3_ = bf16[8,7296]{1,0:T(8,128)(2,1)S(1)} collective-permute-done((bf16[8,7296]{1,0:T(8,128)(2,1)S(1)}, bf16[8,7296]{1,0:T(8,128)(2,1)S(1)}, u32[]{:S(2)}, u32[]{:S(2)}) %collective-permute-start.1) | collective-permute-done | bytes 116768 | tf_op jit(solution)/shard_map/ppermute | solution.py:59
  15.8 2.4 %collective-permute-done.6.refs_4_ = bf16[8,7296]{1,0:T(8,128)(2,1)S(1)} collective-permute-done((bf16[8,7296]{1,0:T(8,128)(2,1)S(1)}, bf16[8,7296]{1,0:T(8,128)(2,1)S(1)}, u32[]{:S(2)}, u32[]{:S(2)}) %collective-permute-start.6) | collective-permute-done | bytes 116768 | tf_op jit(solution)/shard_map/ppermute | solution.py:59
  18.2 1.4 %collective-permute-done.5.refs_3_ = bf16[8,7296]{1,0:T(8,128)(2,1)S(1)} collective-permute-done((bf16[8,7296]{1,0:T(8,128)(2,1)S(1)}, bf16[8,7296]{1,0:T(8,128)(2,1)S(1)}, u32[]{:S(2)}, u32[]{:S(2)}) %collective-permute-start.5) | collective-permute-done | bytes 116768 | tf_op jit(solution)/shard_map/ppermute | solution.py:59
  19.9 1.8 %collective-permute-done.8.refs_5_.refs_6_ = bf16[32,7296]{1,0:T(8,128)(2,1)S(1)} collective-permute-done((bf16[32,7296]{1,0:T(8,128)(2,1)S(1)}, bf16[32,7296]{1,0:T(8,128)(2,1)S(1)}, u32[]{:S(2)}, u32[]{:S(2)}) %collective-permute-start.8) | collective-permute-done | bytes 466976 | tf_op jit(solution)/shard_map/ppermute | solution.py:67
  21.8 4.0 %shard_map.67.refs_2_ = bf16[128,1024]{1,0:T(8,128)(2,1)S(1)} custom-call(bf16[1,7168,1024]{2,1,0:T(8,128)(2,1)S(1)} %bitcast.4, bf16[1,7168,1024]{2,1,0:T(8,128)(2,1)S(1)} %bitcast.6, bf16[32,7296]{1,0:T(8,128)(2,1)S(1)} %shard_map.65.refs_2_.refs_3_, bf16[32,7296]{1,0:T(8,128)(2,1)S(1)} %shard_map.66.refs_3_.refs_4_, ...), custom_call_target="tpu_custom_call" | custom-call | flops 3758096384 | bytes 29360128 | tf_op jit(solution)/shard_map/pallas_call | solution.py:30
  25.9 2.1 %shard_map.68 = (f32[32,7168]{1,0:T(8,128)S(1)}, f32[32,7168]{1,0:T(8,128)S(1)}, bf16[32,7168]{1,0:T(8,128)(2,1)S(1)}, bf16[32,7168]{1,0:T(8,128)(2,1)S(1)}) custom-call(s32[1]{0:T(128)} %bitcast._.refs_0_, bf16[1,1024,7168]{2,1,0:T(8,128)(2,1)S(1)} %bitcast.2, bf16[128,1024]{1,0:T(8,128)(2,1)S(1)} %shard_map.67.refs_2_, ...), custom_call_target="tpu_custom_call" | custom-call | flops 1879048192 | bytes 14680064 | tf_op jit(solution)/shard_map/pallas_call | solution.py:30
  28.6 1.3 %collective-permute-done.12 = bf16[32,7168]{1,0:T(8,128)(2,1)S(1)} collective-permute-done((bf16[32,7168]{1,0:T(8,128)(2,1)S(1)}, bf16[32,7168]{1,0:T(8,128)(2,1)S(1)}, u32[]{:S(2)}, u32[]{:S(2)}) %collective-permute-start.12) | collective-permute-done | bytes 458784 | tf_op jit(solution)/shard_map/ppermute | solution.py:67
  30.0 0.8 %collective-permute-start.13 = (bf16[8,7168]{1,0:T(8,128)(2,1)S(1)}, bf16[8,7168]{1,0:T(8,128)(2,1)S(1)}, u32[]{:S(2)}, u32[]{:S(2)}) collective-permute-start(bf16[8,7168]{1,0:T(8,128)(2,1)S(1)} %get-tuple-element.15), channel_id=1, source_target_pairs={{0,1},{1,0},{2,3},{3,2},{4,5},{5,4},{6,7},{7,6},{8,10},{9,11},{10,... | collective-permute-start | bytes 344072 | tf_op jit(solution)/shard_map/ppermute | solution.py:59
  30.9 2.0 %collective-permute-start.15 = (bf16[8,7168]{1,0:T(8,128)(2,1)S(1)}, bf16[8,7168]{1,0:T(8,128)(2,1)S(1)}, u32[]{:S(2)}, u32[]{:S(2)}) collective-permute-start(bf16[8,7168]{1,0:T(8,128)(2,1)S(1)} %get-tuple-element.16), channel_id=1, source_target_pairs={{0,3},{1,2},{2,1},{3,0},{4,7},{5,6},{6,5},{7,4},{8,11},{9,10},{10,... | collective-permute-start | bytes 344072 | tf_op jit(solution)/shard_map/ppermute | solution.py:59
  32.9 0.7 %collective-permute-start.14 = (bf16[8,7168]{1,0:T(8,128)(2,1)S(1)}, bf16[8,7168]{1,0:T(8,128)(2,1)S(1)}, u32[]{:S(2)}, u32[]{:S(2)}) collective-permute-start(bf16[8,7168]{1,0:T(8,128)(2,1)S(1)} %get-tuple-element.17), channel_id=1, source_target_pairs={{0,2},{1,3},{2,0},{3,1},{4,6},{5,7},{6,4},{7,5},{8,9},{9,8},{10,11... | collective-permute-start | bytes 344072 | tf_op jit(solution)/shard_map/ppermute | solution.py:59
  33.7 1.4 %collective-permute-start.10 = (bf16[16,7168]{1,0:T(8,128)(2,1)S(1)}, bf16[16,7168]{1,0:T(8,128)(2,1)S(1)}, u32[]{:S(2)}, u32[]{:S(2)}) collective-permute-start(bf16[16,7168]{1,0:T(8,128)(2,1)S(1)} %slice.60), channel_id=1, source_target_pairs={{0,2},{1,3},{2,0},{3,1},{4,6},{5,7},{6,4},{7,5},{8,9},{9,8},{10,11... | collective-permute-start | bytes 688136 | tf_op jit(solution)/shard_map/ppermute | solution.py:59
  35.1 2.7 %collective-permute-done.13 = bf16[8,7168]{1,0:T(8,128)(2,1)S(1)} collective-permute-done((bf16[8,7168]{1,0:T(8,128)(2,1)S(1)}, bf16[8,7168]{1,0:T(8,128)(2,1)S(1)}, u32[]{:S(2)}, u32[]{:S(2)}) %collective-permute-start.13) | collective-permute-done | bytes 114720 | tf_op jit(solution)/shard_map/ppermute | solution.py:59
  37.9 3.3 %collective-permute-start.16 = (bf16[8,7168]{1,0:T(8,128)(2,1)S(1)}, bf16[8,7168]{1,0:T(8,128)(2,1)S(1)}, u32[]{:S(2)}, u32[]{:S(2)}) collective-permute-start(bf16[8,7168]{1,0:T(8,128)(2,1)S(1)} %fusion.2), channel_id=1, source_target_pairs={{0,4},{1,5},{2,6},{3,7},{4,0},{5,1},{6,2},{7,3},{8,12},{9,13},{10,... | collective-permute-start | bytes 344072 | tf_op jit(solution)/shard_map/ppermute | solution.py:59
  41.3 0.7 %collective-permute-start.11 = (bf16[8,7168]{1,0:T(8,128)(2,1)S(1)}, bf16[8,7168]{1,0:T(8,128)(2,1)S(1)}, u32[]{:S(2)}, u32[]{:S(2)}) collective-permute-start(bf16[8,7168]{1,0:T(8,128)(2,1)S(1)} %slice.61), channel_id=1, source_target_pairs={{0,1},{1,0},{2,3},{3,2},{4,5},{5,4},{6,7},{7,6},{8,10},{9,11},{10,... | collective-permute-start | bytes 344072 | tf_op jit(solution)/shard_map/ppermute | solution.py:59
  42.0 5.2 %collective-permute-done.16 = bf16[8,7168]{1,0:T(8,128)(2,1)S(1)} collective-permute-done((bf16[8,7168]{1,0:T(8,128)(2,1)S(1)}, bf16[8,7168]{1,0:T(8,128)(2,1)S(1)}, u32[]{:S(2)}, u32[]{:S(2)}) %collective-permute-start.16) | collective-permute-done | bytes 114720 | tf_op jit(solution)/shard_map/ppermute | solution.py:59
  47.2 0.7 %fusion.4 = bf16[8,7168]{1,0:T(8,128)(2,1)} fusion(f32[16,7168]{1,0:T(8,128)S(1)} %slice_add_fusion, bf16[8,7168]{1,0:T(8,128)(2,1)S(1)} %collective-permute-done.16, bf16[8,7168]{1,0:T(8,128)(2,1)S(1)} %collective-permute-done.11), kind=kLoop, calls=%fused_computation.11 | loop fusion | flops 286720 | bytes 573440 | tf_op jit(solution)/shard_map/convert_element_type | solution.py:230
  (50 shorter events, 1.8 us)
Async XLA Ops:
  0.0 21.7 %slice-start.8 = ((s8[14680064]{0:T(1024)(128)(4,1)}), s8[4194304]{0:T(1024)(128)(4,1)S(1)}, s32[]{:S(2)}) async-start(s8[14680064]{0:T(1024)(128)(4,1)} %bitcast.5), calls=%async_computation.8 | async-start | bytes 8388608
  0.0 21.7 %slice-start.9 = ((s8[14680064]{0:T(1024)(128)(4,1)}), s8[4194304]{0:T(1024)(128)(4,1)S(1)}, s32[]{:S(2)}) async-start(s8[14680064]{0:T(1024)(128)(4,1)} %bitcast.5), calls=%async_computation.9 | async-start | bytes 8388608
  1.2 20.6 %slice-start.4 = ((s8[14680064]{0:T(1024)(128)(4,1)}), s8[4194304]{0:T(1024)(128)(4,1)S(1)}, s32[]{:S(2)}) async-start(s8[14680064]{0:T(1024)(128)(4,1)} %bitcast.3), calls=%async_computation.4 | async-start | bytes 8388608
  1.2 20.5 %slice-start.5 = ((s8[14680064]{0:T(1024)(128)(4,1)}), s8[4194304]{0:T(1024)(128)(4,1)S(1)}, s32[]{:S(2)}) async-start(s8[14680064]{0:T(1024)(128)(4,1)} %bitcast.3), calls=%async_computation.5 | async-start | bytes 8388608
  1.2 20.5 %slice-start.10 = ((s8[14680064]{0:T(1024)(128)(4,1)}), s8[4194304]{0:T(1024)(128)(4,1)S(1)}, s32[]{:S(2)}) async-start(s8[14680064]{0:T(1024)(128)(4,1)} %bitcast.5), calls=%async_computation.10 | async-start | bytes 8388608
  1.2 9.9 %collective-permute-start.3 = (bf16[8,7296]{1,0:T(8,128)(2,1)S(1)}, bf16[8,7296]{1,0:T(8,128)(2,1)S(1)}, u32[]{:S(2)}, u32[]{:S(2)}) collective-permute-start(bf16[8,7296]{1,0:T(8,128)(2,1)S(1)} %shard_map.64.refs_1_), channel_id=1, source_target_pairs={{0,4},{1,5},{2,6},{3,7},{4,0},{5,1},{6,2},{7,3},{8,12},{9,13},{10,... | collective-permute-start | bytes 350216 | tf_op jit(solution)/shard_map/ppermute | solution.py:59
  5.3 7.9 %collective-permute-start.2 = (bf16[8,7296]{1,0:T(8,128)(2,1)S(1)}, bf16[8,7296]{1,0:T(8,128)(2,1)S(1)}, u32[]{:S(2)}, u32[]{:S(2)}) collective-permute-start(bf16[8,7296]{1,0:T(8,128)(2,1)S(1)} %shard_map.64.refs_1_), channel_id=1, source_target_pairs={{0,3},{1,2},{2,1},{3,0},{4,7},{5,6},{6,5},{7,4},{8,11},{9,10},{10,... | collective-permute-start | bytes 350216 | tf_op jit(solution)/shard_map/ppermute | solution.py:59
  7.9 7.8 %collective-permute-start.1 = (bf16[8,7296]{1,0:T(8,128)(2,1)S(1)}, bf16[8,7296]{1,0:T(8,128)(2,1)S(1)}, u32[]{:S(2)}, u32[]{:S(2)}) collective-permute-start(bf16[8,7296]{1,0:T(8,128)(2,1)S(1)} %shard_map.64.refs_1_), channel_id=1, source_target_pairs={{0,2},{1,3},{2,0},{3,1},{4,6},{5,7},{6,4},{7,5},{8,9},{9,8},{10,11... | collective-permute-start | bytes 350216 | tf_op jit(solution)/shard_map/ppermute | solution.py:59
  8.3 7.3 %collective-permute-start = (bf16[8,7296]{1,0:T(8,128)(2,1)S(1)}, bf16[8,7296]{1,0:T(8,128)(2,1)S(1)}, u32[]{:S(2)}, u32[]{:S(2)}) collective-permute-start(bf16[8,7296]{1,0:T(8,128)(2,1)S(1)} %shard_map.64.refs_1_), channel_id=1, source_target_pairs={{0,1},{1,0},{2,3},{3,2},{4,5},{5,4},{6,7},{7,6},{8,10},{9,11},{10,... | collective-permute-start | bytes 350216 | tf_op jit(solution)/shard_map/ppermute | solution.py:59
  11.1 7.1 %collective-permute-start.6 = (bf16[8,7296]{1,0:T(8,128)(2,1)S(1)}, bf16[8,7296]{1,0:T(8,128)(2,1)S(1)}, u32[]{:S(2)}, u32[]{:S(2)}) collective-permute-start(bf16[8,7296]{1,0:T(8,128)(2,1)S(1)} %collective-permute-done.3.refs_1_), channel_id=1, source_target_pairs={{0,3},{1,2},{2,1},{3,0},{4,7},{5,6},{6,5},{7,4},{8,11},{9,10},{10,... | collective-permute-start | bytes 350216 | tf_op jit(solution)/shard_map/ppermute | solution.py:59
  12.7 6.9 %collective-permute-start.5 = (bf16[8,7296]{1,0:T(8,128)(2,1)S(1)}, bf16[8,7296]{1,0:T(8,128)(2,1)S(1)}, u32[]{:S(2)}, u32[]{:S(2)}) collective-permute-start(bf16[8,7296]{1,0:T(8,128)(2,1)S(1)} %collective-permute-done.3.refs_1_), channel_id=1, source_target_pairs={{0,1},{1,0},{2,3},{3,2},{4,5},{5,4},{6,7},{7,6},{8,10},{9,11},{10,... | collective-permute-start | bytes 350216 | tf_op jit(solution)/shard_map/ppermute | solution.py:59
  13.3 6.5 %collective-permute-start.4 = (bf16[8,7296]{1,0:T(8,128)(2,1)S(1)}, bf16[8,7296]{1,0:T(8,128)(2,1)S(1)}, u32[]{:S(2)}, u32[]{:S(2)}) collective-permute-start(bf16[8,7296]{1,0:T(8,128)(2,1)S(1)} %collective-permute-done.3.refs_1_), channel_id=1, source_target_pairs={{0,2},{1,3},{2,0},{3,1},{4,6},{5,7},{6,4},{7,5},{8,9},{9,8},{10,11... | collective-permute-start | bytes 350216 | tf_op jit(solution)/shard_map/ppermute | solution.py:59
  15.7 6.1 %slice-start.6 = ((s8[14680064]{0:T(1024)(128)(4,1)}), s8[4194304]{0:T(1024)(128)(4,1)S(1)}, s32[]{:S(2)}) async-start(s8[14680064]{0:T(1024)(128)(4,1)} %bitcast.3), calls=%async_computation.6 | async-start | bytes 8388608
  15.7 4.2 %collective-permute-start.7 = (bf16[32,7296]{1,0:T(8,128)(2,1)S(1)}, bf16[32,7296]{1,0:T(8,128)(2,1)S(1)}, u32[]{:S(2)}, u32[]{:S(2)}) collective-permute-start(bf16[32,7296]{1,0:T(8,128)(2,1)S(1)} %shard_map.65.refs_2_.refs_3_), channel_id=1, source_target_pairs={{0,8},{8,0},{1,9},{9,1},{2,10},{10,2},{3,11},{11,3},{4,12},{12,4},... | collective-permute-start | bytes 1400840 | tf_op jit(solution)/shard_map/ppermute | solution.py:67
  19.8 6.1 %slice-start.1 = ((s8[14680064]{0:T(1024)(128)(4,1)}), s8[4194304]{0:T(1024)(128)(4,1)S(1)}, s32[]{:S(2)}) async-start(s8[14680064]{0:T(1024)(128)(4,1)} %bitcast.1), calls=%async_computation.1 | async-start | bytes 8388608
  19.8 1.9 %collective-permute-start.8 = (bf16[32,7296]{1,0:T(8,128)(2,1)S(1)}, bf16[32,7296]{1,0:T(8,128)(2,1)S(1)}, u32[]{:S(2)}, u32[]{:S(2)}) collective-permute-start(bf16[32,7296]{1,0:T(8,128)(2,1)S(1)} %shard_map.66.refs_3_.refs_4_), channel_id=1, source_target_pairs={{0,8},{8,0},{1,9},{9,1},{2,10},{10,2},{3,11},{11,3},{4,12},{12,4},... | collective-permute-start | bytes 1400840 | tf_op jit(solution)/shard_map/ppermute | solution.py:67
  28.0 1.9 %collective-permute-start.12 = (bf16[32,7168]{1,0:T(8,128)(2,1)S(1)}, bf16[32,7168]{1,0:T(8,128)(2,1)S(1)}, u32[]{:S(2)}, u32[]{:S(2)}) collective-permute-start(bf16[32,7168]{1,0:T(8,128)(2,1)S(1)} %get-tuple-element.12), channel_id=1, source_target_pairs={{0,8},{8,0},{1,9},{9,1},{2,10},{10,2},{3,11},{11,3},{4,12},{12,4},... | collective-permute-start | bytes 1376264 | tf_op jit(solution)/shard_map/ppermute | solution.py:67
  28.2 5.4 %collective-permute-start.9 = (bf16[32,7168]{1,0:T(8,128)(2,1)S(1)}, bf16[32,7168]{1,0:T(8,128)(2,1)S(1)}, u32[]{:S(2)}, u32[]{:S(2)}) collective-permute-start(bf16[32,7168]{1,0:T(8,128)(2,1)S(1)} %get-tuple-element.10), channel_id=1, source_target_pairs={{0,8},{8,0},{1,9},{9,1},{2,10},{10,2},{3,11},{11,3},{4,12},{12,4},... | collective-permute-start | bytes 1376264 | tf_op jit(solution)/shard_map/ppermute | solution.py:67
  30.0 7.8 %collective-permute-start.13 = (bf16[8,7168]{1,0:T(8,128)(2,1)S(1)}, bf16[8,7168]{1,0:T(8,128)(2,1)S(1)}, u32[]{:S(2)}, u32[]{:S(2)}) collective-permute-start(bf16[8,7168]{1,0:T(8,128)(2,1)S(1)} %get-tuple-element.15), channel_id=1, source_target_pairs={{0,1},{1,0},{2,3},{3,2},{4,5},{5,4},{6,7},{7,6},{8,10},{9,11},{10,... | collective-permute-start | bytes 344072 | tf_op jit(solution)/shard_map/ppermute | solution.py:59
  30.9 6.9 %collective-permute-start.15 = (bf16[8,7168]{1,0:T(8,128)(2,1)S(1)}, bf16[8,7168]{1,0:T(8,128)(2,1)S(1)}, u32[]{:S(2)}, u32[]{:S(2)}) collective-permute-start(bf16[8,7168]{1,0:T(8,128)(2,1)S(1)} %get-tuple-element.16), channel_id=1, source_target_pairs={{0,3},{1,2},{2,1},{3,0},{4,7},{5,6},{6,5},{7,4},{8,11},{9,10},{10,... | collective-permute-start | bytes 344072 | tf_op jit(solution)/shard_map/ppermute | solution.py:59
  32.9 4.9 %collective-permute-start.14 = (bf16[8,7168]{1,0:T(8,128)(2,1)S(1)}, bf16[8,7168]{1,0:T(8,128)(2,1)S(1)}, u32[]{:S(2)}, u32[]{:S(2)}) collective-permute-start(bf16[8,7168]{1,0:T(8,128)(2,1)S(1)} %get-tuple-element.17), channel_id=1, source_target_pairs={{0,2},{1,3},{2,0},{3,1},{4,6},{5,7},{6,4},{7,5},{8,9},{9,8},{10,11... | collective-permute-start | bytes 344072 | tf_op jit(solution)/shard_map/ppermute | solution.py:59
  33.7 7.5 %collective-permute-start.10 = (bf16[16,7168]{1,0:T(8,128)(2,1)S(1)}, bf16[16,7168]{1,0:T(8,128)(2,1)S(1)}, u32[]{:S(2)}, u32[]{:S(2)}) collective-permute-start(bf16[16,7168]{1,0:T(8,128)(2,1)S(1)} %slice.60), channel_id=1, source_target_pairs={{0,2},{1,3},{2,0},{3,1},{4,6},{5,7},{6,4},{7,5},{8,9},{9,8},{10,11... | collective-permute-start | bytes 688136 | tf_op jit(solution)/shard_map/ppermute | solution.py:59
  37.9 9.4 %collective-permute-start.16 = (bf16[8,7168]{1,0:T(8,128)(2,1)S(1)}, bf16[8,7168]{1,0:T(8,128)(2,1)S(1)}, u32[]{:S(2)}, u32[]{:S(2)}) collective-permute-start(bf16[8,7168]{1,0:T(8,128)(2,1)S(1)} %fusion.2), channel_id=1, source_target_pairs={{0,4},{1,5},{2,6},{3,7},{4,0},{5,1},{6,2},{7,3},{8,12},{9,13},{10,... | collective-permute-start | bytes 344072 | tf_op jit(solution)/shard_map/ppermute | solution.py:59
  41.3 5.9 %collective-permute-start.11 = (bf16[8,7168]{1,0:T(8,128)(2,1)S(1)}, bf16[8,7168]{1,0:T(8,128)(2,1)S(1)}, u32[]{:S(2)}, u32[]{:S(2)}) collective-permute-start(bf16[8,7168]{1,0:T(8,128)(2,1)S(1)} %slice.61), channel_id=1, source_target_pairs={{0,1},{1,0},{2,3},{3,2},{4,5},{5,4},{6,7},{7,6},{8,10},{9,11},{10,... | collective-permute-start | bytes 344072 | tf_op jit(solution)/shard_map/ppermute | solution.py:59
  (5 other events, 30.4 us)
